TPU v7x, 128 devices: a whole 4x4x4 slice. The times are simulated.
128 devices in a mesh: dom: 32 (over y, x, core), lvl: 4 (over z).
Axes of the slice: x: 4, y: 4, z: 4, core: 2. Of those that a mesh axis runs over, the one named last changes fastest.
Arguments:
- positions: float32 [3, 2097152], P(None, ('dom', 'lvl')), may hold values from -0.8 to 0.8
- charges: float32 [2097152], P(('dom', 'lvl')), may hold values from -3 to 3
- block_leaf: int32 [16384], P(('dom', 'lvl')), may hold values from 0 to 8191, as said below
- leaf_slot: int32 [8192], replicated, may hold values from 0 to 8191, as said below
- m2m_ops: float32 [8, 81, 81], replicated, may hold values from -0.25 to 0.25
- l2l_ops: float32 [8, 81, 81], replicated, may hold values from -0.625 to 0.625
- m2l_ops: float32 [316, 81, 81], replicated, may hold values from -0.0024414062 to 0.0024414062
- item_target: int32 [32, 4, 4096], P('dom', 'lvl'), may hold values from 0 to 255
- item_source: int32 [32, 4, 4096], P('dom', 'lvl'), may hold values from 0 to 8191, as said below
- item_offset: int32 [32, 4, 4096], P('dom', 'lvl'), may hold values from 0 to 315
- coarse_target: int32 [32, 4, 2048], P('dom', 'lvl'), may hold values from 0 to 63
- coarse_source: int32 [32, 4, 2048], P('dom', 'lvl'), may hold values from 0 to 1023
- coarse_offset: int32 [32, 4, 2048], P('dom', 'lvl'), may hold values from 0 to 315
Outputs:
- forces: float32 [3, 2097152], P(None, ('dom', 'lvl'))
- potential: float32 [2097152], P(('dom', 'lvl'))
Inputs may be any that keep to these rules, and one draw needn't show every extreme that they name: `block_leaf`: block b lies on device b // 128 of dom+lvl and names a leaf of that device's lvl group g, one of the leaves g * 2048 to (g + 1) * 2048 - 1. Of one device's blocks at most 8 name leaves owned by any one dom index, and in every lvl group one dom index receives exactly 8 blocks from every device of the group. `leaf_slot`: A permutation of the slots. The leaves of lvl group g take the slots of devices with lvl index g; device (d, g) owns the slots (d * 4 + g) * 64 to (d * 4 + g + 1) * 64 - 1. `item_source`: the items of one device name, among the slots owned by any one device, exactly 32 different slots.
All inputs are finite; a program needn't handle non-finite values.
Results may differ from a plain program's by a relative error of at most 0.0001.
Values sent between devices are 32-bit elements; how exact they have to be, the bound alone decides.
A program may use at most 192 MiB of HBM per device.

v0:
```python
import math

import jax
import jax.numpy as jnp
from jax import lax
from jax.sharding import PartitionSpec as P

LEAF_DEV = 64


HIGH = lax.Precision.HIGHEST
softening = 0.04


def solid_basis(coords):
    along_x, along_y, along_z = (coords[0], coords[1], coords[2])
    squared = along_x * along_x + along_y * along_y + along_z * along_z
    nought = jnp.zeros_like(along_x)
    rows = [None] * 81
    diag_re = jnp.ones_like(along_x)
    diag_im = nought
    for azimuth in range(9):
        if azimuth > 0:
            factor = -1.0 / (2.0 * azimuth)
            diag_re, diag_im = (
                factor * (along_x * diag_re - along_y * diag_im),
                factor * (along_x * diag_im + along_y * diag_re),
            )
        lower_re, lower_im = (nought, nought)
        upper_re, upper_im = (diag_re, diag_im)
        for degree in range(azimuth, 9):
            if degree > azimuth:
                factor = 1.0 / ((degree + azimuth) * (degree - azimuth))
                fresh_re = factor * ((2 * degree - 1) * along_z * upper_re - squared * lower_re)
                fresh_im = factor * ((2 * degree - 1) * along_z * upper_im - squared * lower_im)
                lower_re, lower_im, upper_re, upper_im = (upper_re, upper_im, fresh_re, fresh_im)
            weight = math.sqrt(math.factorial(degree + azimuth) * math.factorial(degree - azimuth))
            start = degree * degree
            if azimuth == 0:
                rows[start] = weight * upper_re
            else:
                rows[start + 2 * azimuth - 1] = weight * upper_re
                rows[start + 2 * azimuth] = weight * upper_im
    return jnp.stack(rows, axis=0)


def near_field(coords, charge):
    delta = coords[:, :, :, None] - coords[:, :, None, :]
    distance = jnp.sum(delta * delta, axis=0) + softening
    inverse = jnp.where(jnp.eye(128, dtype=bool)[None], 0.0, lax.rsqrt(distance))
    potential = jnp.sum(inverse * charge[:, None, :], axis=2)
    strength = inverse * inverse * inverse * charge[:, None, :]
    force = charge[None] * jnp.sum(delta * strength[None], axis=3)
    return (force, potential)


def far_field(values, pullback, charge, local_rows):
    cotangent = jnp.broadcast_to(jnp.transpose(local_rows)[:, :, None], values.shape)
    potential = jnp.sum(values * cotangent, axis=0)
    (slope,) = pullback(cotangent)
    return (-charge[None] * slope, potential)


def by_octant(rows, tables, octant):
    total = jnp.zeros_like(rows)
    for index in range(8):
        moved = jnp.dot(
            rows, jnp.transpose(tables[index]), precision=HIGH, preferred_element_type=jnp.float32
        )
        total = total + jnp.where((octant == index)[:, None], moved, 0.0)
    return total


def translate(sources, source_ids, offsets, targets, rows, tables):
    count = source_ids.shape[0]
    width = 512

    def step(total, batch):
        src, off, tgt = batch
        product = jnp.einsum("ikl,il->ik", tables[off], sources[src], precision=HIGH)
        hits = (tgt[None, :] == jnp.arange(rows, dtype=jnp.int32)[:, None]).astype(jnp.float32)
        return (
            total + jnp.dot(hits, product, precision=HIGH, preferred_element_type=jnp.float32),
            None,
        )

    shaped = (
        source_ids.reshape(count // width, width),
        offsets.reshape(count // width, width),
        targets.reshape(count // width, width),
    )
    total, _ = lax.scan(step, jnp.zeros((rows, sources.shape[1]), jnp.float32), shaped)
    return total


def shards(
    positions,
    charges,
    block_leaf,
    leaf_slot,
    m2m_ops,
    l2l_ops,
    m2l_ops,
    item_target,
    item_source,
    item_offset,
    coarse_target,
    coarse_source,
    coarse_offset,
):
    dom_count = lax.axis_size("dom")
    lvl_count = lax.axis_size("lvl")
    dom_place = lax.axis_index("dom")
    lvl_place = lax.axis_index("lvl")
    blocks = block_leaf.shape[0]
    capacity = max(2, (2 * blocks + dom_count - 1) // dom_count)
    slots_all = dom_count * capacity
    coords = positions.reshape(3, blocks, 128)
    charge = charges.reshape(blocks, 128)
    near_force, near_phi = near_field(coords, charge)
    slots = leaf_slot[block_leaf]
    owner = slots // (LEAF_DEV * lvl_count)
    local_leaf = slots % LEAF_DEV
    hits = (owner[:, None] == jnp.arange(dom_count, dtype=jnp.int32)[None, :]).astype(jnp.int32)
    rank = jnp.sum(jnp.cumsum(hits, axis=0) * hits, axis=1) - 1
    target_row = owner * capacity + rank
    leaf_tags = (
        jnp.full((slots_all,), -1, jnp.int32)
        .at[target_row]
        .set(local_leaf)
        .reshape(dom_count, capacity)
    )
    packed = jnp.concatenate([jnp.transpose(coords, (1, 0, 2)), charge[:, None, :]], axis=1)
    outgoing = (
        jnp.zeros((slots_all, 4, 128), jnp.float32)
        .at[target_row]
        .set(packed)
        .reshape(dom_count, capacity, 4, 128)
    )
    arrived, tags = (
        lax.all_to_all(outgoing, "dom", split_axis=0, concat_axis=0, tiled=True),
        lax.all_to_all(leaf_tags, "dom", split_axis=0, concat_axis=0, tiled=True),
    )
    arrived = arrived.reshape(slots_all, 4, 128)
    arrived_coords = jnp.transpose(arrived[:, :3], (1, 0, 2))
    arrived_charge = arrived[:, 3]
    values, pullback = jax.vjp(solid_basis, arrived_coords)
    moments = jnp.einsum("kbn,bn->bk", values, arrived_charge, precision=HIGH)
    member = (tags.reshape(-1)[None, :] == jnp.arange(LEAF_DEV, dtype=jnp.int32)[:, None]).astype(
        jnp.float32
    )
    leaf_moments = jnp.dot(member, moments, precision=HIGH, preferred_element_type=jnp.float32)
    leaves = leaf_slot.shape[0]
    parents_count = leaves // 8
    first_slot = (dom_place * lvl_count + lvl_place) * LEAF_DEV
    owned = leaf_slot[None, :] == first_slot + jnp.arange(LEAF_DEV, dtype=jnp.int32)[:, None]
    leaf_ids = jnp.sum(jnp.where(owned, jnp.arange(leaves, dtype=jnp.int32)[None, :], 0), axis=1)
    octant = leaf_ids % 8
    parent = leaf_ids // 8
    children = by_octant(leaf_moments, m2m_ops, octant)
    sources = item_source.reshape(-1)
    source_table = lax.all_gather(leaf_moments, ("dom", "lvl"), axis=0, tiled=True)
    picks = (parent[:, None] == jnp.arange(parents_count, dtype=jnp.int32)[None, :]).astype(
        jnp.float32
    )
    partial_value = jnp.dot(
        jnp.transpose(picks), children, precision=HIGH, preferred_element_type=jnp.float32
    )
    all_parents = lax.psum(partial_value, ("dom", "lvl"))
    helper_terms = translate(
        source_table,
        sources,
        item_offset.reshape(-1),
        item_target.reshape(-1),
        lvl_count * LEAF_DEV,
        m2l_ops,
    )
    leaf_locals = lax.psum_scatter(helper_terms, "lvl", scatter_dimension=0, tiled=True)
    parent_locals = translate(
        all_parents,
        coarse_source.reshape(-1),
        coarse_offset.reshape(-1),
        coarse_target.reshape(-1),
        LEAF_DEV,
        m2l_ops,
    )
    slot_locals = leaf_locals + by_octant(parent_locals, l2l_ops, octant)
    arrived_locals = jnp.dot(
        jnp.transpose(member), slot_locals, precision=HIGH, preferred_element_type=jnp.float32
    )
    far_force, far_phi = far_field(values, pullback, arrived_charge, arrived_locals)
    results = jnp.concatenate(
        [jnp.transpose(far_force, (1, 0, 2)), far_phi[:, None, :]], axis=1
    ).reshape(dom_count, capacity, 4, 128)
    returned = lax.all_to_all(results, "dom", split_axis=0, concat_axis=0, tiled=True).reshape(
        slots_all, 4, 128
    )[target_row]
    far_force = jnp.transpose(returned[:, :3], (1, 0, 2))
    far_phi = returned[:, 3]
    forces = (near_force + far_force).reshape(3, blocks * 128)
    potential = (near_phi + far_phi).reshape(blocks * 128)
    return (forces, potential)


def solution(mesh):
    in_specs = (
        P(None, ("dom", "lvl")),
        P(("dom", "lvl")),
        P(("dom", "lvl")),
        P(),
        P(),
        P(),
        P(),
        P("dom", "lvl", None),
        P("dom", "lvl", None),
        P("dom", "lvl", None),
        P("dom", "lvl", None),
        P("dom", "lvl", None),
        P("dom", "lvl", None),
    )
    out_specs = (P(None, ("dom", "lvl")), P(("dom", "lvl")))
    return jax.shard_map(shards, mesh=mesh, in_specs=in_specs, out_specs=out_specs, check_vma=False)
```

profile of v0, /device:TPU:1, one launch (start us, length us, event | category | flops | bytes accessed | tf_op | source)
XLA Modules:
  0.0 1187.3 jit_solution(3576880088796038675)
XLA Ops:
  7.9 1.7 gather_fusion.4
  10.0 1.0 scatter_custom_fusion.1
  11.7 8.6 all-to-all-start.1
  20.3 1.1 select_reduce_fusion
  21.6 1.0 copy.205
  22.5 11.6 fusion.2
  34.1 1.1 pad_maximum_fusion.1
  35.2 7.2 multiply_reduce_fusion.1
  43.2 4.3 scatter_fusion
  48.4 7.4 all-to-all-start
  58.2 14.9 %copy.115 = f32[316,81,81]{2,1,0:T(8,128)} copy(f32[316,81,81]{0,2,1:T(8,128)} %param.23) | data formatting | bytes 16586208
  136.3 1.4 constant_dynamic-update-slice_fusion.4
  139.4 0.9 constant_dynamic-update-slice_fusion.1
  140.3 0.9 constant_dynamic-update-slice_fusion
  141.2 26.4 %fusion.4 = f32[256,1,81]{2,1,0:T(1,128)S(1)} fusion(f32[256,128,1]{1,2,0:T(1,128)S(1)} %bitcast.324, f32[81,256,128]{2,1,0:T(8,128)} %constant_dynamic-update-slice_fusion), kind=kOutput, calls=%fused_computation.29 | convolution fusion | flops 31850496 | bytes 10830848 | tf_op jit(solution)/shard_map/kbn,bn->bk/dot_general | solution.py:148
  169.6 1.1 fusion.24
  171.6 145.6 %all-reduce.5.cloned.1.call-done = f32[1024,81]{0,1:T(8,128)} async-done(((f32[1024,81]{0,1:T(8,128)}), f32[1024,81]{0,1:T(8,128)}) %all-reduce.5.cloned.1.call-update) | async-done | bytes 331792 | tf_op jit(solution)/shard_map/psum | solution.py:169
  317.2 1.2 copy.125
  318.4 257.0 %while.23 = (s32[]{:T(128)}, f32[64,81]{1,0:T(8,128)S(1)}, s32[4,512]{1,0:T(4,128)S(1)}, s32[4,512]{1,0:T(4,128)S(1)}, f32[316,81,81]{2,1,0:T(8,128)}, /*index=5...) while((s32[]{:T(128)}, f32[64,81]{1,0:T(8,128)S(1)}, ...), condition=%wide.region_12.13_spmd.clone, body=%wide.region_11.12_spmd.clone.sunk | while | flops 72209536 | bytes 41212532 | solution.py:92
  318.6 24.1 %gather_fusion.2 = f32[512,81,81]{2,1,0:T(8,128)} fusion(f32[316,81,81]{2,1,0:T(8,128)} %get-tuple-element.538, s32[1024]{0:T(1024)S(1)} %pad_clamp_fusion.12), kind=kCustom, calls=%fused_computation.2.clone.clone.1 | custom fusion | bytes 26875904 | tf_op jit(solution)/shard_map/while/body/eval_jaxpr/gather | solution.py:80
  342.8 1.0 gather_fusion.3
  343.8 38.7 %fusion.136 = f32[512,1,81]{2,1,0:T(1,128)S(1)} fusion(f32[512,81,81]{2,1,0:T(8,128)} %gather_fusion.2, f32[512,81,1]{1,2,0:T(1,128)S(1)} %bitcast.308), kind=kOutput, calls=%fused_computation.553.clone.1 | convolution fusion | flops 40310784 | bytes 13768704 | tf_op jit(solution)/shard_map/while/body/eval_jaxpr/ikl,il->ik/dot_general | solution.py:80
  382.8 24.2 %gather_fusion.2 = f32[512,81,81]{2,1,0:T(8,128)} fusion(f32[316,81,81]{2,1,0:T(8,128)} %get-tuple-element.538, s32[1024]{0:T(1024)S(1)} %pad_clamp_fusion.12), kind=kCustom, calls=%fused_computation.2.clone.clone.1 | custom fusion | bytes 26875904 | tf_op jit(solution)/shard_map/while/body/eval_jaxpr/gather | solution.py:80
  407.0 1.0 gather_fusion.3
  408.0 38.7 %fusion.136 = f32[512,1,81]{2,1,0:T(1,128)S(1)} fusion(f32[512,81,81]{2,1,0:T(8,128)} %gather_fusion.2, f32[512,81,1]{1,2,0:T(1,128)S(1)} %bitcast.308), kind=kOutput, calls=%fused_computation.553.clone.1 | convolution fusion | flops 40310784 | bytes 13768704 | tf_op jit(solution)/shard_map/while/body/eval_jaxpr/ikl,il->ik/dot_general | solution.py:80
  447.0 24.1 %gather_fusion.2 = f32[512,81,81]{2,1,0:T(8,128)} fusion(f32[316,81,81]{2,1,0:T(8,128)} %get-tuple-element.538, s32[1024]{0:T(1024)S(1)} %pad_clamp_fusion.12), kind=kCustom, calls=%fused_computation.2.clone.clone.1 | custom fusion | bytes 26875904 | tf_op jit(solution)/shard_map/while/body/eval_jaxpr/gather | solution.py:80
  471.2 1.0 gather_fusion.3
  472.2 38.7 %fusion.136 = f32[512,1,81]{2,1,0:T(1,128)S(1)} fusion(f32[512,81,81]{2,1,0:T(8,128)} %gather_fusion.2, f32[512,81,1]{1,2,0:T(1,128)S(1)} %bitcast.308), kind=kOutput, calls=%fused_computation.553.clone.1 | convolution fusion | flops 40310784 | bytes 13768704 | tf_op jit(solution)/shard_map/while/body/eval_jaxpr/ikl,il->ik/dot_general | solution.py:80
  511.2 24.1 %gather_fusion.2 = f32[512,81,81]{2,1,0:T(8,128)} fusion(f32[316,81,81]{2,1,0:T(8,128)} %get-tuple-element.538, s32[1024]{0:T(1024)S(1)} %pad_clamp_fusion.12), kind=kCustom, calls=%fused_computation.2.clone.clone.1 | custom fusion | bytes 26875904 | tf_op jit(solution)/shard_map/while/body/eval_jaxpr/gather | solution.py:80
  535.4 1.0 gather_fusion.3
  536.4 38.7 %fusion.136 = f32[512,1,81]{2,1,0:T(1,128)S(1)} fusion(f32[512,81,81]{2,1,0:T(8,128)} %gather_fusion.2, f32[512,81,1]{1,2,0:T(1,128)S(1)} %bitcast.308), kind=kOutput, calls=%fused_computation.553.clone.1 | convolution fusion | flops 40310784 | bytes 13768704 | tf_op jit(solution)/shard_map/while/body/eval_jaxpr/ikl,il->ik/dot_general | solution.py:80
  576.8 532.8 %while.22 = (s32[]{:T(128)}, f32[256,81]{0,1:T(8,128)S(1)}, s32[8,512]{1,0:T(8,128)S(1)}, s32[8,512]{1,0:T(8,128)S(1)}, f32[316,81,81]{2,1,0:T(8,128)}, /*index=...) while((s32[]{:T(128)}, f32[256,81]{0,1:T(8,128)S(1)}, s32[8,512]{1,0:T(8,128)S(1)}, ...), condition=%wide.region_7.8_spmd.clone, body=%wide.region_6.7_spmd.clone.sunk | while | flops 167890432 | bytes 41336948 | solution.py:92
  577.0 24.1 %gather_fusion = f32[512,81,81]{2,1,0:T(8,128)} fusion(f32[316,81,81]{2,1,0:T(8,128)} %get-tuple-element.511, s32[1024]{0:T(1024)S(1)} %pad_clamp_fusion.10), kind=kCustom, calls=%fused_computation.clone.clone.1 | custom fusion | bytes 26875904 | tf_op jit(solution)/shard_map/while/body/eval_jaxpr/gather | solution.py:80
  601.2 3.2 gather_fusion.1
  604.4 38.7 %fusion.132 = f32[512,1,81]{2,1,0:T(1,128)S(1)} fusion(f32[512,81,81]{2,1,0:T(8,128)} %gather_fusion, f32[512,81,1]{1,2,0:T(1,128)S(1)} %bitcast.309), kind=kOutput, calls=%fused_computation.552.clone.1 | convolution fusion | flops 40310784 | bytes 13768704 | tf_op jit(solution)/shard_map/while/body/eval_jaxpr/ikl,il->ik/dot_general | solution.py:80
  643.6 24.1 %gather_fusion = f32[512,81,81]{2,1,0:T(8,128)} fusion(f32[316,81,81]{2,1,0:T(8,128)} %get-tuple-element.511, s32[1024]{0:T(1024)S(1)} %pad_clamp_fusion.10), kind=kCustom, calls=%fused_computation.clone.clone.1 | custom fusion | bytes 26875904 | tf_op jit(solution)/shard_map/while/body/eval_jaxpr/gather | solution.py:80
  667.7 3.2 gather_fusion.1
  671.0 38.7 %fusion.132 = f32[512,1,81]{2,1,0:T(1,128)S(1)} fusion(f32[512,81,81]{2,1,0:T(8,128)} %gather_fusion, f32[512,81,1]{1,2,0:T(1,128)S(1)} %bitcast.309), kind=kOutput, calls=%fused_computation.552.clone.1 | convolution fusion | flops 40310784 | bytes 13768704 | tf_op jit(solution)/shard_map/while/body/eval_jaxpr/ikl,il->ik/dot_general | solution.py:80
  710.1 24.1 %gather_fusion = f32[512,81,81]{2,1,0:T(8,128)} fusion(f32[316,81,81]{2,1,0:T(8,128)} %get-tuple-element.511, s32[1024]{0:T(1024)S(1)} %pad_clamp_fusion.10), kind=kCustom, calls=%fused_computation.clone.clone.1 | custom fusion | bytes 26875904 | tf_op jit(solution)/shard_map/while/body/eval_jaxpr/gather | solution.py:80
  734.3 3.2 gather_fusion.1
  737.5 38.7 %fusion.132 = f32[512,1,81]{2,1,0:T(1,128)S(1)} fusion(f32[512,81,81]{2,1,0:T(8,128)} %gather_fusion, f32[512,81,1]{1,2,0:T(1,128)S(1)} %bitcast.309), kind=kOutput, calls=%fused_computation.552.clone.1 | convolution fusion | flops 40310784 | bytes 13768704 | tf_op jit(solution)/shard_map/while/body/eval_jaxpr/ikl,il->ik/dot_general | solution.py:80
  776.7 24.1 %gather_fusion = f32[512,81,81]{2,1,0:T(8,128)} fusion(f32[316,81,81]{2,1,0:T(8,128)} %get-tuple-element.511, s32[1024]{0:T(1024)S(1)} %pad_clamp_fusion.10), kind=kCustom, calls=%fused_computation.clone.clone.1 | custom fusion | bytes 26875904 | tf_op jit(solution)/shard_map/while/body/eval_jaxpr/gather | solution.py:80
  800.8 3.2 gather_fusion.1
  804.0 38.7 %fusion.132 = f32[512,1,81]{2,1,0:T(1,128)S(1)} fusion(f32[512,81,81]{2,1,0:T(8,128)} %gather_fusion, f32[512,81,1]{1,2,0:T(1,128)S(1)} %bitcast.309), kind=kOutput, calls=%fused_computation.552.clone.1 | convolution fusion | flops 40310784 | bytes 13768704 | tf_op jit(solution)/shard_map/while/body/eval_jaxpr/ikl,il->ik/dot_general | solution.py:80
  843.2 24.1 %gather_fusion = f32[512,81,81]{2,1,0:T(8,128)} fusion(f32[316,81,81]{2,1,0:T(8,128)} %get-tuple-element.511, s32[1024]{0:T(1024)S(1)} %pad_clamp_fusion.10), kind=kCustom, calls=%fused_computation.clone.clone.1 | custom fusion | bytes 26875904 | tf_op jit(solution)/shard_map/while/body/eval_jaxpr/gather | solution.py:80
  867.4 3.2 gather_fusion.1
  870.6 38.7 %fusion.132 = f32[512,1,81]{2,1,0:T(1,128)S(1)} fusion(f32[512,81,81]{2,1,0:T(8,128)} %gather_fusion, f32[512,81,1]{1,2,0:T(1,128)S(1)} %bitcast.309), kind=kOutput, calls=%fused_computation.552.clone.1 | convolution fusion | flops 40310784 | bytes 13768704 | tf_op jit(solution)/shard_map/while/body/eval_jaxpr/ikl,il->ik/dot_general | solution.py:80
  909.8 24.1 %gather_fusion = f32[512,81,81]{2,1,0:T(8,128)} fusion(f32[316,81,81]{2,1,0:T(8,128)} %get-tuple-element.511, s32[1024]{0:T(1024)S(1)} %pad_clamp_fusion.10), kind=kCustom, calls=%fused_computation.clone.clone.1 | custom fusion | bytes 26875904 | tf_op jit(solution)/shard_map/while/body/eval_jaxpr/gather | solution.py:80
  933.9 3.2 gather_fusion.1
  937.1 38.7 %fusion.132 = f32[512,1,81]{2,1,0:T(1,128)S(1)} fusion(f32[512,81,81]{2,1,0:T(8,128)} %gather_fusion, f32[512,81,1]{1,2,0:T(1,128)S(1)} %bitcast.309), kind=kOutput, calls=%fused_computation.552.clone.1 | convolution fusion | flops 40310784 | bytes 13768704 | tf_op jit(solution)/shard_map/while/body/eval_jaxpr/ikl,il->ik/dot_general | solution.py:80
  976.3 24.1 %gather_fusion = f32[512,81,81]{2,1,0:T(8,128)} fusion(f32[316,81,81]{2,1,0:T(8,128)} %get-tuple-element.511, s32[1024]{0:T(1024)S(1)} %pad_clamp_fusion.10), kind=kCustom, calls=%fused_computation.clone.clone.1 | custom fusion | bytes 26875904 | tf_op jit(solution)/shard_map/while/body/eval_jaxpr/gather | solution.py:80
  1000.5 3.2 gather_fusion.1
  1003.7 38.7 %fusion.132 = f32[512,1,81]{2,1,0:T(1,128)S(1)} fusion(f32[512,81,81]{2,1,0:T(8,128)} %gather_fusion, f32[512,81,1]{1,2,0:T(1,128)S(1)} %bitcast.309), kind=kOutput, calls=%fused_computation.552.clone.1 | convolution fusion | flops 40310784 | bytes 13768704 | tf_op jit(solution)/shard_map/while/body/eval_jaxpr/ikl,il->ik/dot_general | solution.py:80
  1042.8 24.1 %gather_fusion = f32[512,81,81]{2,1,0:T(8,128)} fusion(f32[316,81,81]{2,1,0:T(8,128)} %get-tuple-element.511, s32[1024]{0:T(1024)S(1)} %pad_clamp_fusion.10), kind=kCustom, calls=%fused_computation.clone.clone.1 | custom fusion | bytes 26875904 | tf_op jit(solution)/shard_map/while/body/eval_jaxpr/gather | solution.py:80
  1067.0 3.2 gather_fusion.1
  1070.2 38.7 %fusion.132 = f32[512,1,81]{2,1,0:T(1,128)S(1)} fusion(f32[512,81,81]{2,1,0:T(8,128)} %gather_fusion, f32[512,81,1]{1,2,0:T(1,128)S(1)} %bitcast.309), kind=kOutput, calls=%fused_computation.552.clone.1 | convolution fusion | flops 40310784 | bytes 13768704 | tf_op jit(solution)/shard_map/while/body/eval_jaxpr/ikl,il->ik/dot_general | solution.py:80
  1110.7 16.5 %reduce-scatter.4.cloned.1.call-done = f32[64,81]{1,0:T(8,128)} async-done(((f32[256,81]{1,0:T(8,128)}), f32[64,81]{1,0:T(8,128)}) %reduce-scatter.4.cloned.1.call-update) | async-done | bytes 20752 | tf_op jit(solution)/shard_map/reduce_scatter | solution.py:178
  1127.1 1.0 fusion.8
  1128.4 6.1 multiply_reduce_fusion
  1134.8 6.6 add_add_fusion.2
  1141.5 4.5 add_add_fusion
  1146.0 4.6 add_add_fusion.1
  1151.4 9.8 all-to-all-start.2
  1161.2 16.5 %fusion.3 = f32[3,128,128]{2,1,0:T(8,128)S(1)} fusion(f32[128,128,128]{2,1,0:T(8,128)} %get-tuple-element.244, f32[3,128,128]{2,1,0:T(8,128)S(1)} %bitcast.311), kind=kLoop, calls=%fused_computation.27 | loop fusion | flops 18825216 | bytes 8781824 | tf_op jit(solution)/shard_map/reduce_sum | solution.py:53
  (280 shorter events, 84.0 us)
Async XLA Ops:
  7.2 28.1 %copy-start.7 = (f32[16384]{0:T(1024)S(1)}, f32[16384]{0:T(1024)}, u32[]{:S(2)}) copy-start(f32[16384]{0:T(1024)} %param.18) | copy-start | bytes 196612
  11.7 36.7 %all-to-all-start.1 = ((s32[32,1,8]{2,1,0:T(1,128)}), s32[32,1,8]{2,1,0:T(1,128)S(1)}, u32[]{:S(2)}, u32[]{:S(2)}) async-start(s32[32,1,8]{2,1,0:T(1,128)} %bitcast.11), calls=%async_computation.1 | async-start | bytes 32768 | tf_op jit(solution)/shard_map/all_to_all | solution.py:142
  21.5 147.9 %copy-start.25 = (pred[64]{0:T(512)(128)(4,1)}, pred[64]{0:T(512)(128)(4,1)S(1)}, u32[]{:S(2)}) copy-start(pred[64]{0:T(512)(128)(4,1)S(1)} %get-tuple-element.235) | copy-start | bytes 196
  21.5 147.6 %copy-start.23 = (pred[64]{0:T(512)(128)(4,1)}, pred[64]{0:T(512)(128)(4,1)S(1)}, u32[]{:S(2)}) copy-start(pred[64]{0:T(512)(128)(4,1)S(1)} %get-tuple-element.374) | copy-start | bytes 196
  22.5 20.0 %copy-start.4 = (f32[1,3,128,128]{3,2,1,0:T(8,128)}, f32[1,3,128,128]{3,2,1,0:T(8,128)S(1)}, u32[]{:S(2)}) copy-start(f32[1,3,128,128]{3,2,1,0:T(8,128)S(1)} %copy.205) | copy-start | bytes 589828
  34.1 22.8 %copy-start.15 = (s32[1,1,4096]{2,1,0:T(1,128)S(1)}, s32[1,1,4096]{2,1,0:T(1,128)}, u32[]{:S(2)}) copy-start(s32[1,1,4096]{2,1,0:T(1,128)} %param.24) | copy-start | bytes 49156
  34.1 23.4 %copy-start.16 = (s32[1,1,4096]{2,1,0:T(1,128)S(1)}, s32[1,1,4096]{2,1,0:T(1,128)}, u32[]{:S(2)}) copy-start(s32[1,1,4096]{2,1,0:T(1,128)} %param.26) | copy-start | bytes 49156
  48.4 29.0 %all-to-all-start = ((f32[32,8,4,128]{3,1,2,0:T(8,128)}), f32[32,8,4,128]{3,1,2,0:T(8,128)S(1)}, u32[]{:S(2)}, u32[]{:S(2)}) async-start(f32[32,8,4,128]{3,1,2,0:T(8,128)} %copy.112), calls=%async_computation | async-start | bytes 1048576 | tf_op jit(solution)/shard_map/all_to_all | solution.py:141
  55.8 261.4 %all-reduce.5.cloned.1.call-start = ((), (), s32[]{:S(2)}) async-start(), calls=%async_computation.5 | async-start | bytes 720896 | tf_op jit(solution)/shard_map/psum | solution.py:169
  58.2 15.0 %copy-start.17 = (s32[1,1,4096]{2,1,0:T(1,128)S(1)}, s32[1,1,4096]{2,1,0:T(1,128)}, u32[]{:S(2)}) copy-start(s32[1,1,4096]{2,1,0:T(1,128)} %param.25) | copy-start | bytes 49156
  58.2 15.6 %copy-start.20 = (s32[1,1,2048]{2,1,0:T(1,128)S(1)}, s32[1,1,2048]{2,1,0:T(1,128)}, u32[]{:S(2)}) copy-start(s32[1,1,2048]{2,1,0:T(1,128)} %param.27) | copy-start | bytes 24580
  58.2 16.2 %copy-start.21 = (s32[1,1,2048]{2,1,0:T(1,128)S(1)}, s32[1,1,2048]{2,1,0:T(1,128)}, u32[]{:S(2)}) copy-start(s32[1,1,2048]{2,1,0:T(1,128)} %param.29) | copy-start | bytes 24580
  58.2 16.8 %copy-start.22 = (s32[1,1,2048]{2,1,0:T(1,128)S(1)}, s32[1,1,2048]{2,1,0:T(1,128)}, u32[]{:S(2)}) copy-start(s32[1,1,2048]{2,1,0:T(1,128)} %param.28) | copy-start | bytes 24580
  58.2 17.4 %copy-start.10 = (f32[8,81,81]{2,0,1:T(8,128)S(1)}, f32[8,81,81]{2,0,1:T(8,128)}, u32[]{:S(2)}) copy-start(f32[8,81,81]{2,0,1:T(8,128)} %param.21) | copy-start | bytes 629860
  58.2 17.6 %copy-start.11 = (f32[8,81,81]{2,0,1:T(8,128)S(1)}, f32[8,81,81]{2,0,1:T(8,128)}, u32[]{:S(2)}) copy-start(f32[8,81,81]{2,0,1:T(8,128)} %param.22) | copy-start | bytes 629860
  77.4 90.3 %copy-start.18 = (s32[256]{0:T(256)}, s32[256]{0:T(256)S(1)}, u32[]{:S(2)}) copy-start(s32[256]{0:T(256)S(1)} %eq.163) | copy-start | bytes 3076
  77.5 62.8 %copy-start = (f32[3,256,128]{2,1,0:T(8,128)}, f32[3,256,128]{2,1,0:T(8,128)S(1)}, u32[]{:S(2)}) copy-start(f32[3,256,128]{2,1,0:T(8,128)S(1)} %slice_bitcast_fusion) | copy-start | bytes 1179652
  78.3 60.2 %copy-start.2 = (f32[1,256,128]{2,1,0:T(8,128)}, f32[1,256,128]{2,1,0:T(8,128)S(1)}, u32[]{:S(2)}) copy-start(f32[1,256,128]{2,1,0:T(8,128)S(1)} %get-tuple-element.238) | copy-start | bytes 393220
  167.9 3.6 copy-start.6
  170.8 406.0 %all-gather.2.cloned.1.call-start = ((), (), s32[]{:S(2)}) async-start(), calls=%async_computation.4 | async-start | bytes 4227072 | tf_op jit(solution)/shard_map/all_gather | solution.py:162
  171.5 955.6 %reduce-scatter.4.cloned.1.call-start = ((), (), s32[]{:S(2)}) async-start(), calls=%async_computation.6 | async-start | bytes 163840 | tf_op jit(solution)/shard_map/reduce_scatter | solution.py:178
  576.7 533.7 %copy-start.14 = (f32[1,81,81]{2,0,1:T(1,128)S(1)}, f32[1,81,81]{2,0,1:T(1,128)}, u32[]{:S(2)}) copy-start(f32[1,81,81]{2,0,1:T(1,128)} %get-tuple-element.246) | copy-start | bytes 78736
  576.8 533.7 %copy-start.24 = (pred[64]{0:T(512)(128)(4,1)S(1)}, pred[64]{0:T(512)(128)(4,1)}, u32[]{:S(2)}) copy-start(pred[64]{0:T(512)(128)(4,1)} %copy-done.23) | copy-start | bytes 196
  576.8 550.4 %copy-start.13 = (f32[1,81,81]{2,0,1:T(1,128)S(1)}, f32[1,81,81]{2,0,1:T(1,128)}, u32[]{:S(2)}) copy-start(f32[1,81,81]{2,0,1:T(1,128)} %get-tuple-element.245) | copy-start | bytes 78736
  576.8 550.4 %copy-start.26 = (pred[64]{0:T(512)(128)(4,1)S(1)}, pred[64]{0:T(512)(128)(4,1)}, u32[]{:S(2)}) copy-start(pred[64]{0:T(512)(128)(4,1)} %copy-done.25) | copy-start | bytes 196
  576.8 551.3 %copy-start.19 = (s32[256]{0:T(256)S(1)}, s32[256]{0:T(256)}, u32[]{:S(2)}) copy-start(s32[256]{0:T(256)} %copy-done.18) | copy-start | bytes 3076
  1109.6 25.2 %copy-start.1 = (f32[3,256,128]{2,1,0:T(8,128)S(1)}, f32[3,256,128]{2,1,0:T(8,128)}, u32[]{:S(2)}) copy-start(f32[3,256,128]{2,1,0:T(8,128)} %copy-done) | copy-start | bytes 1179652
  1109.6 25.2 %copy-start.3 = (f32[1,256,128]{2,1,0:T(8,128)S(1)}, f32[1,256,128]{2,1,0:T(8,128)}, u32[]{:S(2)}) copy-start(f32[1,256,128]{2,1,0:T(8,128)} %copy-done.2) | copy-start | bytes 393220
  1109.6 40.9 %copy-start.9 = (f32[256,128]{1,0:T(8,128)S(1)}, f32[256,128]{1,0:T(8,128)}, u32[]{:S(2)}) copy-start(f32[256,128]{1,0:T(8,128)} %bitcast_negate_fusion) | copy-start | bytes 393220
  1109.6 51.5 %copy-start.5 = (f32[1,3,128,128]{3,2,1,0:T(8,128)S(1)}, f32[1,3,128,128]{3,2,1,0:T(8,128)}, u32[]{:S(2)}) copy-start(f32[1,3,128,128]{3,2,1,0:T(8,128)} %copy-done.4) | copy-start | bytes 589828
  1134.5 44.3 %copy-start.8 = (f32[16384]{0:T(1024)S(1)}, f32[16384]{0:T(1024)}, u32[]{:S(2)}) copy-start(f32[16384]{0:T(1024)} %param.18) | copy-start | bytes 196612
  1134.5 45.2 %copy-start.12 = (f32[128,128]{1,0:T(8,128)S(1)}, f32[128,128]{1,0:T(8,128)}, u32[]{:S(2)}) copy-start(f32[128,128]{1,0:T(8,128)} %get-tuple-element.243) | copy-start | bytes 196612
  1151.4 26.2 %all-to-all-start.2 = ((f32[32,8,4,128]{3,1,2,0:T(8,128)}), f32[32,8,4,128]{3,1,2,0:T(8,128)S(1)}, u32[]{:S(2)}, u32[]{:S(2)}) async-start(f32[32,8,4,128]{3,1,2,0:T(8,128)} %pad_maximum_fusion), calls=%async_computation.2 | async-start | bytes 1048576 | tf_op jit(solution)/shard_map/all_to_all | solution.py:195
Sparse Core Ops, SparseCore 0:
  170.9 146.2 all-reduce.4
  320.4 65.5 all-gather.1
  1110.5 16.5 reduce-scatter.3
where the time goes:
time: 1190 us
  matrix products  501 us (42%)
  local copies, waits for them, and re-layouts  350 us (29%)
  waiting for transfers between devices  162 us (14%)
  other arithmetic  132 us (11%)
  starting transfers between devices  25.9 us (2%)
  between operations  15.2 us (1%)
    dot_general x12, matrix products, step(): jnp.einsum('ikl,il->ik', tables[off], sources[src], precision=HIGH)  464 us
    gather x12, local copies, waits for them, and re-layouts, step(): tables[off]  290 us
    psum x1, waiting for transfers between devices, shards(): all_parents = lax.psum(partial_value, ('dom', 'lvl'))  146 us
    unnamed x87, other arithmetic  66.3 us
    gather x12, local copies, waits for them, and re-layouts, step(): sources[src]  29.9 us
    dot_general x1, matrix products, shards(): moments = jnp.einsum('kbn,bn->bk', values, arrived_charge, precision=HIGH)  26.4 us
  transfers between devices with their start and end apart: 6, of which 2 were waited for; matrix products, arithmetic and copies ran while one was open for 27% of the time, Pallas kernels for 0%

commit v1 on v0

v1 whole, which is shorter than its diff:
```python
import functools
import math

import jax
import jax.numpy as jnp
import numpy as np
from jax import lax
from jax.experimental import pallas as pl
from jax.experimental.pallas import tpu as pltpu
from jax.sharding import PartitionSpec as P

COEF = 81
TOP = 8
LANES = 128
LEAF_DEV = 64
CAP = 8
GROUP = 4
SOFTENING = 0.04
HIGH = lax.Precision.HIGHEST
VMEM = pltpu.VMEM
MIB = 1 << 20


def dot(a, b, contract=((1,), (0,))):
    return lax.dot_general(
        a, b, (contract, ((), ())), precision=HIGH, preferred_element_type=jnp.float32
    )


def row_index(degree, azimuth, imaginary):
    start = degree * degree
    return start if azimuth == 0 else start + 2 * azimuth - 1 + int(imaginary)


def row_weight(degree, azimuth):
    return math.sqrt(math.factorial(degree + azimuth) * math.factorial(degree - azimuth))


def harmonics(x, y, z, emit):
    squared = x * x + y * y + z * z
    diag_re, diag_im = None, None
    for azimuth in range(TOP + 1):
        if azimuth == 1:
            diag_re, diag_im = -0.5 * x, -0.5 * y
        elif azimuth > 1:
            factor = -1.0 / (2.0 * azimuth)
            fx, fy = factor * x, factor * y
            diag_re, diag_im = fx * diag_re - fy * diag_im, fx * diag_im + fy * diag_re
        if azimuth == 0:
            parts = [jnp.ones_like(x)]
        else:
            parts = [diag_re, diag_im]
        for which, value in enumerate(parts):
            lower, upper = None, value
            for degree in range(azimuth, TOP + 1):
                if degree > azimuth:
                    factor = 1.0 / ((degree + azimuth) * (degree - azimuth))
                    if degree == 1 and azimuth == 0:
                        fresh = z
                    elif lower is None:
                        fresh = (factor * (2 * degree - 1)) * z * upper
                    else:
                        fresh = (factor * (2 * degree - 1)) * z * upper - (factor * squared) * lower
                    lower, upper = upper, fresh
                emit(row_index(degree, azimuth, which == 1), degree, upper)


def weight_column():
    out = np.zeros((LANES, 1), np.float32)
    for degree in range(TOP + 1):
        for azimuth in range(degree + 1):
            for imaginary in range(2 if azimuth else 1):
                out[row_index(degree, azimuth, imaginary), 0] = row_weight(degree, azimuth)
    return out


G_ROWS = 96 + 3 * 64


def gradient_matrix():
    out = np.zeros((G_ROWS, LANES), np.float64)

    def add(axis, row, degree, azimuth, value_re, value_im):
        if degree < 0 or azimuth > degree:
            return
        out[96 + 64 * axis + row_index(degree, azimuth, 0), row] += value_re
        if azimuth:
            out[96 + 64 * axis + row_index(degree, azimuth, 1), row] += value_im

    for degree in range(TOP + 1):
        for azimuth in range(degree + 1):
            for imaginary in range(2 if azimuth else 1):
                row = row_index(degree, azimuth, imaginary)
                w = row_weight(degree, azimuth)
                out[row, row] = w
                below = degree - 1
                if imaginary:
                    add(2, row, below, azimuth, 0.0, w)
                    add(0, row, below, azimuth + 1, 0.0, 0.5 * w)
                    add(0, row, below, azimuth - 1, 0.0, -0.5 * w)
                    add(1, row, below, azimuth + 1, -0.5 * w, 0.0)
                    add(1, row, below, azimuth - 1, -0.5 * w, 0.0)
                elif azimuth:
                    add(2, row, below, azimuth, w, 0.0)
                    add(0, row, below, azimuth + 1, 0.5 * w, 0.0)
                    add(0, row, below, azimuth - 1, -0.5 * w, 0.0)
                    add(1, row, below, azimuth + 1, 0.0, 0.5 * w)
                    add(1, row, below, azimuth - 1, 0.0, 0.5 * w)
                else:
                    add(2, row, below, 0, w, 0.0)
                    add(0, row, below, 1, w, 0.0)
                    add(1, row, below, 1, 0.0, w)
    return out.astype(np.float32)


def iota(shape, dim):
    return lax.broadcasted_iota(jnp.int32, shape, dim)


def moments_kernel(pos_ref, q_ref, leaf_ref, table_ref, weight_ref, packed_ref, place_ref, turned, acc, rows):
    blocks = leaf_ref.shape[1]
    leaf = leaf_ref[...]
    high = (iota((64, blocks), 0) == (leaf >> 7)).astype(jnp.float32)
    lines = dot(table_ref[...].astype(jnp.float32), high, ((0,), (0,)))
    slot = jnp.sum(
        jnp.where(iota((LANES, blocks), 0) == (leaf & 127), lines, 0.0), axis=0, keepdims=True
    ).astype(jnp.int32)
    owner = slot >> 8
    hits = iota((32, blocks), 0) == owner
    earlier = (iota((blocks, blocks), 0) < iota((blocks, blocks), 1)).astype(jnp.float32)
    before = dot(hits.astype(jnp.float32), earlier)
    rank = jnp.sum(jnp.where(hits, before, 0.0), axis=0, keepdims=True).astype(jnp.int32)
    place = owner * CAP + rank
    place_ref[...] = place

    for d in range(3):
        turned[d] = pos_ref[d].T
    turned[3] = q_ref[...].T
    acc[...] = jnp.zeros_like(acc)

    def chunk(i, carry):
        at = pl.ds(pl.multiple_of(i * 32, 32), 32)
        x, y, z, q = (turned[d, at, :] for d in range(4))

        def emit(row, degree, value):
            part = q * value
            acc[row] += (part[0:8] + part[8:16]) + (part[16:24] + part[24:32])

        harmonics(x, y, z, emit)
        return carry

    lax.fori_loop(0, 4, chunk, 0)
    rows[...] = jnp.zeros_like(rows)
    for k in range(COEF):
        rows[k : k + 1, :] = jnp.sum(acc[k], axis=0, keepdims=True)
    rows[...] = rows[...] * weight_ref[...]
    rows[127:128, :] = ((slot & 63) + 1).astype(jnp.float32)
    moments = rows[...].T
    spread = (iota((32 * CAP, blocks), 0) == place).astype(jnp.float32)
    packed_ref[...] = dot(spread, moments)


def block_moments(coords, charge, leaf, table):
    blocks = coords.shape[1]
    whole = pl.BlockSpec(memory_space=VMEM)
    return pl.pallas_call(
        moments_kernel,
        out_shape=(
            jax.ShapeDtypeStruct((32 * CAP, LANES), jnp.float32),
            jax.ShapeDtypeStruct((1, blocks), jnp.int32),
        ),
        in_specs=[whole] * 5,
        out_specs=(whole, whole),
        scratch_shapes=[
            VMEM((4, LANES, blocks), jnp.float32),
            VMEM((COEF, 8, blocks), jnp.float32),
            VMEM((LANES, blocks), jnp.float32),
        ],
        compiler_params=pltpu.CompilerParams(vmem_limit_bytes=16 * MIB),
        name="block_moments",
    )(coords, charge, leaf, table, jnp.asarray(weight_column()))


def leaves_kernel(arrived_ref, table_ref, ops_ref, leaf_ref, parent_ref, ids_ref):
    group = lax.axis_index("lvl")
    first = (lax.axis_index("dom") * GROUP + group) * LEAF_DEV
    arrived = arrived_ref[...]
    tags = arrived[:, 127:128].astype(jnp.int32)
    member = (iota((arrived.shape[0], LEAF_DEV), 1) + 1 == tags).astype(jnp.float32)
    leaf = dot(member, arrived, ((0,), (0,)))
    leaf = jnp.where(iota(leaf.shape, 1) < COEF, leaf, 0.0)
    leaf_ref[...] = leaf
    slots = first + iota((LEAF_DEV, LANES), 0)
    found = jnp.zeros((LEAF_DEV, LANES), jnp.int32)
    lane = iota((LEAF_DEV, LANES), 1)
    table = table_ref[pl.ds(pl.multiple_of(group * 16, 16), 16), :]
    for h in range(16):
        number = (group * 16 + h) * 128 + lane
        found = found + jnp.where(table[h : h + 1, :] == slots, number, 0)
    ids = jnp.sum(found.astype(jnp.float32), axis=1, keepdims=True).astype(jnp.int32)
    ids_ref[...] = jnp.broadcast_to(ids, (LEAF_DEV, LANES))
    octant = ids & 7
    children = jnp.zeros((LEAF_DEV, LANES), jnp.float32)
    for o in range(8):
        children = children + dot(jnp.where(octant == o, leaf, 0.0), ops_ref[o], ((1,), (1,)))
    within = (ids >> 3) - group * 256
    picks = (iota((LEAF_DEV, 256), 1) == within).astype(jnp.float32)
    parent_ref[...] = dot(picks, children, ((0,), (0,)))


def leaves(arrived, table, ops):
    whole = pl.BlockSpec(memory_space=VMEM)
    return pl.pallas_call(
        leaves_kernel,
        out_shape=(
            jax.ShapeDtypeStruct((LEAF_DEV, LANES), jnp.float32),
            jax.ShapeDtypeStruct((256, LANES), jnp.float32),
            jax.ShapeDtypeStruct((LEAF_DEV, LANES), jnp.int32),
        ),
        in_specs=[whole] * 3,
        out_specs=(whole,) * 3,
        compiler_params=pltpu.CompilerParams(vmem_limit_bytes=16 * MIB),
        name="leaf_moments",
    )(arrived, table, ops)


def bitonic(x):
    rows = x.shape[0]
    index = iota(x.shape, 0) * LANES + iota(x.shape, 1)
    size = rows * LANES
    span = 2
    while span <= size:
        step = span // 2
        while step >= 1:
            axis, shift, extent = (1, step, LANES) if step < LANES else (0, step // LANES, rows)
            second = (index & step) != 0
            other = jnp.where(
                second, pltpu.roll(x, shift, axis), pltpu.roll(x, extent - shift, axis)
            )
            ascending = (index & span) == 0
            take_small = ascending != second
            x = jnp.where(take_small, jnp.minimum(x, other), jnp.maximum(x, other))
            step //= 2
        span *= 2
    return x


def order_kernel(leaf_ref, coarse_ref, leaf_out, coarse_out):
    leaf_out[...] = bitonic(leaf_ref[...])
    coarse_out[...] = bitonic(coarse_ref[...])


def listed(target, source, offset, targets, none, room):
    key = (target << 23) | (source << 9) | offset
    numbers = jnp.arange(targets, dtype=jnp.int32)
    count = jnp.sum((target[:, None] == numbers[None, :]).astype(jnp.int32), axis=0)
    fours = (count + 3) >> 2
    missing = fours * 4 - count
    turn = jnp.arange(3, dtype=jnp.int32)[:, None]
    fill_target = jnp.where(turn < missing[None, :], numbers[None, :], targets - 1)
    fill = ((fill_target << 23) | (none << 9)).reshape(-1)
    rest = jnp.full((room - key.shape[0] - fill.shape[0],), ((targets - 1) << 23) | (none << 9), jnp.int32)
    keys = jnp.concatenate([key, fill, rest]).reshape(room // LANES, LANES)
    return keys, jnp.sum(fours).reshape(1)


def ordered(leaf_keys, coarse_keys):
    whole = pl.BlockSpec(memory_space=VMEM)
    return pl.pallas_call(
        order_kernel,
        out_shape=(
            jax.ShapeDtypeStruct(leaf_keys.shape, jnp.int32),
            jax.ShapeDtypeStruct(coarse_keys.shape, jnp.int32),
        ),
        in_specs=[whole] * 2,
        out_specs=(whole,) * 2,
        name="order",
    )(leaf_keys, coarse_keys)


def translate_kernel(targets, sources, keys, count, src_hbm, ops_hbm, out_ref, ops, src, acc, sems):
    load_ops = pltpu.make_async_copy(ops_hbm, ops, sems.at[0])
    load_src = pltpu.make_async_copy(src_hbm, src.at[pl.ds(0, sources)], sems.at[1])
    load_ops.start()
    load_src.start()
    src[pl.ds(sources, 8), :] = jnp.zeros((8, LANES), jnp.float32)

    def clear(t, carry):
        acc[t] = jnp.zeros(acc.shape[1:], jnp.float32)
        return carry

    lax.fori_loop(0, targets, clear, 0)
    load_ops.wait()
    load_src.wait()

    def term(at):
        key = keys[at]
        row = src[pl.ds((key >> 9) & 16383, 1), :][:, :COEF]
        return ops[key & 511] * row

    def step(i, carry):
        for u in range(2):
            at = i * 8 + u * 4
            target = keys[at] >> 23
            total = (term(at) + term(at + 1)) + (term(at + 2) + term(at + 3))
            acc[target] += total
        return carry

    lax.fori_loop(0, (count[0] + 1) // 2, step, 0)
    diagonal = iota((COEF, LANES), 0) == iota((COEF, LANES), 1)

    def finish(i, carry):
        for u in range(4):
            t = i * 4 + u
            sums = jnp.sum(acc[t], axis=1, keepdims=True)
            out_ref[pl.ds(t, 1), :] = jnp.sum(
                jnp.where(diagonal, sums, 0.0), axis=0, keepdims=True
            )
        return carry

    lax.fori_loop(0, targets // 4, finish, 0)


def translate(keys, count, table, ops, targets):
    sources = table.shape[0]
    smem = pl.BlockSpec(memory_space=pltpu.SMEM)
    far = pl.BlockSpec(memory_space=pl.ANY)
    return pl.pallas_call(
        functools.partial(translate_kernel, targets, sources),
        out_shape=jax.ShapeDtypeStruct((targets, LANES), jnp.float32),
        in_specs=[smem, smem, far, far],
        out_specs=pl.BlockSpec(memory_space=VMEM),
        scratch_shapes=[
            VMEM(ops.shape, jnp.float32),
            VMEM((sources + 8, LANES), jnp.float32),
            VMEM((targets, COEF, COEF), jnp.float32),
            pltpu.SemaphoreType.DMA((2,)),
        ],
        compiler_params=pltpu.CompilerParams(vmem_limit_bytes=48 * MIB),
        name="translate",
    )(keys.reshape(-1), count, table, ops)


def near_kernel(pos_ref, q_ref, out_ref):
    def group(g, carry):
        at = pl.ds(pl.multiple_of(g * 8, 8), 8)
        rows = [pos_ref[d, at, :] for d in range(3)] + [q_ref[at, :]]
        columns = [r.T for r in rows]
        for b in range(8):
            xj, yj, zj, qj = (r[b : b + 1, :] for r in rows)
            xi, yi, zi, qi = (c[:, b : b + 1] for c in columns)
            sums = [jnp.zeros((8, LANES), jnp.float32) for _ in range(4)]
            for c in range(4):
                part = slice(c * 32, c * 32 + 32)
                dx = xj - xi[part]
                dy = yj - yi[part]
                dz = zj - zi[part]
                inverse = lax.rsqrt(dx * dx + dy * dy + dz * dz + SOFTENING)
                same = iota((32, LANES), 0) + c * 32 == iota((32, LANES), 1)
                weighted = jnp.where(same, 0.0, inverse * qi[part])
                strength = weighted * (inverse * inverse)
                for n, term in enumerate((strength * dx, strength * dy, strength * dz, weighted)):
                    sums[n] = sums[n] + ((term[0:8] + term[8:16]) + (term[16:24] + term[24:32]))
            for n in range(4):
                line = jnp.sum(sums[n], axis=0, keepdims=True)
                if n < 3:
                    line = line * qj
                out_ref[n, pl.ds(g * 8 + b, 1), :] = line
        return carry

    lax.fori_loop(0, q_ref.shape[0] // 8, group, 0)


def near_field(coords, charge):
    whole = pl.BlockSpec(memory_space=VMEM)
    return pl.pallas_call(
        near_kernel,
        out_shape=jax.ShapeDtypeStruct((4,) + charge.shape, jnp.float32),
        in_specs=[whole] * 2,
        out_specs=whole,
        compiler_params=pltpu.CompilerParams(vmem_limit_bytes=16 * MIB),
        cost_estimate=pl.CostEstimate(flops=60_000_000, bytes_accessed=1 << 19, transcendentals=2_000_000),
        name="near_field",
    )(coords, charge)


def locals_kernel(leaf_ref, parent_ref, ids_ref, arrived_ref, ops_ref, out_ref):
    octant = ids_ref[...] & 7
    parent = parent_ref[...]
    total = leaf_ref[...]
    for o in range(8):
        total = total + dot(jnp.where(octant == o, parent, 0.0), ops_ref[o], ((1,), (1,)))
    tags = arrived_ref[:, 127:128].astype(jnp.int32)
    member = (iota((arrived_ref.shape[0], LEAF_DEV), 1) + 1 == tags).astype(jnp.float32)
    out_ref[...] = dot(member, total)


def slot_locals(leaf_locals, parent_locals, ids, arrived, ops):
    whole = pl.BlockSpec(memory_space=VMEM)
    return pl.pallas_call(
        locals_kernel,
        out_shape=jax.ShapeDtypeStruct(arrived.shape, jnp.float32),
        in_specs=[whole] * 5,
        out_specs=whole,
        compiler_params=pltpu.CompilerParams(vmem_limit_bytes=16 * MIB),
        name="slot_locals",
    )(leaf_locals, parent_locals, ids, arrived, ops)


def far_kernel(pos_ref, q_ref, place_ref, returned_ref, near_ref, matrix_ref, force_ref, phi_ref, turned, lines):
    blocks = q_ref.shape[0]
    spread = (iota((32 * CAP, blocks), 0) == place_ref[...]).astype(jnp.float32)
    columns = dot(returned_ref[...], spread, ((0,), (0,)))
    lines[...] = dot(matrix_ref[...], columns)
    for d in range(3):
        turned[d] = pos_ref[d].T

    def chunk(i, carry):
        at = pl.ds(pl.multiple_of(i * 32, 32), 32)
        x, y, z = (turned[d, at, :] for d in range(3))
        sums = [None] * 4

        def emit(row, degree, value):
            starts = [(3, 0)] + ([(d, 96 + 64 * d) for d in range(3)] if degree < TOP else [])
            for n, start in starts:
                term = lines[start + row : start + row + 1, :] * value
                sums[n] = term if sums[n] is None else sums[n] + term

        harmonics(x, y, z, emit)
        for n in range(4):
            turned[n, at, :] = sums[n]
        return carry

    lax.fori_loop(0, 4, chunk, 0)
    charge = q_ref[...]
    for d in range(3):
        force_ref[d] = near_ref[d] - charge * turned[d].T
    phi_ref[...] = near_ref[3] + turned[3].T


def far_field(coords, charge, place, returned, near):
    whole = pl.BlockSpec(memory_space=VMEM)
    return pl.pallas_call(
        far_kernel,
        out_shape=(
            jax.ShapeDtypeStruct(coords.shape, jnp.float32),
            jax.ShapeDtypeStruct(charge.shape, jnp.float32),
        ),
        in_specs=[whole] * 6,
        out_specs=(whole, whole),
        scratch_shapes=[
            VMEM((4,) + charge.shape, jnp.float32),
            VMEM((G_ROWS, LANES), jnp.float32),
        ],
        compiler_params=pltpu.CompilerParams(vmem_limit_bytes=16 * MIB),
        name="far_field",
    )(coords, charge, place, returned, near, jnp.asarray(gradient_matrix()))


def padded(ops):
    return jnp.pad(ops, ((0, 0), (0, LANES - COEF), (0, LANES - COEF)))


def shards(
    positions,
    charges,
    block_leaf,
    leaf_slot,
    m2m_ops,
    l2l_ops,
    m2l_ops,
    item_target,
    item_source,
    item_offset,
    coarse_target,
    coarse_source,
    coarse_offset,
):
    blocks = block_leaf.shape[0]
    leaves_all = leaf_slot.shape[0]
    parents_all = leaves_all // 8
    coords = positions.reshape(3, blocks, LANES)
    charge = charges.reshape(blocks, LANES)
    table = leaf_slot.reshape(leaves_all // LANES, LANES)

    packed, place = block_moments(coords, charge, block_leaf.reshape(1, blocks), table)
    arrived = lax.all_to_all(packed, "dom", split_axis=0, concat_axis=0, tiled=True)
    leaf_moments, parents_part, ids = leaves(arrived, table, padded(m2m_ops))
    source_table = lax.all_gather(leaf_moments, ("dom", "lvl"), axis=0, tiled=True)
    parents_own = lax.psum_scatter(parents_part, "dom", scatter_dimension=0, tiled=True)
    parent_table = lax.all_gather(parents_own, ("lvl", "dom"), axis=0, tiled=True)

    leaf_keys, leaf_count = listed(
        item_target.reshape(-1), item_source.reshape(-1), item_offset.reshape(-1), 4 * LEAF_DEV, leaves_all, 8192
    )
    coarse_keys, coarse_count = listed(
        coarse_target.reshape(-1), coarse_source.reshape(-1), coarse_offset.reshape(-1), LEAF_DEV, parents_all, 4096
    )
    leaf_keys, coarse_keys = ordered(leaf_keys, coarse_keys)
    near = near_field(coords, charge)

    helper_terms = translate(leaf_keys, leaf_count, source_table, m2l_ops, 4 * LEAF_DEV)
    leaf_locals = lax.psum_scatter(helper_terms, "lvl", scatter_dimension=0, tiled=True)
    parent_locals = translate(coarse_keys, coarse_count, parent_table, m2l_ops, LEAF_DEV)
    sent = slot_locals(leaf_locals, parent_locals, ids, arrived, padded(l2l_ops))
    returned = lax.all_to_all(sent, "dom", split_axis=0, concat_axis=0, tiled=True)
    forces, potential = far_field(coords, charge, place, returned, near)
    return forces.reshape(3, blocks * LANES), potential.reshape(blocks * LANES)


def solution(mesh):
    in_specs = (
        P(None, ("dom", "lvl")),
        P(("dom", "lvl")),
        P(("dom", "lvl")),
        P(),
        P(),
        P(),
        P(),
        P("dom", "lvl", None),
        P("dom", "lvl", None),
        P("dom", "lvl", None),
        P("dom", "lvl", None),
        P("dom", "lvl", None),
        P("dom", "lvl", None),
    )
    out_specs = (P(None, ("dom", "lvl")), P(("dom", "lvl")))
    return jax.shard_map(shards, mesh=mesh, in_specs=in_specs, out_specs=out_specs, check_vma=False)
```

time: 1190 us -> 243 us (0.20)
  matrix products: 501 us -> 0 us
  local copies, waits for them, and re-layouts: 350 us -> 27.4 us
  other arithmetic: 132 us -> 5.38 us
  waiting for transfers between devices: 162 us -> 58.5 us
  Pallas kernels: 0 us -> 83.4 us
  blocking collectives: 0 us -> 37.2 us
  starting transfers between devices: 25.9 us -> 12.9 us
    dot_general x44 -> x0, matrix products: 501 us -> none  [the longest x12 464 us: step(): jnp.einsum('ikl,il->ik', tables[off], sources[src], precision=HIGH)]
    gather x26 -> x0, local copies, waits for them, and re-layouts: 322 us -> none  [the longest x12 290 us: step(): tables[off]]
    psum x1 -> x0, waiting for transfers between devices: 146 us -> none  [shards(): all_parents = lax.psum(partial_value, ('dom', 'lvl'))]
    pallas_call x0 -> x8, Pallas kernels: none -> 83.4 us  [the longest x2 53.4 us: translate(): pl.pallas_call(functools.partial(translate_kernel, targets, sources), out...]
    unnamed x87 -> x0, other arithmetic: 66.3 us -> none
    reduce_sum x6 -> x4, other arithmetic: 42.7 us -> 4.7 us  [the longest x2 3.34 us: listed(): jnp.sum((target[:, None] == numbers[None, :]).astype(jnp.int32), axis=0)]
    all_gather x0 -> x1, blocking collectives: none -> 37.2 us  [shards(): lax.all_gather(parents_own, ('lvl', 'dom'), axis=0, tiled=True)]
    all_gather x1, waiting for transfers between devices: 0.02 us -> 36 us  [shards(): lax.all_gather(leaf_moments, ('dom', 'lvl'), axis=0, tiled=True)]
  transfers between devices with their start and end apart: 6 -> 5, of which waited for: 2 -> 3; matrix products, arithmetic and copies ran while one was open for 27% -> 10% of each run, Pallas kernels for 0% -> 30%
where the time goes in v1:
time: 243 us; the launch traced here: 241 us
  Pallas kernels  83.4 us (34%)
  waiting for transfers between devices  58.5 us (24%)
  blocking collectives  37.2 us (15%)
  local copies, waits for them, and re-layouts  27.4 us (11%)
  between operations  16.4 us (7%)
  starting transfers between devices  12.9 us (5%)
  other arithmetic  5.38 us (2%)
    pallas_call x2, Pallas kernels, translate(): pl.pallas_call(functools.partial(translate_kernel, targets, sources), out...  53.4 us
    all_gather x1, blocking collectives, shards(): lax.all_gather(parents_own, ('lvl', 'dom'), axis=0, tiled=True)  37.2 us
    all_gather x1, waiting for transfers between devices, shards(): lax.all_gather(leaf_moments, ('dom', 'lvl'), axis=0, tiled=True)  36 us
    unnamed x45, local copies, waits for them, and re-layouts  26.6 us
    unnamed x4, waiting for transfers between devices  16 us
    pallas_call x1, Pallas kernels, near_field(): pl.pallas_call(near_kernel, out_shape=jax.ShapeDtypeStruct((4,) + charge....  12.1 us
    all_to_all x1, starting transfers between devices, shards(): lax.all_to_all(packed, 'dom', split_axis=0, concat_axis=0, tiled=True)  8.59 us
    pallas_call x1, Pallas kernels, ordered(): pl.pallas_call(order_kernel, out_shape=(jax.ShapeDtypeStruct(leaf_keys.sh...  7.47 us
  transfers between devices with their start and end apart: 5, of which 3 were waited for; matrix products, arithmetic and copies ran while one was open for 10% of the time, Pallas kernels for 30%

profile of v1, /device:TPU:1, one launch (start us, length us, event | category | flops | bytes accessed | tf_op | source)
XLA Modules:
  0.0 241.2 jit_solution(17047369627886603942)
XLA Ops:
  8.0 1.0 copy.34
  9.0 0.0 copy-start.1
  9.0 0.8 copy-done.1
  9.8 0.0 copy-start.4
  9.8 0.8 copy-done.4
  10.6 0.0 copy-start.6
  10.6 0.8 copy-done.6
  11.4 0.7 copy-done.10
  12.1 2.6 %block_moments.1 = (f32[256,128]{1,0:T(8,128)}, s32[1,128]{1,0:T(1,128)S(1)}) custom-call(f32[3,128,128]{2,1,0:T(8,128)S(1)} %bitcast.30, f32[128,128]{1,0:T(8,128)S(1)} %bitcast.36, s32[1,128]{1,0:T(1,128)S(1)} %bitcast.44, s32[64,128]{1,0:T(8,128)S(1)} %bitcast.40, f32[128,1]{1,0:T(8,128)S(1)} %copy-done.6), custom_call_target="tpu_custom_call" | custom-call | tf_op jit(solution)/shard_map/block_moments/pallas_call | solution.py:166
  14.6 8.6 %all-to-all-start = ((f32[32,8,128]{2,1,0:T(8,128)}), f32[32,8,128]{2,1,0:T(8,128)S(1)}, u32[]{:S(2)}, u32[]{:S(2)}) async-start(f32[32,8,128]{2,1,0:T(8,128)} %bitcast.13), calls=%async_computation | async-start | bytes 262144 | tf_op jit(solution)/shard_map/all_to_all | solution.py:487
  23.2 0.0 all-gather.2.cloned.1.call-start
  23.3 1.0 copy.25
  24.4 6.5 %all-to-all-done = f32[32,8,128]{2,1,0:T(8,128)S(1)} async-done(((f32[32,8,128]{2,1,0:T(8,128)}), f32[32,8,128]{2,1,0:T(8,128)S(1)}, u32[]{:S(2)}, u32[]{:S(2)}) %all-to-all-start) | async-done | bytes 131104 | tf_op jit(solution)/shard_map/all_to_all | solution.py:487
  30.9 0.8 copy-done.5
  31.6 2.5 %leaf_moments.1 = (f32[64,128]{1,0:T(8,128)}, f32[256,128]{1,0:T(8,128)}, s32[64,128]{1,0:T(8,128)S(1)}) custom-call(f32[256,128]{1,0:T(8,128)S(1)} %bitcast.33, s32[64,128]{1,0:T(8,128)S(1)} %bitcast.41, f32[8,128,128]{2,1,0:T(8,128)S(1)} %pad.7.ops_ref), custom_call_target="tpu_custom_call" | custom-call | tf_op jit(solution)/shard_map/leaf_moments/pallas_call | solution.py:213
  34.1 0.0 all-gather.2.cloned.1.call-update
  34.1 0.0 all-reduce.5.cloned.1.call-start
  34.2 2.5 %convert_reduce_fusion = s32[256]{0:T(256)S(1)} fusion(s32[4096]{0:T(1024)} %bitcast.48), kind=kLoop, calls=%fused_computation | loop fusion | flops 3145472 | bytes 17408 | tf_op jit(solution)/shard_map/reduce_sum | solution.py:256
  36.7 0.7 fusion
  37.3 0.8 convert_reduce_fusion.1
  38.2 0.7 fusion.1
  38.9 0.1 or.41
  39.0 0.0 copy-start.17
  39.0 0.0 copy-start.14
  39.0 0.0 copy-start.12
  39.0 0.0 copy-start.15
  39.0 14.8 %copy.26.ops_hbm = f32[316,81,81]{2,1,0:T(8,128)} copy(f32[316,81,81]{0,2,1:T(8,128)} %param.21) | data formatting | bytes 16586208 | tf_op args[6]
  53.8 0.0 copy-done.11
  53.8 0.1 copy.28
  53.9 0.0 copy-done.18
  53.9 0.6 dynamic-slice
  55.2 0.0 copy-done.16
  55.2 0.0 copy-done.13
  55.2 0.0 copy-done.17
  55.2 0.7 concatenate.7
  55.9 0.0 copy-done.14
  55.9 0.0 copy-done.12
  55.9 0.0 copy-done.15
  56.0 0.0 all-reduce.5.cloned.1.call-update
  56.0 0.0 reduce-scatter.2.cloned.1.call-start
  56.0 0.6 add_bitcast_fusion.leaf_ref
  56.7 7.5 %order.1 = (s32[64,128]{1,0:T(8,128)}, s32[32,128]{1,0:T(8,128)}) custom-call(s32[64,128]{1,0:T(8,128)} %add_bitcast_fusion.leaf_ref, s32[32,128]{1,0:T(8,128)} %bitcast.47), custom_call_target="tpu_custom_call" | custom-call | tf_op jit(solution)/shard_map/order/pallas_call | solution.py:269
  64.1 36.0 %all-gather.2.cloned.1.call-done.src_hbm = f32[8192,128]{1,0:T(8,128)} async-done(((f32[64,128]{1,0:T(8,128)}), f32[8192,128]{1,0:T(8,128)}) %all-gather.2.cloned.1.call-update) | async-done | bytes 4194320 | tf_op jit(solution)/shard_map/all_gather | solution.py:489
  100.1 2.2 copy-done
  102.3 0.8 copy-done.7
  103.1 35.4 %translate.2 = f32[256,128]{1,0:T(8,128)} custom-call(s32[8192]{0:T(1024)S(1)} %bitcast.42, s32[1]{0:T(128)} %bitcast.12.count, f32[8192,128]{1,0:T(8,128)S(1)} %copy-done, f32[316,81,81]{2,1,0:T(8,128)} %copy.26.ops_hbm), custom_call_target="tpu_custom_call" | custom-call | tf_op jit(solution)/shard_map/translate/pallas_call | solution.py:328
  138.4 0.0 reduce-scatter.2.cloned.1.call-update
  138.5 16.0 %all-reduce.5.cloned.1.call-done = f32[256,128]{1,0:T(8,128)} async-done(((f32[256,128]{1,0:T(8,128)}), f32[256,128]{1,0:T(8,128)}) %all-reduce.5.cloned.1.call-update) | async-done | bytes 131088
  154.5 0.7 constant_dynamic-slice_fusion
  155.1 37.2 %all_gather.7.src_hbm = f32[1024,128]{1,0:T(8,128)S(1)} all-gather(f32[8,128]{1,0:T(8,128)S(1)} %constant_dynamic-slice_fusion), channel_id=1, replica_groups=mesh['dom'=32,'lvl'=4] {'lvl','dom'}, dimensions={0}, use_global_device_ids=true | all-gather | bytes 528384 | tf_op jit(solution)/shard_map/all_gather | solution.py:491
  192.3 0.0 copy-done.9
  192.3 18.0 %translate.3.parent_ref = f32[64,128]{1,0:T(8,128)S(1)} custom-call(s32[4096]{0:T(1024)S(1)} %bitcast.43, s32[1]{0:T(128)} %bitcast.16.count, f32[1024,128]{1,0:T(8,128)S(1)} %all_gather.7.src_hbm, f32[316,81,81]{2,1,0:T(8,128)} %copy.26.ops_hbm), custom_call_target="tpu_custom_call" | custom-call | tf_op jit(solution)/shard_map/translate/pallas_call | solution.py:328
  210.3 0.0 copy-start.3
  210.3 0.0 reduce-scatter.2.cloned.1.call-done.leaf_ref
  210.3 0.0 copy-start.8
  210.3 0.8 copy-done.8
  211.1 2.2 slot_locals.1
  213.3 4.2 %all-to-all-start.1 = ((f32[32,8,128]{2,1,0:T(8,128)}), f32[32,8,128]{2,1,0:T(8,128)S(1)}, u32[]{:S(2)}, u32[]{:S(2)}) async-start(f32[32,8,128]{2,1,0:T(8,128)} %bitcast.18), calls=%async_computation.2 | async-start | bytes 262144 | tf_op jit(solution)/shard_map/all_to_all | solution.py:506
  217.5 0.0 copy-done.2
  217.5 12.1 %near_field.1.near_ref = f32[4,128,128]{2,1,0:T(8,128)S(1)} custom-call(f32[3,128,128]{2,1,0:T(8,128)S(1)} %bitcast.31, f32[128,128]{1,0:T(8,128)S(1)} %bitcast.37), custom_call_target="tpu_custom_call" | custom-call | flops 60000000 | bytes 524288 | tf_op jit(solution)/shard_map/near_field/pallas_call | solution.py:376
  229.6 0.0 all-to-all-done.1
  229.6 0.0 copy-done.3
  229.6 3.3 %far_field.1 = (f32[3,128,128]{2,1,0:T(8,128)S(1)}, f32[128,128]{1,0:T(8,128)}) custom-call(f32[3,128,128]{2,1,0:T(8,128)S(1)} %bitcast.32, f32[128,128]{1,0:T(8,128)S(1)} %bitcast.38, s32[1,128]{1,0:T(1,128)S(1)} %get-tuple-element.11.place_ref, f32[256,128]{1,0:T(8,128)S(1)} %bitcast.35, f32[4,128,128]{2,1,0:T(8,128)S(1)} %near_field.1.near_ref, ...), custom_call_target="tpu_custom_call" | custom-call | tf_op jit(solution)/shard_map/far_field/pallas_call | solution.py:443
  232.9 0.8 copy.33
  (21 shorter events, 0.2 us)
Async XLA Ops:
  9.0 0.8 copy-start.1
  9.8 0.8 copy-start.4
  10.6 0.8 copy-start.6
  11.4 0.7 copy-start.10
  14.6 16.2 %all-to-all-start = ((f32[32,8,128]{2,1,0:T(8,128)}), f32[32,8,128]{2,1,0:T(8,128)S(1)}, u32[]{:S(2)}, u32[]{:S(2)}) async-start(f32[32,8,128]{2,1,0:T(8,128)} %bitcast.13), calls=%async_computation | async-start | bytes 262144 | tf_op jit(solution)/shard_map/all_to_all | solution.py:487
  23.2 76.9 %all-gather.2.cloned.1.call-start = ((), (), s32[]{:S(2)}) async-start(), calls=%async_computation.3 | async-start | bytes 4227072 | tf_op jit(solution)/shard_map/all_gather | solution.py:489
  30.9 0.8 copy-start.5
  34.1 120.3 %all-reduce.5.cloned.1.call-start = ((), (), s32[]{:S(2)}) async-start(), calls=%async_computation.5 | async-start | bytes 262144
  39.0 14.8 %copy-start.11 = (f32[8,81,81]{2,0,1:T(8,128)S(1)}, f32[8,81,81]{2,0,1:T(8,128)}, u32[]{:S(2)}) copy-start(f32[8,81,81]{2,0,1:T(8,128)} %param.20) | copy-start | bytes 629860
  39.0 14.9 %copy-start.18 = (u32[128]{0:T(128)S(1)}, u32[128]{0:T(128)}, u32[]{:S(2)}) copy-start(u32[128]{0:T(128)} %constant.51) | copy-start | bytes 1540
  39.0 16.2 %copy-start.16 = (s32[1,1,2048]{2,1,0:T(1,128)S(1)}, s32[1,1,2048]{2,1,0:T(1,128)}, u32[]{:S(2)}) copy-start(s32[1,1,2048]{2,1,0:T(1,128)} %param.26) | copy-start | bytes 24580
  39.0 16.2 %copy-start.13 = (s32[1,1,2048]{2,1,0:T(1,128)S(1)}, s32[1,1,2048]{2,1,0:T(1,128)}, u32[]{:S(2)}) copy-start(s32[1,1,2048]{2,1,0:T(1,128)} %param.25) | copy-start | bytes 24580
  39.0 16.2 %copy-start.17 = (s32[1,1,2048]{2,1,0:T(1,128)S(1)}, s32[1,1,2048]{2,1,0:T(1,128)}, u32[]{:S(2)}) copy-start(s32[1,1,2048]{2,1,0:T(1,128)} %param.27) | copy-start | bytes 24580
  39.0 16.9 %copy-start.14 = (s32[1,1,4096]{2,1,0:T(1,128)S(1)}, s32[1,1,4096]{2,1,0:T(1,128)}, u32[]{:S(2)}) copy-start(s32[1,1,4096]{2,1,0:T(1,128)} %param.23) | copy-start | bytes 49156
  39.0 16.9 %copy-start.12 = (s32[1,1,4096]{2,1,0:T(1,128)S(1)}, s32[1,1,4096]{2,1,0:T(1,128)}, u32[]{:S(2)}) copy-start(s32[1,1,4096]{2,1,0:T(1,128)} %param.22) | copy-start | bytes 49156
  39.0 16.9 %copy-start.15 = (s32[1,1,4096]{2,1,0:T(1,128)S(1)}, s32[1,1,4096]{2,1,0:T(1,128)}, u32[]{:S(2)}) copy-start(s32[1,1,4096]{2,1,0:T(1,128)} %param.24) | copy-start | bytes 49156
  56.0 154.3 %reduce-scatter.2.cloned.1.call-start = ((), (), s32[]{:S(2)}) async-start(), calls=%async_computation.4 | async-start | bytes 163840 | tf_op jit(solution)/shard_map/reduce_scatter | solution.py:503
  100.1 2.2 copy-start
  102.3 0.8 copy-start.7
  103.1 89.2 %copy-start.9 = (s32[32,128]{1,0:T(8,128)S(1)}, s32[32,128]{1,0:T(8,128)}, u32[]{:S(2)}) copy-start(s32[32,128]{1,0:T(8,128)} %get-tuple-element.15) | copy-start | bytes 49156
  192.3 25.2 %copy-start.2 = (f32[16384]{0:T(1024)S(1)}, f32[16384]{0:T(1024)}, u32[]{:S(2)}) copy-start(f32[16384]{0:T(1024)} %param.16) | copy-start | bytes 196612
  210.3 19.3 %copy-start.3 = (f32[288,128]{1,0:T(8,128)S(1)}, f32[288,128]{1,0:T(8,128)}, u32[]{:S(2)}) copy-start(f32[288,128]{1,0:T(8,128)} %constant.11.clone.matrix_ref) | copy-start | bytes 442372
  210.3 0.8 copy-start.8
  213.3 16.3 %all-to-all-start.1 = ((f32[32,8,128]{2,1,0:T(8,128)}), f32[32,8,128]{2,1,0:T(8,128)S(1)}, u32[]{:S(2)}, u32[]{:S(2)}) async-start(f32[32,8,128]{2,1,0:T(8,128)} %bitcast.18), calls=%async_computation.2 | async-start | bytes 262144 | tf_op jit(solution)/shard_map/all_to_all | solution.py:506
Sparse Core Ops, SparseCore 0:
  34.2 65.8 all-gather.1
  138.6 15.8 reduce-scatter.1
Sparse Core Ops, SparseCore 1:
  56.1 98.3 all-reduce.4

commit v2 on v1

--- a/solution.py
+++ b/solution.py
@@ -19,6 +19,7 @@
 HIGH = lax.Precision.HIGHEST
 VMEM = pltpu.VMEM
 MIB = 1 << 20
+MESH = pl.DeviceIdType.MESH
 
 
 def dot(a, b, contract=((1,), (0,))):
@@ -341,7 +342,7 @@
     )(keys.reshape(-1), count, table, ops)
 
 
-def near_kernel(pos_ref, q_ref, out_ref):
+def near_groups(pos_ref, q_ref, out_ref, low, high):
     def group(g, carry):
         at = pl.ds(pl.multiple_of(g * 8, 8), 8)
         rows = [pos_ref[d, at, :] for d in range(3)] + [q_ref[at, :]]
@@ -368,20 +369,152 @@
                 out_ref[n, pl.ds(g * 8 + b, 1), :] = line
         return carry
 
-    lax.fori_loop(0, q_ref.shape[0] // 8, group, 0)
-
-
-def near_field(coords, charge):
+    lax.fori_loop(low, high, group, 0)
+
+
+PARTS = ((0, 16, 24, (2, 0, 1)), (24, 32, 48, (0, 1, 2)), (48, 56, 64, (1, 2, 0)))
+COPIES = 81
+
+
+def gather_kernel(leaf_ref, part_ref, pos_ref, q_ref, all_ref, parent_ref, near_ref, got_c, got_x, got_y, sum_c, sum_x, send_sem, recv_sem):
+    dom = lax.axis_index("dom")
+    here = (dom // 8, (dom // 2) % 4, lax.axis_index("lvl"))
+    core = dom % 2
+
+    def device(place, which):
+        return ((place[0] * 4 + place[1]) * 2 + which, place[2])
+
+    def moved(axis, by):
+        return tuple((v + by) % 4 if n == axis else v for n, v in enumerate(here))
+
+    twin = device(here, 1 - core)
+    barrier = pltpu.get_barrier_semaphore()
+    for axis in range(3):
+        for by in (1, 2, 3):
+            pl.semaphore_signal(barrier, inc=1, device_id=device(moved(axis, by), core), device_id_type=MESH)
+    pl.semaphore_signal(barrier, inc=1, device_id=twin, device_id_type=MESH)
+    all_ref[here[0], here[1], core, here[2]] = leaf_ref[...]
+    pl.semaphore_wait(barrier, 10)
+
+    started = []
+
+    def send(source, target, where):
+        n = len(started)
+        copy = pltpu.make_async_remote_copy(
+            src_ref=source,
+            dst_ref=target,
+            send_sem=send_sem.at[n],
+            recv_sem=recv_sem.at[n],
+            device_id=where,
+            device_id_type=MESH,
+        )
+        copy.start()
+        started.append(copy)
+        return copy
+
+    def block(done, axis, by, low, high):
+        y, x, z = (
+            slice(None) if n in done else ((here[n] + by) % 4 if n == axis else here[n]) for n in range(3)
+        )
+        return all_ref.at[y, x, core, z, slice(low, high)]
+
+    def put(ref, where):
+        return send(ref, ref, where)
+
+    def parents(done):
+        y, x, z = (slice(None) if n in done else here[n] for n in range(3))
+        return parent_ref.at[z, y, x, core]
+
+    waiting = {}
+
+    def stage(n):
+        if n == 0:
+            waiting["p"] = [send(part_ref.at[:, :, 1 - core], got_c, twin)]
+            return
+        for copy in waiting["p"]:
+            copy.wait_recv()
+        if n == 1:
+            sum_c[...] = part_ref[:, :, core] + got_c[...]
+            waiting["p"] = [
+                send(sum_c.at[:, (here[1] + by) % 4], got_x.at[by - 1], device(moved(1, by), core)) for by in (1, 2, 3)
+            ]
+        elif n == 2:
+            sum_x[...] = (sum_c[:, here[1]] + got_x[0]) + (got_x[1] + got_x[2])
+            waiting["p"] = [
+                send(sum_x.at[(here[0] + by) % 4], got_y.at[by - 1], device(moved(0, by), core)) for by in (1, 2, 3)
+            ]
+        elif n == 3:
+            parent_ref[here[2], here[0], here[1], core] = (sum_x[here[0]] + got_y[0]) + (got_y[1] + got_y[2])
+            waiting["p"] = [put(parents(()), device(moved(2, by), core)) for by in (1, 2, 3)]
+        elif n == 4:
+            waiting["p"] = [put(parents((2,)), device(moved(0, by), core)) for by in (1, 2, 3)]
+        elif n == 5:
+            waiting["p"] = [put(parents((2, 0)), device(moved(1, by), core)) for by in (1, 2, 3)]
+        elif n == 6:
+            waiting["p"] = [put(parents((2, 0, 1)), twin)]
+
+    fill = ((0, 1), (1, 3), (3, 5), (5, 8), (8, 12), (12, 16))
+    last = [put(block((), 0, 0, 0, 64), twin)]
+    for phase in range(3):
+        first = []
+        for low, middle, high, order in PARTS:
+            axis, done = order[phase], order[:phase]
+            first.append(
+                [put(block(done, axis, 0, low, high), device(moved(axis, by), core)) for by in (1, 3)]
+            )
+        stage(2 * phase)
+        near_groups(pos_ref, q_ref, near_ref, *fill[2 * phase])
+        second = []
+        for (low, middle, high, order), (right, left) in zip(PARTS, first):
+            axis, done = order[phase], order[:phase]
+            right.wait_recv()
+            a = put(block(done, axis, 3, low, middle), device(moved(axis, 1), core))
+            left.wait_recv()
+            b = put(block(done, axis, 1, middle, high), device(moved(axis, 3), core))
+            second.append((a, b))
+            last.append(put(block(done, axis, 3, low, high), twin))
+            last.append(put(block(done, axis, 1, low, high), twin))
+        stage(2 * phase + 1)
+        near_groups(pos_ref, q_ref, near_ref, *fill[2 * phase + 1])
+        for (low, middle, high, order), pair in zip(PARTS, second):
+            axis, done = order[phase], order[:phase]
+            for copy in pair:
+                copy.wait_recv()
+            last.append(put(block(done, axis, 2, low, high), twin))
+    stage(6)
+    for copy in last:
+        copy.wait_recv()
+    for copy in waiting["p"]:
+        copy.wait_recv()
+    for copy in started:
+        copy.wait_send()
+    assert len(started) == COPIES
+
+
+def gather(leaf, parts, coords, charge):
     whole = pl.BlockSpec(memory_space=VMEM)
+    f32 = jnp.float32
     return pl.pallas_call(
-        near_kernel,
-        out_shape=jax.ShapeDtypeStruct((4,) + charge.shape, jnp.float32),
-        in_specs=[whole] * 2,
-        out_specs=whole,
-        compiler_params=pltpu.CompilerParams(vmem_limit_bytes=16 * MIB),
-        cost_estimate=pl.CostEstimate(flops=60_000_000, bytes_accessed=1 << 19, transcendentals=2_000_000),
-        name="near_field",
-    )(coords, charge)
+        gather_kernel,
+        out_shape=(
+            jax.ShapeDtypeStruct((4, 4, 2, 4, LEAF_DEV, LANES), f32),
+            jax.ShapeDtypeStruct((4, 4, 4, 2, 8, LANES), f32),
+            jax.ShapeDtypeStruct((4,) + charge.shape, f32),
+        ),
+        in_specs=[whole] * 4,
+        out_specs=(whole,) * 3,
+        scratch_shapes=[
+            VMEM((4, 4, 8, LANES), f32),
+            VMEM((3, 4, 8, LANES), f32),
+            VMEM((3, 8, LANES), f32),
+            VMEM((4, 4, 8, LANES), f32),
+            VMEM((4, 8, LANES), f32),
+            pltpu.SemaphoreType.DMA((COPIES,)),
+            pltpu.SemaphoreType.DMA((COPIES,)),
+        ],
+        compiler_params=pltpu.CompilerParams(collective_id=0, has_side_effects=True, vmem_limit_bytes=24 * MIB),
+        name="gather",
+    )(leaf, parts.reshape(4, 4, 2, 8, LANES), coords, charge)
 
 
 def locals_kernel(leaf_ref, parent_ref, ids_ref, arrived_ref, ops_ref, out_ref):
@@ -486,10 +619,9 @@
     packed, place = block_moments(coords, charge, block_leaf.reshape(1, blocks), table)
     arrived = lax.all_to_all(packed, "dom", split_axis=0, concat_axis=0, tiled=True)
     leaf_moments, parents_part, ids = leaves(arrived, table, padded(m2m_ops))
-    source_table = lax.all_gather(leaf_moments, ("dom", "lvl"), axis=0, tiled=True)
-    parents_own = lax.psum_scatter(parents_part, "dom", scatter_dimension=0, tiled=True)
-    parent_table = lax.all_gather(parents_own, ("lvl", "dom"), axis=0, tiled=True)
-
+    source_table, parent_table, near = gather(leaf_moments, parents_part, coords, charge)
+    source_table = source_table.reshape(leaves_all, LANES)
+    parent_table = parent_table.reshape(parents_all, LANES)
     leaf_keys, leaf_count = listed(
         item_target.reshape(-1), item_source.reshape(-1), item_offset.reshape(-1), 4 * LEAF_DEV, leaves_all, 8192
     )
@@ -497,7 +629,6 @@
         coarse_target.reshape(-1), coarse_source.reshape(-1), coarse_offset.reshape(-1), LEAF_DEV, parents_all, 4096
     )
     leaf_keys, coarse_keys = ordered(leaf_keys, coarse_keys)
-    near = near_field(coords, charge)
 
     helper_terms = translate(leaf_keys, leaf_count, source_table, m2l_ops, 4 * LEAF_DEV)
     leaf_locals = lax.psum_scatter(helper_terms, "lvl", scatter_dimension=0, tiled=True)

time: 243 us -> 177 us (0.73)
  waiting for transfers between devices: 58.5 us -> 0.04 us
  Pallas kernels: 83.4 us -> 106 us
  blocking collectives: 37.2 us -> 15.1 us
  starting transfers between devices: 12.9 us -> 8.63 us
  local copies, waits for them, and re-layouts: 27.4 us -> 23.2 us
  other arithmetic: 5.38 us -> 8.27 us
    all_gather x1 -> x0, blocking collectives: 37.2 us -> none  [shards(): lax.all_gather(parents_own, ('lvl', 'dom'), axis=0, tiled=True)]
    all_gather x1 -> x0, waiting for transfers between devices: 36 us -> none  [shards(): lax.all_gather(leaf_moments, ('dom', 'lvl'), axis=0, tiled=True)]
    pallas_call x1, Pallas kernels: 12.1 us -> 36.2 us  [gather(): pl.pallas_call(gather_kernel, out_shape=(jax.ShapeDtypeStruct((4, 4, 2, 4...]
    unnamed x4 -> x1, waiting for transfers between devices: 16 us -> 0.02 us
    all_to_all x0 -> x1, blocking collectives: none -> 15.1 us  [shards(): lax.all_to_all(sent, 'dom', split_axis=0, concat_axis=0, tiled=True)]
    all_to_all x1, waiting for transfers between devices: 6.49 us -> 0.01 us  [shards(): lax.all_to_all(packed, 'dom', split_axis=0, concat_axis=0, tiled=True)]
    unnamed x45 -> x27, local copies, waits for them, and re-layouts: 26.6 us -> 22.3 us
    all_to_all x1 -> x0, starting transfers between devices: 4.16 us -> none  [shards(): lax.all_to_all(sent, 'dom', split_axis=0, concat_axis=0, tiled=True)]
  transfers between devices with their start and end apart: 5 -> 2, of which waited for: 3 -> 0; matrix products, arithmetic and copies ran while one was open for 10% -> 14% of each run, Pallas kernels for 30% -> 14%
where the time goes in v2:
time: 177 us; the launch traced here: 176 us
  Pallas kernels  106 us (60%)
  local copies, waits for them, and re-layouts  23.2 us (13%)
  blocking collectives  15.1 us (9%)
  between operations  14.2 us (8%)
  starting transfers between devices  8.63 us (5%)
  other arithmetic  8.27 us (5%)
    pallas_call x2, Pallas kernels, translate(): pl.pallas_call(functools.partial(translate_kernel, targets, sources), out...  53.6 us
    pallas_call x1, Pallas kernels, gather(): pl.pallas_call(gather_kernel, out_shape=(jax.ShapeDtypeStruct((4, 4, 2, 4...  36.2 us
    unnamed x27, local copies, waits for them, and re-layouts  22.3 us
    all_to_all x1, blocking collectives, shards(): lax.all_to_all(sent, 'dom', split_axis=0, concat_axis=0, tiled=True)  15.1 us
    all_to_all x1, starting transfers between devices, shards(): lax.all_to_all(packed, 'dom', split_axis=0, concat_axis=0, tiled=True)  8.59 us
    pallas_call x1, Pallas kernels, ordered(): pl.pallas_call(order_kernel, out_shape=(jax.ShapeDtypeStruct(leaf_keys.sh...  7.48 us
  transfers between devices with their start and end apart: 2, of which 0 were waited for; matrix products, arithmetic and copies ran while one was open for 14% of the time, Pallas kernels for 14%

profile of v2, /device:TPU:1, one launch (start us, length us, event | category | flops | bytes accessed | tf_op | source)
XLA Modules:
  0.0 175.9 jit_solution(14820809253590899405)
XLA Ops:
  7.2 1.0 copy.30
  8.1 0.0 copy-start
  8.1 0.8 copy-done
  9.0 0.0 copy-start.3
  9.0 0.8 copy-done.3
  9.7 0.0 copy-start.5
  9.7 0.8 copy-done.5
  10.6 0.0 copy-start.9
  10.6 0.7 copy-done.9
  11.2 2.6 %block_moments.1 = (f32[256,128]{1,0:T(8,128)}, s32[1,128]{1,0:T(1,128)S(1)}) custom-call(f32[3,128,128]{2,1,0:T(8,128)S(1)} %bitcast.33, f32[128,128]{1,0:T(8,128)S(1)} %bitcast.38, s32[1,128]{1,0:T(1,128)S(1)} %bitcast.50, s32[64,128]{1,0:T(8,128)S(1)} %bitcast.46, f32[128,1]{1,0:T(8,128)S(1)} %copy-done.5), custom_call_target="tpu_custom_call" | custom-call | tf_op jit(solution)/shard_map/block_moments/pallas_call | solution.py:167
  13.8 8.6 %all-to-all-start = ((f32[32,8,128]{2,1,0:T(8,128)}), f32[32,8,128]{2,1,0:T(8,128)S(1)}, u32[]{:S(2)}, u32[]{:S(2)}) async-start(f32[32,8,128]{2,1,0:T(8,128)} %bitcast.13), calls=%async_computation | async-start | bytes 262144 | tf_op jit(solution)/shard_map/all_to_all | solution.py:620
  22.4 0.0 reduce-scatter.2.cloned.1.call-start
  22.5 2.5 %convert_reduce_fusion = s32[256]{0:T(256)S(1)} fusion(s32[4096]{0:T(1024)} %bitcast.54), kind=kLoop, calls=%fused_computation | loop fusion | flops 3145472 | bytes 17408 | tf_op jit(solution)/shard_map/reduce_sum | solution.py:257
  24.9 0.7 fusion
  25.7 0.7 broadcast_shift-left_fusion
  26.4 0.9 convert_reduce_fusion.1
  27.2 0.7 fusion.1
  27.9 0.7 broadcast_shift-left_fusion.1
  28.6 0.7 or_or_fusion
  29.4 0.7 or_or_fusion.1
  30.1 1.0 copy.21
  31.2 0.1 or.41
  31.3 0.0 copy-start.4
  31.3 0.0 copy-start.1
  31.3 14.8 %copy.22.ops_hbm = f32[316,81,81]{2,1,0:T(8,128)} copy(f32[316,81,81]{0,2,1:T(8,128)} %param.21) | data formatting | bytes 16586208 | tf_op args[6]
  46.1 0.7 concatenate.7
  46.8 0.6 add_bitcast_fusion.leaf_ref
  47.4 7.5 %order.1 = (s32[64,128]{1,0:T(8,128)}, s32[32,128]{1,0:T(8,128)}) custom-call(s32[64,128]{1,0:T(8,128)} %add_bitcast_fusion.leaf_ref, s32[32,128]{1,0:T(8,128)} %bitcast.53), custom_call_target="tpu_custom_call" | custom-call | tf_op jit(solution)/shard_map/order/pallas_call | solution.py:270
  54.9 0.0 all-to-all-done
  54.9 0.0 copy-done.4
  54.9 1.8 %leaf_moments.1 = (f32[64,128]{1,0:T(8,128)S(1)}, f32[256,128]{1,0:T(8,128)S(1)}, s32[64,128]{1,0:T(8,128)S(1)}) custom-call(f32[256,128]{1,0:T(8,128)S(1)} %bitcast.36, s32[64,128]{1,0:T(8,128)S(1)} %bitcast.47, f32[8,128,128]{2,1,0:T(8,128)S(1)} %pad.7.ops_ref), custom_call_target="tpu_custom_call" | custom-call | tf_op jit(solution)/shard_map/leaf_moments/pallas_call | solution.py:214
  56.7 0.0 copy-done.1
  56.7 36.2 %gather.1 = (f32[4,4,2,4,64,128]{5,4,3,2,1,0:T(8,128)S(1)}, f32[4,4,4,2,8,128]{5,4,3,2,1,0:T(8,128)S(1)}, f32[4,128,128]{2,1,0:T(8,128)S(1)}) custom-call(f32[64,128]{1,0:T(8,128)S(1)} %get-tuple-element.17.leaf_ref, f32[4,4,2,8,128]{4,3,2,1,0:T(8,128)S(1)} %bitcast.45, f32[3,128,128]{2,1,0:T(8,128)S(1)} %bitcast.34, f32[128,128]{1,0:T(8,128)S(1)} %bitcast.39), custom_call_target="tpu_custom_call" | custom-call | tf_op jit(solution)/shard_map/gather/pallas_call | solution.py:497
  92.9 0.0 copy-start.6
  92.9 0.7 copy-done.6
  93.7 0.0 copy-start.10
  93.7 0.0 copy-start.8
  93.7 35.7 %translate.2 = f32[256,128]{1,0:T(8,128)} custom-call(s32[8192]{0:T(1024)S(1)} %bitcast.48, s32[1]{0:T(128)} %bitcast.12.count, f32[8192,128]{1,0:T(8,128)S(1)} %bitcast.32, f32[316,81,81]{2,1,0:T(8,128)} %copy.22.ops_hbm), custom_call_target="tpu_custom_call" | custom-call | tf_op jit(solution)/shard_map/translate/pallas_call | solution.py:329
  129.4 0.0 reduce-scatter.2.cloned.1.call-update
  129.5 0.0 copy-done.10
  129.5 0.1 copy.24
  129.6 0.0 copy-done.8
  129.6 0.0 copy-start.2
  129.6 17.9 %translate.3.parent_ref = f32[64,128]{1,0:T(8,128)S(1)} custom-call(s32[4096]{0:T(1024)S(1)} %bitcast.49, s32[1]{0:T(128)} %bitcast.18.count, f32[1024,128]{1,0:T(8,128)S(1)} %bitcast.41, f32[316,81,81]{2,1,0:T(8,128)} %copy.22.ops_hbm), custom_call_target="tpu_custom_call" | custom-call | tf_op jit(solution)/shard_map/translate/pallas_call | solution.py:329
  147.5 0.0 reduce-scatter.2.cloned.1.call-done.leaf_ref
  147.5 0.0 copy-start.7
  147.5 0.7 copy-done.7
  148.3 1.5 slot_locals.1
  149.8 15.1 %all_to_all.22 = f32[32,8,128]{2,1,0:T(8,128)S(1)} all-to-all(f32[32,8,128]{2,1,0:T(8,128)S(1)} %bitcast.42), channel_id=1, replica_groups=mesh['dom'=32,'lvl'=4] {'dom'}, dimensions={0} | all-to-all | bytes 262144 | tf_op jit(solution)/shard_map/all_to_all | solution.py:637
  164.9 0.0 copy-done.2
  164.9 3.3 %far_field.1 = (f32[3,128,128]{2,1,0:T(8,128)S(1)}, f32[128,128]{1,0:T(8,128)}) custom-call(f32[3,128,128]{2,1,0:T(8,128)S(1)} %bitcast.35, f32[128,128]{1,0:T(8,128)S(1)} %bitcast.40, s32[1,128]{1,0:T(1,128)S(1)} %get-tuple-element.14.place_ref, f32[256,128]{1,0:T(8,128)S(1)} %bitcast.43, f32[4,128,128]{2,1,0:T(8,128)S(1)} %get-tuple-element.23.near_ref, ...), custom_call_target="tpu_custom_call" | custom-call | tf_op jit(solution)/shard_map/far_field/pallas_call | solution.py:576
  168.2 0.8 copy.29
  (7 shorter events, 0.1 us)
Async XLA Ops:
  8.1 0.8 copy-start
  9.0 0.8 copy-start.3
  9.7 0.8 copy-start.5
  10.6 0.7 copy-start.9
  13.8 41.1 %all-to-all-start = ((f32[32,8,128]{2,1,0:T(8,128)}), f32[32,8,128]{2,1,0:T(8,128)S(1)}, u32[]{:S(2)}, u32[]{:S(2)}) async-start(f32[32,8,128]{2,1,0:T(8,128)} %bitcast.13), calls=%async_computation | async-start | bytes 262144 | tf_op jit(solution)/shard_map/all_to_all | solution.py:620
  22.4 125.1 %reduce-scatter.2.cloned.1.call-start = ((), (), s32[]{:S(2)}) async-start(), calls=%async_computation.3 | async-start | bytes 163840 | tf_op jit(solution)/shard_map/reduce_scatter | solution.py:634
  31.3 23.6 %copy-start.4 = (s32[8192]{0:T(1024)S(1)}, s32[8192]{0:T(1024)}, u32[]{:S(2)}) copy-start(s32[8192]{0:T(1024)} %param.18) | copy-start | bytes 98308
  31.3 25.4 %copy-start.1 = (f32[16384]{0:T(1024)S(1)}, f32[16384]{0:T(1024)}, u32[]{:S(2)}) copy-start(f32[16384]{0:T(1024)} %param.16) | copy-start | bytes 196612
  92.9 0.8 copy-start.6
  93.7 35.8 %copy-start.10 = (f32[8,81,81]{2,0,1:T(8,128)S(1)}, f32[8,81,81]{2,0,1:T(8,128)}, u32[]{:S(2)}) copy-start(f32[8,81,81]{2,0,1:T(8,128)} %param.20) | copy-start | bytes 629860
  93.7 35.9 %copy-start.8 = (s32[32,128]{1,0:T(8,128)S(1)}, s32[32,128]{1,0:T(8,128)}, u32[]{:S(2)}) copy-start(s32[32,128]{1,0:T(8,128)} %get-tuple-element.20) | copy-start | bytes 49156
  129.6 35.3 %copy-start.2 = (f32[288,128]{1,0:T(8,128)S(1)}, f32[288,128]{1,0:T(8,128)}, u32[]{:S(2)}) copy-start(f32[288,128]{1,0:T(8,128)} %constant.11.clone.matrix_ref) | copy-start | bytes 442372
  147.5 0.8 copy-start.7
Sparse Core Ops, SparseCore 0:
  129.6 15.7 reduce-scatter.1

commit v3 on v2

--- a/solution.py
+++ b/solution.py
@@ -1,4 +1,5 @@
 import functools
+import itertools
 import math
 
 import jax
@@ -225,58 +226,51 @@
     )(arrived, table, ops)
 
 
-def bitonic(x):
-    rows = x.shape[0]
-    index = iota(x.shape, 0) * LANES + iota(x.shape, 1)
-    size = rows * LANES
-    span = 2
+def bitonic_stages(size):
+    out, span = [], 2
     while span <= size:
         step = span // 2
         while step >= 1:
-            axis, shift, extent = (1, step, LANES) if step < LANES else (0, step // LANES, rows)
-            second = (index & step) != 0
-            other = jnp.where(
-                second, pltpu.roll(x, shift, axis), pltpu.roll(x, extent - shift, axis)
-            )
-            ascending = (index & span) == 0
-            take_small = ascending != second
-            x = jnp.where(take_small, jnp.minimum(x, other), jnp.maximum(x, other))
+            out.append((span, step))
             step //= 2
         span *= 2
-    return x
-
-
-def order_kernel(leaf_ref, coarse_ref, leaf_out, coarse_out):
-    leaf_out[...] = bitonic(leaf_ref[...])
-    coarse_out[...] = bitonic(coarse_ref[...])
-
-
-def listed(target, source, offset, targets, none, room):
-    key = (target << 23) | (source << 9) | offset
-    numbers = jnp.arange(targets, dtype=jnp.int32)
-    count = jnp.sum((target[:, None] == numbers[None, :]).astype(jnp.int32), axis=0)
-    fours = (count + 3) >> 2
-    missing = fours * 4 - count
-    turn = jnp.arange(3, dtype=jnp.int32)[:, None]
-    fill_target = jnp.where(turn < missing[None, :], numbers[None, :], targets - 1)
-    fill = ((fill_target << 23) | (none << 9)).reshape(-1)
-    rest = jnp.full((room - key.shape[0] - fill.shape[0],), ((targets - 1) << 23) | (none << 9), jnp.int32)
-    keys = jnp.concatenate([key, fill, rest]).reshape(room // LANES, LANES)
-    return keys, jnp.sum(fours).reshape(1)
-
-
-def ordered(leaf_keys, coarse_keys):
-    whole = pl.BlockSpec(memory_space=VMEM)
-    return pl.pallas_call(
-        order_kernel,
-        out_shape=(
-            jax.ShapeDtypeStruct(leaf_keys.shape, jnp.int32),
-            jax.ShapeDtypeStruct(coarse_keys.shape, jnp.int32),
-        ),
-        in_specs=[whole] * 2,
-        out_specs=(whole,) * 2,
-        name="order",
-    )(leaf_keys, coarse_keys)
+    return out
+
+
+def bitonic_stage(x, span, step):
+    rows = x.shape[0]
+    index = iota(x.shape, 0) * LANES + iota(x.shape, 1)
+    axis, shift, extent = (1, step, LANES) if step < LANES else (0, step // LANES, rows)
+    second = (index & step) != 0
+    other = jnp.where(second, pltpu.roll(x, shift, axis), pltpu.roll(x, extent - shift, axis))
+    take_small = ((index & span) == 0) != second
+    return jnp.where(take_small, jnp.minimum(x, other), jnp.maximum(x, other))
+
+
+def write_keys(items, targets, none, keys_ref, count_ref):
+    target_ref, source_ref, offset_ref = items
+    rows = target_ref.shape[0]
+    keys_ref[...] = jnp.full(keys_ref.shape, ((targets - 1) << 23) | (none << 9), jnp.int32)
+    keys_ref[0:rows, :] = (target_ref[...] << 23) | (source_ref[...] << 9) | offset_ref[...]
+    numbers = iota((targets, LANES), 0)
+    count = jnp.zeros((targets, LANES), jnp.float32)
+    for r in range(rows):
+        count = count + (numbers == target_ref[r : r + 1, :]).astype(jnp.float32)
+    count = jnp.sum(count, axis=1, keepdims=True)
+    fours = jnp.zeros((1, 1), jnp.int32)
+    for p in range((targets + LANES - 1) // LANES):
+        size = min(LANES, targets - p * LANES)
+        part = count[p * LANES : p * LANES + size]
+        diagonal = iota((size, LANES), 0) == iota((size, LANES), 1)
+        line = jnp.sum(jnp.where(diagonal, part, 0.0), axis=0, keepdims=True).astype(jnp.int32)
+        filled = (line + 3) >> 2
+        fours = fours + jnp.sum(filled.astype(jnp.float32), axis=1, keepdims=True).astype(jnp.int32)
+        own = iota((1, LANES), 1) + p * LANES
+        for turn in range(3):
+            goal = jnp.where(turn < filled * 4 - line, own, targets - 1)
+            at = rows + 3 * p + turn
+            keys_ref[at : at + 1, :] = (goal << 23) | (none << 9)
+    count_ref[...] = jnp.broadcast_to(fours, count_ref.shape)
 
 
 def translate_kernel(targets, sources, keys, count, src_hbm, ops_hbm, out_ref, ops, src, acc, sems):
@@ -307,7 +301,7 @@
             acc[target] += total
         return carry
 
-    lax.fori_loop(0, (count[0] + 1) // 2, step, 0)
+    lax.fori_loop(0, (count[0, 0] + 1) // 2, step, 0)
     diagonal = iota((COEF, LANES), 0) == iota((COEF, LANES), 1)
 
     def finish(i, carry):
@@ -376,7 +370,10 @@
 COPIES = 81
 
 
-def gather_kernel(leaf_ref, part_ref, pos_ref, q_ref, all_ref, parent_ref, near_ref, got_c, got_x, got_y, sum_c, sum_x, send_sem, recv_sem):
+def gather_kernel(
+    leaf_ref, part_ref, pos_ref, q_ref, lt_ref, ls_ref, lo_ref, ct_ref, cs_ref, co_ref,
+    all_ref, parent_ref, near_ref, lkeys_ref, lcount_ref, ckeys_ref, ccount_ref, got_c, got_x, got_y, sum_c, sum_x, send_sem, recv_sem
+):
     dom = lax.axis_index("dom")
     here = (dom // 8, (dom // 2) % 4, lax.axis_index("lvl"))
     core = dom % 2
@@ -453,7 +450,33 @@
         elif n == 6:
             waiting["p"] = [put(parents((2, 0, 1)), twin)]
 
-    fill = ((0, 1), (1, 3), (3, 5), (5, 8), (8, 12), (12, 16))
+    sorts = [
+        (keys, stage)
+        for pair in itertools.zip_longest(
+            *([(keys, stage) for stage in bitonic_stages(keys.shape[0] * LANES)] for keys in (lkeys_ref, ckeys_ref))
+        )
+        for keys, stage in filter(None, pair)
+    ]
+
+    def sort(low, high):
+        now = {}
+        for keys, stage in sorts[low:high]:
+            name = id(keys)
+            if name not in now:
+                now[name] = (keys, keys[...])
+            now[name] = (keys, bitonic_stage(now[name][1], *stage))
+        for keys, value in now.values():
+            keys[...] = value
+
+    def fill(n):
+        if n == 0:
+            write_keys((lt_ref, ls_ref, lo_ref), 4 * LEAF_DEV, 8192, lkeys_ref, lcount_ref)
+            write_keys((ct_ref, cs_ref, co_ref), LEAF_DEV, 1024, ckeys_ref, ccount_ref)
+        elif n < 4:
+            sort(60 * (n - 1), 60 * n)
+        else:
+            near_groups(pos_ref, q_ref, near_ref, *((0, 7), (7, 14), (14, 16))[n - 4])
+
     last = [put(block((), 0, 0, 0, 64), twin)]
     for phase in range(3):
         first = []
@@ -463,7 +486,7 @@
                 [put(block(done, axis, 0, low, high), device(moved(axis, by), core)) for by in (1, 3)]
             )
         stage(2 * phase)
-        near_groups(pos_ref, q_ref, near_ref, *fill[2 * phase])
+        fill(2 * phase)
         second = []
         for (low, middle, high, order), (right, left) in zip(PARTS, first):
             axis, done = order[phase], order[:phase]
@@ -475,13 +498,14 @@
             last.append(put(block(done, axis, 3, low, high), twin))
             last.append(put(block(done, axis, 1, low, high), twin))
         stage(2 * phase + 1)
-        near_groups(pos_ref, q_ref, near_ref, *fill[2 * phase + 1])
+        fill(2 * phase + 1)
         for (low, middle, high, order), pair in zip(PARTS, second):
             axis, done = order[phase], order[:phase]
             for copy in pair:
                 copy.wait_recv()
             last.append(put(block(done, axis, 2, low, high), twin))
     stage(6)
+    fill(6)
     for copy in last:
         copy.wait_recv()
     for copy in waiting["p"]:
@@ -491,7 +515,7 @@
     assert len(started) == COPIES
 
 
-def gather(leaf, parts, coords, charge):
+def gather(leaf, parts, coords, charge, leaf_items, coarse_items):
     whole = pl.BlockSpec(memory_space=VMEM)
     f32 = jnp.float32
     return pl.pallas_call(
@@ -500,9 +524,13 @@
             jax.ShapeDtypeStruct((4, 4, 2, 4, LEAF_DEV, LANES), f32),
             jax.ShapeDtypeStruct((4, 4, 4, 2, 8, LANES), f32),
             jax.ShapeDtypeStruct((4,) + charge.shape, f32),
+            jax.ShapeDtypeStruct((64, LANES), jnp.int32),
+            jax.ShapeDtypeStruct((1, LANES), jnp.int32),
+            jax.ShapeDtypeStruct((32, LANES), jnp.int32),
+            jax.ShapeDtypeStruct((1, LANES), jnp.int32),
         ),
-        in_specs=[whole] * 4,
-        out_specs=(whole,) * 3,
+        in_specs=[whole] * 10,
+        out_specs=(whole,) * 7,
         scratch_shapes=[
             VMEM((4, 4, 8, LANES), f32),
             VMEM((3, 4, 8, LANES), f32),
@@ -514,39 +542,83 @@
         ],
         compiler_params=pltpu.CompilerParams(collective_id=0, has_side_effects=True, vmem_limit_bytes=24 * MIB),
         name="gather",
-    )(leaf, parts.reshape(4, 4, 2, 8, LANES), coords, charge)
-
-
-def locals_kernel(leaf_ref, parent_ref, ids_ref, arrived_ref, ops_ref, out_ref):
+    )(
+        leaf, parts.reshape(4, 4, 2, 8, LANES), coords, charge,
+        *(a.reshape(-1, LANES) for a in leaf_items + coarse_items),
+    )
+
+
+def far_kernel(
+    terms_ref, parent_ref, ids_ref, arrived_ref, ops_ref, pos_ref, q_ref, place_ref, near_ref, matrix_ref,
+    force_ref, phi_ref, got, sent, returned, turned, lines, send_sem, recv_sem
+):
+    dom, lvl = lax.axis_index("dom"), lax.axis_index("lvl")
+    blocks = q_ref.shape[0]
+    barrier = pltpu.get_barrier_semaphore()
+
+    def greet(d, carry):
+        pl.semaphore_signal(barrier, inc=1, device_id=((dom + d) % 32, lvl), device_id_type=MESH)
+        return carry
+
+    for by in (1, 2, 3):
+        pl.semaphore_signal(barrier, inc=1, device_id=(dom, (lvl + by) % 4), device_id_type=MESH)
+    lax.fori_loop(1, 32, greet, 0)
+    pl.semaphore_wait(barrier, 34)
+
+    shared = []
+    for by in (1, 2, 3):
+        goal = (lvl + by) % 4
+        copy = pltpu.make_async_remote_copy(
+            src_ref=terms_ref.at[goal],
+            dst_ref=got.at[by - 1],
+            send_sem=send_sem.at[31 + by],
+            recv_sem=recv_sem.at[31 + by],
+            device_id=(dom, goal),
+            device_id_type=MESH,
+        )
+        copy.start()
+        shared.append(copy)
+
     octant = ids_ref[...] & 7
     parent = parent_ref[...]
-    total = leaf_ref[...]
+    total = terms_ref[lvl]
     for o in range(8):
         total = total + dot(jnp.where(octant == o, parent, 0.0), ops_ref[o], ((1,), (1,)))
     tags = arrived_ref[:, 127:128].astype(jnp.int32)
     member = (iota((arrived_ref.shape[0], LEAF_DEV), 1) + 1 == tags).astype(jnp.float32)
-    out_ref[...] = dot(member, total)
-
-
-def slot_locals(leaf_locals, parent_locals, ids, arrived, ops):
-    whole = pl.BlockSpec(memory_space=VMEM)
-    return pl.pallas_call(
-        locals_kernel,
-        out_shape=jax.ShapeDtypeStruct(arrived.shape, jnp.float32),
-        in_specs=[whole] * 5,
-        out_specs=whole,
-        compiler_params=pltpu.CompilerParams(vmem_limit_bytes=16 * MIB),
-        name="slot_locals",
-    )(leaf_locals, parent_locals, ids, arrived, ops)
-
-
-def far_kernel(pos_ref, q_ref, place_ref, returned_ref, near_ref, matrix_ref, force_ref, phi_ref, turned, lines):
-    blocks = q_ref.shape[0]
-    spread = (iota((32 * CAP, blocks), 0) == place_ref[...]).astype(jnp.float32)
-    columns = dot(returned_ref[...], spread, ((0,), (0,)))
-    lines[...] = dot(matrix_ref[...], columns)
+    for copy in shared:
+        copy.wait_recv()
+    total = (total + got[0]) + (got[1] + got[2])
+    sent[...] = dot(member, total).reshape(sent.shape)
+
+    def message(d):
+        goal = (dom + d) % 32
+        return pltpu.make_async_remote_copy(
+            src_ref=sent.at[goal],
+            dst_ref=returned.at[dom],
+            send_sem=send_sem.at[d],
+            recv_sem=recv_sem.at[d],
+            device_id=(goal, lvl),
+            device_id_type=MESH,
+        )
+
+    def start(d, carry):
+        message(d).start()
+        return carry
+
+    lax.fori_loop(1, 32, start, 0)
+    returned[dom] = sent[dom]
     for d in range(3):
         turned[d] = pos_ref[d].T
+    spread = (iota((32 * CAP, blocks), 0) == place_ref[...]).astype(jnp.float32)
+
+    def receive(d, carry):
+        message(d).wait_recv()
+        return carry
+
+    lax.fori_loop(1, 32, receive, 0)
+    columns = dot(returned[...].reshape(32 * CAP, LANES), spread, ((0,), (0,)))
+    lines[...] = dot(matrix_ref[...], columns)
 
     def chunk(i, carry):
         at = pl.ds(pl.multiple_of(i * 32, 32), 32)
@@ -570,24 +642,41 @@
         force_ref[d] = near_ref[d] - charge * turned[d].T
     phi_ref[...] = near_ref[3] + turned[3].T
 
-
-def far_field(coords, charge, place, returned, near):
+    def leave(d, carry):
+        message(d).wait_send()
+        return carry
+
+    lax.fori_loop(1, 32, leave, 0)
+    for copy in shared:
+        copy.wait_send()
+
+
+def far_field(terms, parent_locals, ids, arrived, ops, coords, charge, place, near):
     whole = pl.BlockSpec(memory_space=VMEM)
+    f32 = jnp.float32
     return pl.pallas_call(
         far_kernel,
         out_shape=(
-            jax.ShapeDtypeStruct(coords.shape, jnp.float32),
-            jax.ShapeDtypeStruct(charge.shape, jnp.float32),
+            jax.ShapeDtypeStruct(coords.shape, f32),
+            jax.ShapeDtypeStruct(charge.shape, f32),
         ),
-        in_specs=[whole] * 6,
+        in_specs=[whole] * 10,
         out_specs=(whole, whole),
         scratch_shapes=[
-            VMEM((4,) + charge.shape, jnp.float32),
-            VMEM((G_ROWS, LANES), jnp.float32),
+            VMEM((3, LEAF_DEV, LANES), f32),
+            VMEM((32, CAP, LANES), f32),
+            VMEM((32, CAP, LANES), f32),
+            VMEM((4,) + charge.shape, f32),
+            VMEM((G_ROWS, LANES), f32),
+            pltpu.SemaphoreType.DMA((35,)),
+            pltpu.SemaphoreType.DMA((35,)),
         ],
-        compiler_params=pltpu.CompilerParams(vmem_limit_bytes=16 * MIB),
+        compiler_params=pltpu.CompilerParams(collective_id=1, has_side_effects=True, vmem_limit_bytes=16 * MIB),
         name="far_field",
-    )(coords, charge, place, returned, near, jnp.asarray(gradient_matrix()))
+    )(
+        terms.reshape(GROUP, LEAF_DEV, LANES), parent_locals, ids, arrived, ops, coords, charge, place, near,
+        jnp.asarray(gradient_matrix()),
+    )
 
 
 def padded(ops):
@@ -619,23 +708,21 @@
     packed, place = block_moments(coords, charge, block_leaf.reshape(1, blocks), table)
     arrived = lax.all_to_all(packed, "dom", split_axis=0, concat_axis=0, tiled=True)
     leaf_moments, parents_part, ids = leaves(arrived, table, padded(m2m_ops))
-    source_table, parent_table, near = gather(leaf_moments, parents_part, coords, charge)
+    source_table, parent_table, near, leaf_keys, leaf_count, coarse_keys, coarse_count = gather(
+        leaf_moments,
+        parents_part,
+        coords,
+        charge,
+        (item_target, item_source, item_offset),
+        (coarse_target, coarse_source, coarse_offset),
+    )
     source_table = source_table.reshape(leaves_all, LANES)
     parent_table = parent_table.reshape(parents_all, LANES)
-    leaf_keys, leaf_count = listed(
-        item_target.reshape(-1), item_source.reshape(-1), item_offset.reshape(-1), 4 * LEAF_DEV, leaves_all, 8192
+    parent_locals = translate(coarse_keys, coarse_count, parent_table, m2l_ops, LEAF_DEV)
+    terms = translate(leaf_keys, leaf_count, source_table, m2l_ops, 4 * LEAF_DEV)
+    forces, potential = far_field(
+        terms, parent_locals, ids, arrived, padded(l2l_ops), coords, charge, place, near
     )
-    coarse_keys, coarse_count = listed(
-        coarse_target.reshape(-1), coarse_source.reshape(-1), coarse_offset.reshape(-1), LEAF_DEV, parents_all, 4096
-    )
-    leaf_keys, coarse_keys = ordered(leaf_keys, coarse_keys)
-
-    helper_terms = translate(leaf_keys, leaf_count, source_table, m2l_ops, 4 * LEAF_DEV)
-    leaf_locals = lax.psum_scatter(helper_terms, "lvl", scatter_dimension=0, tiled=True)
-    parent_locals = translate(coarse_keys, coarse_count, parent_table, m2l_ops, LEAF_DEV)
-    sent = slot_locals(leaf_locals, parent_locals, ids, arrived, padded(l2l_ops))
-    returned = lax.all_to_all(sent, "dom", split_axis=0, concat_axis=0, tiled=True)
-    forces, potential = far_field(coords, charge, place, returned, near)
     return forces.reshape(3, blocks * LANES), potential.reshape(blocks * LANES)
 
 

time: 177 us -> 141 us (0.80)
  blocking collectives: 15.1 us -> 0 us
  between operations: 14.2 us -> 0.87 us
  other arithmetic: 8.27 us -> 0 us
  Pallas kernels: 106 us -> 109 us
    all_to_all x1 -> x0, blocking collectives: 15.1 us -> none  [shards(): lax.all_to_all(sent, 'dom', split_axis=0, concat_axis=0, tiled=True)]
    pallas_call x1, Pallas kernels: 3.3 us -> 17 us  [far_field(): pl.pallas_call(far_kernel, out_shape=(jax.ShapeDtypeStruct(coords.shape,...]
    pallas_call x2 -> x0, Pallas kernels: 8.99 us -> none  [the longest x1 7.48 us: ordered(): pl.pallas_call(order_kernel, out_shape=(jax.ShapeDtypeStruct(leaf_keys.sh...]
    reduce_sum x4 -> x0, other arithmetic: 4.74 us -> none  [the longest x2 3.34 us: listed(): jnp.sum((target[:, None] == numbers[None, :]).astype(jnp.int32), axis=0)]
    pallas_call x2, Pallas kernels: 53.6 us -> 51.6 us  [translate(): pl.pallas_call(functools.partial(translate_kernel, targets, sources), out...]
    unnamed x27 -> x34, local copies, waits for them, and re-layouts: 22.3 us -> 21.6 us
  transfers between devices with their start and end apart: 2 -> 1, of which waited for: 0 -> 0; matrix products, arithmetic and copies ran while one was open for 14% -> 11% of each run, Pallas kernels for 14% -> 0%
where the time goes in v3:
time: 141 us; the launch traced here: 140 us
  Pallas kernels  109 us (77%)
  local copies, waits for them, and re-layouts  21.6 us (15%)
  starting transfers between devices  8.59 us (6%)
    pallas_call x2, Pallas kernels, translate(): pl.pallas_call(functools.partial(translate_kernel, targets, sources), out...  51.6 us
    pallas_call x1, Pallas kernels, gather(): pl.pallas_call(gather_kernel, out_shape=(jax.ShapeDtypeStruct((4, 4, 2, 4...  35.7 us
    unnamed x34, local copies, waits for them, and re-layouts  21.6 us
    pallas_call x1, Pallas kernels, far_field(): pl.pallas_call(far_kernel, out_shape=(jax.ShapeDtypeStruct(coords.shape,...  17 us
    all_to_all x1, starting transfers between devices, shards(): lax.all_to_all(packed, 'dom', split_axis=0, concat_axis=0, tiled=True)  8.59 us
  transfers between devices with their start and end apart: 1, of which 0 were waited for; matrix products, arithmetic and copies ran while one was open for 11% of the time, Pallas kernels for 0%

profile of v3, /device:TPU:1, one launch (start us, length us, event | category | flops | bytes accessed | tf_op | source)
XLA Modules:
  0.0 139.8 jit_solution(7924023054905151611)
XLA Ops:
  0.6 1.0 copy.26
  1.6 0.0 copy-start
  1.6 0.8 copy-done
  2.4 0.0 copy-start.3
  2.4 0.8 copy-done.3
  3.2 0.0 copy-start.5
  3.2 0.8 copy-done.5
  4.0 0.0 copy-start.12
  4.0 0.7 copy-done.12
  4.7 2.6 %block_moments.1 = (f32[256,128]{1,0:T(8,128)}, s32[1,128]{1,0:T(1,128)S(1)}) custom-call(f32[3,128,128]{2,1,0:T(8,128)S(1)} %bitcast.27, f32[128,128]{1,0:T(8,128)S(1)} %bitcast.32, s32[1,128]{1,0:T(1,128)S(1)} %bitcast.50, s32[64,128]{1,0:T(8,128)S(1)} %bitcast.39, f32[128,1]{1,0:T(8,128)S(1)} %copy-done.5), custom_call_target="tpu_custom_call" | custom-call | tf_op jit(solution)/shard_map/block_moments/pallas_call | solution.py:168
  7.3 8.6 %all-to-all-start = ((f32[32,8,128]{2,1,0:T(8,128)}), f32[32,8,128]{2,1,0:T(8,128)S(1)}, u32[]{:S(2)}, u32[]{:S(2)}) async-start(f32[32,8,128]{2,1,0:T(8,128)} %bitcast.3), calls=%async_computation | async-start | bytes 262144 | tf_op jit(solution)/shard_map/all_to_all | solution.py:709
  15.9 1.0 copy.17
  16.9 0.0 copy-start.13
  16.9 0.0 copy-start.4
  16.9 0.0 copy-start.1
  17.0 0.0 copy-start.6
  17.0 0.0 copy-start.7
  17.0 0.0 copy-start.8
  17.0 0.0 copy-start.9
  17.0 0.0 copy-start.10
  17.0 0.0 copy-start.11
  17.0 14.9 %copy.18.ops_hbm = f32[316,81,81]{2,1,0:T(8,128)} copy(f32[316,81,81]{0,2,1:T(8,128)} %param.21) | data formatting | bytes 16586208 | tf_op args[6]
  31.9 0.0 copy-done.13
  31.9 0.1 copy.20
  32.1 0.0 all-to-all-done
  32.1 0.0 copy-done.4
  32.1 1.8 %leaf_moments.1 = (f32[64,128]{1,0:T(8,128)S(1)}, f32[256,128]{1,0:T(8,128)S(1)}, s32[64,128]{1,0:T(8,128)S(1)}) custom-call(f32[256,128]{1,0:T(8,128)S(1)} %bitcast.30, s32[64,128]{1,0:T(8,128)S(1)} %bitcast.40, f32[8,128,128]{2,1,0:T(8,128)S(1)} %pad.7.ops_ref), custom_call_target="tpu_custom_call" | custom-call | tf_op jit(solution)/shard_map/leaf_moments/pallas_call | solution.py:215
  33.9 0.0 copy-done.1
  33.9 0.0 copy-done.6
  33.9 0.0 copy-done.7
  33.9 0.0 copy-done.8
  33.9 0.0 copy-done.9
  33.9 0.0 copy-done.10
  33.9 0.0 copy-done.11
  34.0 35.7 %gather.1 = (f32[4,4,2,4,64,128]{5,4,3,2,1,0:T(8,128)S(1)}, f32[4,4,4,2,8,128]{5,4,3,2,1,0:T(8,128)S(1)}, f32[4,128,128]{2,1,0:T(8,128)S(1)}, s32[64,128]{1,0:T(...) custom-call(f32[64,128]{1,0:T(8,128)S(1)} %get-tuple-element.17.leaf_ref, ...), custom_call_target="tpu_custom_call" | custom-call | tf_op jit(solution)/shard_map/gather/pallas_call | solution.py:521
  69.7 17.2 %translate.3.parent_ref = f32[64,128]{1,0:T(8,128)S(1)} custom-call(s32[4096]{0:T(1024)S(1)} %bitcast.46, s32[1,128]{1,0:T(1,128)S(1)} %get-tuple-element.23.count, f32[1024,128]{1,0:T(8,128)S(1)} %bitcast.36, f32[316,81,81]{2,1,0:T(8,128)} %copy.18.ops_hbm), custom_call_target="tpu_custom_call" | custom-call | tf_op jit(solution)/shard_map/translate/pallas_call | solution.py:323
  86.9 0.0 copy-start.2
  86.9 34.4 %translate.2 = f32[256,128]{1,0:T(8,128)S(1)} custom-call(s32[8192]{0:T(1024)S(1)} %bitcast.42, s32[1,128]{1,0:T(1,128)S(1)} %get-tuple-element.20.count, f32[8192,128]{1,0:T(8,128)S(1)} %bitcast.26, f32[316,81,81]{2,1,0:T(8,128)} %copy.18.ops_hbm), custom_call_target="tpu_custom_call" | custom-call | tf_op jit(solution)/shard_map/translate/pallas_call | solution.py:323
  121.3 0.0 copy-done.2
  121.3 17.0 %far_field.1 = (f32[3,128,128]{2,1,0:T(8,128)S(1)}, f32[128,128]{1,0:T(8,128)S(1)}) custom-call(f32[4,64,128]{2,1,0:T(8,128)S(1)} %bitcast.35, f32[64,128]{1,0:T(8,128)S(1)} %translate.3.parent_ref, s32[64,128]{1,0:T(8,128)S(1)} %get-tuple-element.25.ids_ref, f32[256,128]{1,0:T(8,128)S(1)} %bitcast.31, f32[8,128,128]{2,1,0:T(8,128)S(1)} %pad.8.ops_ref, ...), custom_call_target="tpu_custom_call" | custom-call | tf_op jit(solution)/shard_map/far_field/pallas_call | solution.py:657
  138.3 0.8 copy.25
  139.2 0.6 copy.28
  (2 shorter events, 0.1 us)
Async XLA Ops:
  1.6 0.8 copy-start
  2.4 0.8 copy-start.3
  3.2 0.8 copy-start.5
  4.0 0.7 copy-start.12
  7.3 24.8 %all-to-all-start = ((f32[32,8,128]{2,1,0:T(8,128)}), f32[32,8,128]{2,1,0:T(8,128)S(1)}, u32[]{:S(2)}, u32[]{:S(2)}) async-start(f32[32,8,128]{2,1,0:T(8,128)} %bitcast.3), calls=%async_computation | async-start | bytes 262144 | tf_op jit(solution)/shard_map/all_to_all | solution.py:709
  16.9 15.0 %copy-start.13 = (f32[8,81,81]{2,0,1:T(8,128)S(1)}, f32[8,81,81]{2,0,1:T(8,128)}, u32[]{:S(2)}) copy-start(f32[8,81,81]{2,0,1:T(8,128)} %param.20) | copy-start | bytes 629860
  16.9 15.1 %copy-start.4 = (s32[8192]{0:T(1024)S(1)}, s32[8192]{0:T(1024)}, u32[]{:S(2)}) copy-start(s32[8192]{0:T(1024)} %param.18) | copy-start | bytes 98308
  16.9 16.9 %copy-start.1 = (f32[16384]{0:T(1024)S(1)}, f32[16384]{0:T(1024)}, u32[]{:S(2)}) copy-start(f32[16384]{0:T(1024)} %param.16) | copy-start | bytes 196612
  17.0 16.9 %copy-start.6 = (s32[1,1,4096]{2,1,0:T(1,128)S(1)}, s32[1,1,4096]{2,1,0:T(1,128)}, u32[]{:S(2)}) copy-start(s32[1,1,4096]{2,1,0:T(1,128)} %param.22) | copy-start | bytes 49156
  17.0 16.9 %copy-start.7 = (s32[1,1,4096]{2,1,0:T(1,128)S(1)}, s32[1,1,4096]{2,1,0:T(1,128)}, u32[]{:S(2)}) copy-start(s32[1,1,4096]{2,1,0:T(1,128)} %param.23) | copy-start | bytes 49156
  17.0 16.9 %copy-start.8 = (s32[1,1,4096]{2,1,0:T(1,128)S(1)}, s32[1,1,4096]{2,1,0:T(1,128)}, u32[]{:S(2)}) copy-start(s32[1,1,4096]{2,1,0:T(1,128)} %param.24) | copy-start | bytes 49156
  17.0 16.9 %copy-start.9 = (s32[1,1,2048]{2,1,0:T(1,128)S(1)}, s32[1,1,2048]{2,1,0:T(1,128)}, u32[]{:S(2)}) copy-start(s32[1,1,2048]{2,1,0:T(1,128)} %param.25) | copy-start | bytes 24580
  17.0 16.9 %copy-start.10 = (s32[1,1,2048]{2,1,0:T(1,128)S(1)}, s32[1,1,2048]{2,1,0:T(1,128)}, u32[]{:S(2)}) copy-start(s32[1,1,2048]{2,1,0:T(1,128)} %param.26) | copy-start | bytes 24580
  17.0 16.9 %copy-start.11 = (s32[1,1,2048]{2,1,0:T(1,128)S(1)}, s32[1,1,2048]{2,1,0:T(1,128)}, u32[]{:S(2)}) copy-start(s32[1,1,2048]{2,1,0:T(1,128)} %param.27) | copy-start | bytes 24580
  86.9 34.4 %copy-start.2 = (f32[288,128]{1,0:T(8,128)S(1)}, f32[288,128]{1,0:T(8,128)}, u32[]{:S(2)}) copy-start(f32[288,128]{1,0:T(8,128)} %constant.8.clone.matrix_ref) | copy-start | bytes 442372

commit v4 on v3

--- a/solution.py
+++ b/solution.py
@@ -11,6 +11,8 @@
 from jax.sharding import PartitionSpec as P
 
 COEF = 81
+OFFSETS = 316
+ROWS = 88
 TOP = 8
 LANES = 128
 LEAF_DEV = 64
@@ -247,10 +249,11 @@
     return jnp.where(take_small, jnp.minimum(x, other), jnp.maximum(x, other))
 
 
-def write_keys(items, targets, none, keys_ref, count_ref):
+def write_keys(items, targets, sources, keys_ref, count_ref):
     target_ref, source_ref, offset_ref = items
     rows = target_ref.shape[0]
-    keys_ref[...] = jnp.full(keys_ref.shape, ((targets - 1) << 23) | (none << 9), jnp.int32)
+    none = ((sources - 1) << 9) | OFFSETS
+    keys_ref[...] = jnp.full(keys_ref.shape, ((targets - 1) << 23) | none, jnp.int32)
     keys_ref[0:rows, :] = (target_ref[...] << 23) | (source_ref[...] << 9) | offset_ref[...]
     numbers = iota((targets, LANES), 0)
     count = jnp.zeros((targets, LANES), jnp.float32)
@@ -269,71 +272,66 @@
         for turn in range(3):
             goal = jnp.where(turn < filled * 4 - line, own, targets - 1)
             at = rows + 3 * p + turn
-            keys_ref[at : at + 1, :] = (goal << 23) | (none << 9)
+            keys_ref[at : at + 1, :] = (goal << 23) | none
     count_ref[...] = jnp.broadcast_to(fours, count_ref.shape)
 
 
-def translate_kernel(targets, sources, keys, count, src_hbm, ops_hbm, out_ref, ops, src, acc, sems):
-    load_ops = pltpu.make_async_copy(ops_hbm, ops, sems.at[0])
-    load_src = pltpu.make_async_copy(src_hbm, src.at[pl.ds(0, sources)], sems.at[1])
-    load_ops.start()
-    load_src.start()
-    src[pl.ds(sources, 8), :] = jnp.zeros((8, LANES), jnp.float32)
-
-    def clear(t, carry):
-        acc[t] = jnp.zeros(acc.shape[1:], jnp.float32)
-        return carry
-
-    lax.fori_loop(0, targets, clear, 0)
-    load_ops.wait()
-    load_src.wait()
-
-    def term(at):
-        key = keys[at]
-        row = src[pl.ds((key >> 9) & 16383, 1), :][:, :COEF]
-        return ops[key & 511] * row
-
-    def step(i, carry):
-        for u in range(2):
-            at = i * 8 + u * 4
-            target = keys[at] >> 23
-            total = (term(at) + term(at + 1)) + (term(at + 2) + term(at + 3))
-            acc[target] += total
-        return carry
-
-    lax.fori_loop(0, (count[0, 0] + 1) // 2, step, 0)
-    diagonal = iota((COEF, LANES), 0) == iota((COEF, LANES), 1)
-
-    def finish(i, carry):
-        for u in range(4):
-            t = i * 4 + u
-            sums = jnp.sum(acc[t], axis=1, keepdims=True)
-            out_ref[pl.ds(t, 1), :] = jnp.sum(
-                jnp.where(diagonal, sums, 0.0), axis=0, keepdims=True
-            )
-        return carry
-
-    lax.fori_loop(0, targets // 4, finish, 0)
-
-
-def translate(keys, count, table, ops, targets):
-    sources = table.shape[0]
+def translate_kernel(leaf_keys, leaf_count, coarse_keys, coarse_count, leaf_src, coarse_src, ops, leaf_out, coarse_out, acc):
+    def work(keys, count, src, out):
+        targets = out.shape[0]
+
+        def clear(t, carry):
+            for u in range(4):
+                acc[t * 4 + u] = jnp.zeros(acc.shape[1:], jnp.float32)
+            return carry
+
+        lax.fori_loop(0, targets // 4, clear, 0)
+
+        def term(key):
+            row = src[pl.ds((key >> 9) & (src.shape[0] - 1), 1), :][:, :COEF]
+            return ops[key & 511, :COEF, :COEF] * row
+
+        def step(i, carry):
+            for u in range(4):
+                four = [keys[i * 16 + u * 4 + n] for n in range(4)]
+                total = (term(four[0]) + term(four[1])) + (term(four[2]) + term(four[3]))
+                acc[four[0] >> 23, :COEF, :COEF] += total
+            return carry
+
+        lax.fori_loop(0, (count[0, 0] + 3) // 4, step, 0)
+        lane = iota((ROWS, LANES), 1)
+        for low in range(0, targets, LANES):
+            size = min(LANES, targets - low)
+
+            def finish(i, columns):
+                for u in range(8):
+                    t = i * 8 + u
+                    columns = jnp.where(lane == t, jnp.sum(acc[low + t], axis=1, keepdims=True), columns)
+                return columns
+
+            columns = lax.fori_loop(0, size // 8, finish, jnp.zeros((ROWS, LANES), jnp.float32))
+            padded = jnp.concatenate([columns, jnp.zeros((LANES - ROWS, LANES), jnp.float32)], axis=0)
+            out[low : low + size, :] = padded.T[:size]
+
+    work(coarse_keys, coarse_count, coarse_src, coarse_out)
+    work(leaf_keys, leaf_count, leaf_src, leaf_out)
+
+
+def translate(leaf_keys, leaf_count, coarse_keys, coarse_count, leaf_table, coarse_table, ops):
     smem = pl.BlockSpec(memory_space=pltpu.SMEM)
-    far = pl.BlockSpec(memory_space=pl.ANY)
+    whole = pl.BlockSpec(memory_space=VMEM)
     return pl.pallas_call(
-        functools.partial(translate_kernel, targets, sources),
-        out_shape=jax.ShapeDtypeStruct((targets, LANES), jnp.float32),
-        in_specs=[smem, smem, far, far],
-        out_specs=pl.BlockSpec(memory_space=VMEM),
-        scratch_shapes=[
-            VMEM(ops.shape, jnp.float32),
-            VMEM((sources + 8, LANES), jnp.float32),
-            VMEM((targets, COEF, COEF), jnp.float32),
-            pltpu.SemaphoreType.DMA((2,)),
-        ],
-        compiler_params=pltpu.CompilerParams(vmem_limit_bytes=48 * MIB),
+        translate_kernel,
+        out_shape=(
+            jax.ShapeDtypeStruct((4 * LEAF_DEV, LANES), jnp.float32),
+            jax.ShapeDtypeStruct((LEAF_DEV, LANES), jnp.float32),
+        ),
+        in_specs=[smem] * 4 + [whole] * 3,
+        out_specs=(whole, whole),
+        scratch_shapes=[VMEM((4 * LEAF_DEV, ROWS, LANES), jnp.float32)],
+        compiler_params=pltpu.CompilerParams(vmem_limit_bytes=36 * MIB),
         name="translate",
-    )(keys.reshape(-1), count, table, ops)
+    )(leaf_keys.reshape(-1), leaf_count, coarse_keys.reshape(-1), coarse_count, leaf_table, coarse_table, ops)
 
 
 def near_groups(pos_ref, q_ref, out_ref, low, high):
@@ -368,11 +366,12 @@
 
 PARTS = ((0, 16, 24, (2, 0, 1)), (24, 32, 48, (0, 1, 2)), (48, 56, 64, (1, 2, 0)))
 COPIES = 81
+SLABS = 9
 
 
 def gather_kernel(
-    leaf_ref, part_ref, pos_ref, q_ref, lt_ref, ls_ref, lo_ref, ct_ref, cs_ref, co_ref,
-    all_ref, parent_ref, near_ref, lkeys_ref, lcount_ref, ckeys_ref, ccount_ref, got_c, got_x, got_y, sum_c, sum_x, send_sem, recv_sem
+    leaf_ref, part_ref, pos_ref, q_ref, lt_ref, ls_ref, lo_ref, ct_ref, cs_ref, co_ref, m2l_hbm,
+    all_ref, parent_ref, near_ref, lkeys_ref, lcount_ref, ckeys_ref, ccount_ref, m2l_ref, got_c, got_x, got_y, sum_c, sum_x, slabs, send_sem, recv_sem, slab_sem
 ):
     dom = lax.axis_index("dom")
     here = (dom // 8, (dom // 2) % 4, lax.axis_index("lvl"))
@@ -383,6 +382,9 @@
 
     def moved(axis, by):
         return tuple((v + by) % 4 if n == axis else v for n, v in enumerate(here))
+
+    def slab(g, slot):
+        return pltpu.make_async_copy(m2l_hbm.at[pl.ds(g * SLABS, SLABS)], slabs.at[slot], slab_sem.at[slot])
 
     twin = device(here, 1 - core)
     barrier = pltpu.get_barrier_semaphore()
@@ -391,6 +393,8 @@
             pl.semaphore_signal(barrier, inc=1, device_id=device(moved(axis, by), core), device_id_type=MESH)
     pl.semaphore_signal(barrier, inc=1, device_id=twin, device_id_type=MESH)
     all_ref[here[0], here[1], core, here[2]] = leaf_ref[...]
+    m2l_ref[OFFSETS * ROWS :, :] = jnp.zeros((ROWS, LANES), jnp.float32)
+    slab(0, 0).start()
     pl.semaphore_wait(barrier, 10)
 
     started = []
@@ -468,14 +472,36 @@
         for keys, value in now.values():
             keys[...] = value
 
+    def turn(low, high):
+        def group(g, carry):
+            slot = g % 2
+
+            @pl.when(g < COEF // SLABS - 1)
+            def _():
+                slab(g + 1, 1 - slot).start()
+
+            slab(g, slot).wait()
+            for u in range(SLABS):
+                for p in range(3):
+                    wide = min(LANES, OFFSETS - p * LANES)
+                    lines = slabs[slot, u, :, p * LANES : p * LANES + wide].T
+                    start = p * LANES * ROWS + g * SLABS + u
+                    even = wide // 8 * 8
+                    m2l_ref[pl.ds(start, even, stride=ROWS), 0:COEF] = lines[:even]
+                    if even < wide:
+                        m2l_ref[pl.ds(start + even * ROWS, wide - even, stride=ROWS), 0:COEF] = lines[even:]
+            return carry
+
+        lax.fori_loop(low, high, group, 0)
+
     def fill(n):
         if n == 0:
             write_keys((lt_ref, ls_ref, lo_ref), 4 * LEAF_DEV, 8192, lkeys_ref, lcount_ref)
             write_keys((ct_ref, cs_ref, co_ref), LEAF_DEV, 1024, ckeys_ref, ccount_ref)
         elif n < 4:
             sort(60 * (n - 1), 60 * n)
-        else:
-            near_groups(pos_ref, q_ref, near_ref, *((0, 7), (7, 14), (14, 16))[n - 4])
+        turn(*((0, 1), (1, 1), (1, 1), (1, 2), (2, 6), (6, 9), (9, 9))[n])
+        near_groups(pos_ref, q_ref, near_ref, *((0, 0), (0, 0), (0, 0), (0, 0), (0, 0), (0, 2), (2, 16))[n])
 
     last = [put(block((), 0, 0, 0, 64), twin)]
     for phase in range(3):
@@ -515,7 +541,7 @@
     assert len(started) == COPIES
 
 
-def gather(leaf, parts, coords, charge, leaf_items, coarse_items):
+def gather(leaf, parts, coords, charge, leaf_items, coarse_items, ops):
     whole = pl.BlockSpec(memory_space=VMEM)
     f32 = jnp.float32
     return pl.pallas_call(
@@ -528,23 +554,26 @@
             jax.ShapeDtypeStruct((1, LANES), jnp.int32),
             jax.ShapeDtypeStruct((32, LANES), jnp.int32),
             jax.ShapeDtypeStruct((1, LANES), jnp.int32),
+            jax.ShapeDtypeStruct(((OFFSETS + 1) * ROWS, LANES), f32),
         ),
-        in_specs=[whole] * 10,
-        out_specs=(whole,) * 7,
+        in_specs=[whole] * 10 + [pl.BlockSpec(memory_space=pl.ANY)],
+        out_specs=(whole,) * 8,
         scratch_shapes=[
             VMEM((4, 4, 8, LANES), f32),
             VMEM((3, 4, 8, LANES), f32),
             VMEM((3, 8, LANES), f32),
             VMEM((4, 4, 8, LANES), f32),
             VMEM((4, 8, LANES), f32),
+            VMEM((2, SLABS, COEF, OFFSETS), f32),
             pltpu.SemaphoreType.DMA((COPIES,)),
             pltpu.SemaphoreType.DMA((COPIES,)),
+            pltpu.SemaphoreType.DMA((2,)),
         ],
-        compiler_params=pltpu.CompilerParams(collective_id=0, has_side_effects=True, vmem_limit_bytes=24 * MIB),
+        compiler_params=pltpu.CompilerParams(collective_id=0, has_side_effects=True, vmem_limit_bytes=42 * MIB),
         name="gather",
     )(
         leaf, parts.reshape(4, 4, 2, 8, LANES), coords, charge,
-        *(a.reshape(-1, LANES) for a in leaf_items + coarse_items),
+        *(a.reshape(-1, LANES) for a in leaf_items + coarse_items), ops.transpose(1, 2, 0),
     )
 
 
@@ -708,18 +737,26 @@
     packed, place = block_moments(coords, charge, block_leaf.reshape(1, blocks), table)
     arrived = lax.all_to_all(packed, "dom", split_axis=0, concat_axis=0, tiled=True)
     leaf_moments, parents_part, ids = leaves(arrived, table, padded(m2m_ops))
-    source_table, parent_table, near, leaf_keys, leaf_count, coarse_keys, coarse_count = gather(
+    source_table, parent_table, near, leaf_keys, leaf_count, coarse_keys, coarse_count, turned_ops = gather(
         leaf_moments,
         parents_part,
         coords,
         charge,
         (item_target, item_source, item_offset),
         (coarse_target, coarse_source, coarse_offset),
+        m2l_ops,
     )
     source_table = source_table.reshape(leaves_all, LANES)
     parent_table = parent_table.reshape(parents_all, LANES)
-    parent_locals = translate(coarse_keys, coarse_count, parent_table, m2l_ops, LEAF_DEV)
-    terms = translate(leaf_keys, leaf_count, source_table, m2l_ops, 4 * LEAF_DEV)
+    terms, parent_locals = translate(
+        leaf_keys,
+        leaf_count,
+        coarse_keys,
+        coarse_count,
+        source_table,
+        parent_table,
+        turned_ops.reshape(OFFSETS + 1, ROWS, LANES),
+    )
     forces, potential = far_field(
         terms, parent_locals, ids, arrived, padded(l2l_ops), coords, charge, place, near
     )

time: 141 us -> 137 us (0.972)
  local copies, waits for them, and re-layouts: 21.6 us -> 13.5 us
  waiting for transfers between devices: 0.01 us -> 5.44 us
  Pallas kernels: 109 us -> 107 us
    pallas_call x2 -> x1, Pallas kernels: 51.6 us -> 38.8 us  [translate(): pl.pallas_call(translate_kernel, out_shape=(jax.ShapeDtypeStruct((4 * LEA...]
    unnamed x34 -> x31, local copies, waits for them, and re-layouts: 21.6 us -> 13.4 us
    pallas_call x1, Pallas kernels: 35.7 us -> 42.9 us  [gather(): pl.pallas_call(gather_kernel, out_shape=(jax.ShapeDtypeStruct((4, 4, 2, 4...]
    all_to_all x1, waiting for transfers between devices: 0.01 us -> 5.44 us  [shards(): lax.all_to_all(packed, 'dom', split_axis=0, concat_axis=0, tiled=True)]
    pallas_call x1, Pallas kernels: 17 us -> 21.2 us  [far_field(): pl.pallas_call(far_kernel, out_shape=(jax.ShapeDtypeStruct(coords.shape,...]
  transfers between devices with their start and end apart: 1 -> 1, of which waited for: 0 -> 1; matrix products, arithmetic and copies ran while one was open for 11% -> 2% of each run, Pallas kernels for 0% -> 0%
where the time goes in v4:
time: 137 us; the launch traced here: 136 us
  Pallas kernels  107 us (78%)
  local copies, waits for them, and re-layouts  13.5 us (10%)
  starting transfers between devices  8.59 us (6%)
  waiting for transfers between devices  5.44 us (4%)
    pallas_call x1, Pallas kernels, gather(): pl.pallas_call(gather_kernel, out_shape=(jax.ShapeDtypeStruct((4, 4, 2, 4...  42.9 us
    pallas_call x1, Pallas kernels, translate(): pl.pallas_call(translate_kernel, out_shape=(jax.ShapeDtypeStruct((4 * LEA...  38.8 us
    pallas_call x1, Pallas kernels, far_field(): pl.pallas_call(far_kernel, out_shape=(jax.ShapeDtypeStruct(coords.shape,...  21.2 us
    unnamed x31, local copies, waits for them, and re-layouts  13.4 us
    all_to_all x1, starting transfers between devices, shards(): lax.all_to_all(packed, 'dom', split_axis=0, concat_axis=0, tiled=True)  8.59 us
    all_to_all x1, waiting for transfers between devices, shards(): lax.all_to_all(packed, 'dom', split_axis=0, concat_axis=0, tiled=True)  5.44 us
  transfers between devices with their start and end apart: 1, of which 1 were waited for; matrix products, arithmetic and copies ran while one was open for 2% of the time, Pallas kernels for 0%

profile of v4, /device:TPU:1, one launch (start us, length us, event | category | flops | bytes accessed | tf_op | source)
XLA Modules:
  0.0 135.6 jit_solution(12361927665444022524)
XLA Ops:
  0.6 1.0 copy.24
  1.6 0.0 copy-start
  1.6 0.8 copy-done
  2.4 0.0 copy-start.3
  2.4 0.8 copy-done.3
  3.2 0.0 copy-start.5
  3.2 0.8 copy-done.5
  4.0 0.0 copy-start.12
  4.0 0.7 copy-done.12
  4.7 2.6 %block_moments.1 = (f32[256,128]{1,0:T(8,128)}, s32[1,128]{1,0:T(1,128)S(1)}) custom-call(f32[3,128,128]{2,1,0:T(8,128)S(1)} %bitcast.29, f32[128,128]{1,0:T(8,128)S(1)} %bitcast.34, s32[1,128]{1,0:T(1,128)S(1)} %bitcast.52, s32[64,128]{1,0:T(8,128)S(1)} %bitcast.41, f32[128,1]{1,0:T(8,128)S(1)} %copy-done.5), custom_call_target="tpu_custom_call" | custom-call | tf_op jit(solution)/shard_map/block_moments/pallas_call | solution.py:170
  7.3 8.6 %all-to-all-start = ((f32[32,8,128]{2,1,0:T(8,128)}), f32[32,8,128]{2,1,0:T(8,128)S(1)}, u32[]{:S(2)}, u32[]{:S(2)}) async-start(f32[32,8,128]{2,1,0:T(8,128)} %bitcast.3), calls=%async_computation | async-start | bytes 262144 | tf_op jit(solution)/shard_map/all_to_all | solution.py:738
  15.9 1.0 copy.17
  16.9 1.0 copy.18
  18.0 5.4 %all-to-all-done = f32[32,8,128]{2,1,0:T(8,128)S(1)} async-done(((f32[32,8,128]{2,1,0:T(8,128)}), f32[32,8,128]{2,1,0:T(8,128)S(1)}, u32[]{:S(2)}, u32[]{:S(2)}) %all-to-all-start) | async-done | bytes 131104 | tf_op jit(solution)/shard_map/all_to_all | solution.py:738
  23.5 0.0 copy-start.4
  23.5 0.8 copy-done.4
  24.2 1.8 %leaf_moments.1 = (f32[64,128]{1,0:T(8,128)S(1)}, f32[256,128]{1,0:T(8,128)S(1)}, s32[64,128]{1,0:T(8,128)S(1)}) custom-call(f32[256,128]{1,0:T(8,128)S(1)} %bitcast.32, s32[64,128]{1,0:T(8,128)S(1)} %bitcast.42, f32[8,128,128]{2,1,0:T(8,128)S(1)} %pad.7.ops_ref), custom_call_target="tpu_custom_call" | custom-call | tf_op jit(solution)/shard_map/leaf_moments/pallas_call | solution.py:217
  26.0 0.0 copy-start.1
  26.1 0.8 copy-done.1
  26.9 0.0 copy-start.6
  26.9 0.7 copy-done.6
  27.6 0.0 copy-start.7
  27.6 0.7 copy-done.7
  28.3 0.0 copy-start.8
  28.3 0.7 copy-done.8
  29.0 0.0 copy-start.9
  29.0 0.7 copy-done.9
  29.7 0.0 copy-start.10
  29.7 0.7 copy-done.10
  30.4 0.0 copy-start.11
  30.4 0.7 copy-done.11
  31.1 42.9 %gather.1 = (f32[4,4,2,4,64,128]{5,4,3,2,1,0:T(8,128)S(1)}, f32[4,4,4,2,8,128]{5,4,3,2,1,0:T(8,128)S(1)}, f32[4,128,128]{2,1,0:T(8,128)S(1)}, s32[64,128]{1,0:T(...) custom-call(f32[64,128]{1,0:T(8,128)S(1)} %get-tuple-element.20.leaf_ref, ...), custom_call_target="tpu_custom_call" | custom-call | tf_op jit(solution)/shard_map/gather/pallas_call | solution.py:547
  74.1 0.0 copy-start.2
  74.1 38.8 %translate.1 = (f32[256,128]{1,0:T(8,128)S(1)}, f32[64,128]{1,0:T(8,128)S(1)}) custom-call(s32[8192]{0:T(1024)S(1)} %bitcast.44, s32[1,128]{1,0:T(1,128)S(1)} %get-tuple-element.23.leaf_count, s32[4096]{0:T(1024)S(1)} %bitcast.48, s32[1,128]{1,0:T(1,128)S(1)} %get-tuple-element.25.coarse_count, f32[8192,128]{1,0:T(8,128)S(1)} %bitcast.28, ...), custom_call_target="tpu_custom_call" | custom-call | tf_op jit(solution)/shard_map/translate/pallas_call | solution.py:323
  112.9 0.0 copy-done.2
  112.9 21.2 %far_field.1 = (f32[3,128,128]{2,1,0:T(8,128)S(1)}, f32[128,128]{1,0:T(8,128)S(1)}) custom-call(f32[4,64,128]{2,1,0:T(8,128)S(1)} %bitcast.40, f32[64,128]{1,0:T(8,128)S(1)} %get-tuple-element.30.parent_ref, s32[64,128]{1,0:T(8,128)S(1)} %get-tuple-element.31.ids_ref, f32[256,128]{1,0:T(8,128)S(1)} %bitcast.33, f32[8,128,128]{2,1,0:T(8,128)S(1)} %pad.8.ops_ref, ...), custom_call_target="tpu_custom_call" | custom-call | tf_op jit(solution)/shard_map/far_field/pallas_call | solution.py:686
  134.1 0.8 copy.23
  135.0 0.6 copy.26
  (2 shorter events, 0.1 us)
Async XLA Ops:
  1.6 0.8 copy-start
  2.4 0.8 copy-start.3
  3.2 0.8 copy-start.5
  4.0 0.7 copy-start.12
  7.3 16.2 %all-to-all-start = ((f32[32,8,128]{2,1,0:T(8,128)}), f32[32,8,128]{2,1,0:T(8,128)S(1)}, u32[]{:S(2)}, u32[]{:S(2)}) async-start(f32[32,8,128]{2,1,0:T(8,128)} %bitcast.3), calls=%async_computation | async-start | bytes 262144 | tf_op jit(solution)/shard_map/all_to_all | solution.py:738
  23.5 0.8 copy-start.4
  26.0 0.8 copy-start.1
  26.9 0.7 copy-start.6
  27.6 0.7 copy-start.7
  28.3 0.7 copy-start.8
  29.0 0.7 copy-start.9
  29.7 0.7 copy-start.10
  30.4 0.7 copy-start.11
  74.1 38.8 %copy-start.2 = (f32[288,128]{1,0:T(8,128)S(1)}, f32[288,128]{1,0:T(8,128)}, u32[]{:S(2)}) copy-start(f32[288,128]{1,0:T(8,128)} %constant.8.clone.matrix_ref) | copy-start | bytes 442372

commit v5 on v4

--- a/solution.py
+++ b/solution.py
@@ -69,15 +69,6 @@
                 emit(row_index(degree, azimuth, which == 1), degree, upper)
 
 
-def weight_column():
-    out = np.zeros((LANES, 1), np.float32)
-    for degree in range(TOP + 1):
-        for azimuth in range(degree + 1):
-            for imaginary in range(2 if azimuth else 1):
-                out[row_index(degree, azimuth, imaginary), 0] = row_weight(degree, azimuth)
-    return out
-
-
 G_ROWS = 96 + 3 * 64
 
 
@@ -121,11 +112,13 @@
     return lax.broadcasted_iota(jnp.int32, shape, dim)
 
 
-def moments_kernel(pos_ref, q_ref, leaf_ref, table_ref, weight_ref, packed_ref, place_ref, turned, acc, rows):
-    blocks = leaf_ref.shape[1]
-    leaf = leaf_ref[...]
+WEIGHTS = [row_weight(l, (row - l * l + 1) // 2) for l in range(TOP + 1) for row in range(l * l, (l + 1) * (l + 1))]
+
+
+def block_moments(atoms_ref, table, leaf, place_ref, packed_ref, turned, acc, rows):
+    blocks = leaf.shape[1]
     high = (iota((64, blocks), 0) == (leaf >> 7)).astype(jnp.float32)
-    lines = dot(table_ref[...].astype(jnp.float32), high, ((0,), (0,)))
+    lines = dot(table.astype(jnp.float32), high, ((0,), (0,)))
     slot = jnp.sum(
         jnp.where(iota((LANES, blocks), 0) == (leaf & 127), lines, 0.0), axis=0, keepdims=True
     ).astype(jnp.int32)
@@ -137,9 +130,8 @@
     place = owner * CAP + rank
     place_ref[...] = place
 
-    for d in range(3):
-        turned[d] = pos_ref[d].T
-    turned[3] = q_ref[...].T
+    for d in range(4):
+        turned[d] = atoms_ref[d].T
     acc[...] = jnp.zeros_like(acc)
 
     def chunk(i, carry):
@@ -156,44 +148,25 @@
     lax.fori_loop(0, 4, chunk, 0)
     rows[...] = jnp.zeros_like(rows)
     for k in range(COEF):
-        rows[k : k + 1, :] = jnp.sum(acc[k], axis=0, keepdims=True)
-    rows[...] = rows[...] * weight_ref[...]
+        rows[k : k + 1, :] = WEIGHTS[k] * jnp.sum(acc[k], axis=0, keepdims=True)
     rows[127:128, :] = ((slot & 63) + 1).astype(jnp.float32)
-    moments = rows[...].T
     spread = (iota((32 * CAP, blocks), 0) == place).astype(jnp.float32)
-    packed_ref[...] = dot(spread, moments)
-
-
-def block_moments(coords, charge, leaf, table):
-    blocks = coords.shape[1]
-    whole = pl.BlockSpec(memory_space=VMEM)
-    return pl.pallas_call(
-        moments_kernel,
-        out_shape=(
-            jax.ShapeDtypeStruct((32 * CAP, LANES), jnp.float32),
-            jax.ShapeDtypeStruct((1, blocks), jnp.int32),
-        ),
-        in_specs=[whole] * 5,
-        out_specs=(whole, whole),
-        scratch_shapes=[
-            VMEM((4, LANES, blocks), jnp.float32),
-            VMEM((COEF, 8, blocks), jnp.float32),
-            VMEM((LANES, blocks), jnp.float32),
-        ],
-        compiler_params=pltpu.CompilerParams(vmem_limit_bytes=16 * MIB),
-        name="block_moments",
-    )(coords, charge, leaf, table, jnp.asarray(weight_column()))
-
-
-def leaves_kernel(arrived_ref, table_ref, ops_ref, leaf_ref, parent_ref, ids_ref):
-    group = lax.axis_index("lvl")
-    first = (lax.axis_index("dom") * GROUP + group) * LEAF_DEV
-    arrived = arrived_ref[...]
+    packed_ref[...] = dot(spread, rows[...].T).reshape(packed_ref.shape)
+
+
+def by_octant(values, ops_ref, octant):
+    lines = ops_ref.shape[0] * 8
+    moved = dot(values[:, :COEF], ops_ref[...].reshape(lines, COEF), ((1,), (1,)))
+    moved = jnp.where(iota(moved.shape, 1) & 7 == octant, moved, 0.0)
+    fold = (iota((lines, LANES), 0) >> 3 == iota((lines, LANES), 1)).astype(jnp.float32)
+    return dot(moved, fold)
+
+
+def leaf_moments(arrived, table_ref, ops_ref, group, first, part_ref, ids_ref):
     tags = arrived[:, 127:128].astype(jnp.int32)
     member = (iota((arrived.shape[0], LEAF_DEV), 1) + 1 == tags).astype(jnp.float32)
     leaf = dot(member, arrived, ((0,), (0,)))
     leaf = jnp.where(iota(leaf.shape, 1) < COEF, leaf, 0.0)
-    leaf_ref[...] = leaf
     slots = first + iota((LEAF_DEV, LANES), 0)
     found = jnp.zeros((LEAF_DEV, LANES), jnp.int32)
     lane = iota((LEAF_DEV, LANES), 1)
@@ -203,29 +176,11 @@
         found = found + jnp.where(table[h : h + 1, :] == slots, number, 0)
     ids = jnp.sum(found.astype(jnp.float32), axis=1, keepdims=True).astype(jnp.int32)
     ids_ref[...] = jnp.broadcast_to(ids, (LEAF_DEV, LANES))
-    octant = ids & 7
-    children = jnp.zeros((LEAF_DEV, LANES), jnp.float32)
-    for o in range(8):
-        children = children + dot(jnp.where(octant == o, leaf, 0.0), ops_ref[o], ((1,), (1,)))
+    children = by_octant(leaf, ops_ref, ids & 7)
     within = (ids >> 3) - group * 256
     picks = (iota((LEAF_DEV, 256), 1) == within).astype(jnp.float32)
-    parent_ref[...] = dot(picks, children, ((0,), (0,)))
-
-
-def leaves(arrived, table, ops):
-    whole = pl.BlockSpec(memory_space=VMEM)
-    return pl.pallas_call(
-        leaves_kernel,
-        out_shape=(
-            jax.ShapeDtypeStruct((LEAF_DEV, LANES), jnp.float32),
-            jax.ShapeDtypeStruct((256, LANES), jnp.float32),
-            jax.ShapeDtypeStruct((LEAF_DEV, LANES), jnp.int32),
-        ),
-        in_specs=[whole] * 3,
-        out_specs=(whole,) * 3,
-        compiler_params=pltpu.CompilerParams(vmem_limit_bytes=16 * MIB),
-        name="leaf_moments",
-    )(arrived, table, ops)
+    part_ref[...] = dot(picks, children, ((0,), (0,))).reshape(part_ref.shape)
+    return leaf
 
 
 def bitonic_stages(size):
@@ -365,17 +320,21 @@
 
 
 PARTS = ((0, 16, 24, (2, 0, 1)), (24, 32, 48, (0, 1, 2)), (48, 56, 64, (1, 2, 0)))
-COPIES = 81
+COPIES = 68
 SLABS = 9
 
 
 def gather_kernel(
-    leaf_ref, part_ref, pos_ref, q_ref, lt_ref, ls_ref, lo_ref, ct_ref, cs_ref, co_ref, m2l_hbm,
-    all_ref, parent_ref, near_ref, lkeys_ref, lcount_ref, ckeys_ref, ccount_ref, m2l_ref, got_c, got_x, got_y, sum_c, sum_x, slabs, send_sem, recv_sem, slab_sem
+    atoms_ref, whole_ref, m2m_ref, m2l_hbm,
+    all_ref, parent_ref, near_ref, lkeys_ref, lcount_ref, ckeys_ref, ccount_ref, m2l_ref, arrived_ref, place_ref, ids_ref,
+    packed, turned, acc, rows, part_ref, got_c, got_x, got_y, sum_c, sum_x, slabs, send_sem, recv_sem, slab_sem, out_sem, in_sem
 ):
-    dom = lax.axis_index("dom")
-    here = (dom // 8, (dom // 2) % 4, lax.axis_index("lvl"))
+    dom, lvl = lax.axis_index("dom"), lax.axis_index("lvl")
+    here = (dom // 8, (dom // 2) % 4, lvl)
     core = dom % 2
+    table_ref = whole_ref.at[0:64]
+    leaf_items = [whole_ref.at[64 + 32 * n : 96 + 32 * n] for n in range(3)]
+    coarse_items = [whole_ref.at[160 + 16 * n : 176 + 16 * n] for n in range(3)]
 
     def device(place, which):
         return ((place[0] * 4 + place[1]) * 2 + which, place[2])
@@ -387,15 +346,19 @@
         return pltpu.make_async_copy(m2l_hbm.at[pl.ds(g * SLABS, SLABS)], slabs.at[slot], slab_sem.at[slot])
 
     twin = device(here, 1 - core)
-    barrier = pltpu.get_barrier_semaphore()
-    for axis in range(3):
-        for by in (1, 2, 3):
-            pl.semaphore_signal(barrier, inc=1, device_id=device(moved(axis, by), core), device_id_type=MESH)
-    pl.semaphore_signal(barrier, inc=1, device_id=twin, device_id_type=MESH)
-    all_ref[here[0], here[1], core, here[2]] = leaf_ref[...]
     m2l_ref[OFFSETS * ROWS :, :] = jnp.zeros((ROWS, LANES), jnp.float32)
     slab(0, 0).start()
-    pl.semaphore_wait(barrier, 10)
+    barrier = pltpu.get_barrier_semaphore()
+
+    def greet(d, carry):
+        pl.semaphore_signal(barrier, inc=1, device_id=((dom + d) % 32, lvl), device_id_type=MESH)
+        return carry
+
+    lax.fori_loop(1, 32, greet, 0)
+    for by in (1, 2, 3):
+        pl.semaphore_signal(barrier, inc=1, device_id=(dom, (lvl + by) % 4), device_id_type=MESH)
+    block_moments(atoms_ref, table_ref[...], whole_ref[208:209, :], place_ref, packed, turned, acc, rows)
+    pl.semaphore_wait(barrier, 34)
 
     started = []
 
@@ -495,70 +458,120 @@
         lax.fori_loop(low, high, group, 0)
 
     def fill(n):
-        if n == 0:
-            write_keys((lt_ref, ls_ref, lo_ref), 4 * LEAF_DEV, 8192, lkeys_ref, lcount_ref)
-            write_keys((ct_ref, cs_ref, co_ref), LEAF_DEV, 1024, ckeys_ref, ccount_ref)
-        elif n < 4:
-            sort(60 * (n - 1), 60 * n)
-        turn(*((0, 1), (1, 1), (1, 1), (1, 2), (2, 6), (6, 9), (9, 9))[n])
-        near_groups(pos_ref, q_ref, near_ref, *((0, 0), (0, 0), (0, 0), (0, 0), (0, 0), (0, 2), (2, 16))[n])
-
-    last = [put(block((), 0, 0, 0, 64), twin)]
-    for phase in range(3):
-        first = []
+        if n < 3:
+            sort(60 * n, 60 * n + 60)
+        turn(*((0, 0), (0, 0), (0, 0), (0, 4), (4, 7), (7, 9), (9, 9), (9, 9))[n])
+        near_groups(atoms_ref, atoms_ref.at[3], near_ref, *((0, 0), (0, 0), (0, 0), (0, 0), (0, 0), (0, 2), (2, 6), (6, 16))[n])
+
+    def message(d):
+        goal = (dom + d) % 32
+        return pltpu.make_async_remote_copy(
+            src_ref=packed.at[goal],
+            dst_ref=arrived_ref.at[dom],
+            send_sem=out_sem.at[d],
+            recv_sem=in_sem.at[d],
+            device_id=(goal, lvl),
+            device_id_type=MESH,
+        )
+
+    def each(act):
+        def one(d, carry):
+            act(message(d))
+            return carry
+
+        lax.fori_loop(1, 32, one, 0)
+
+    each(lambda copy: copy.start())
+    arrived_ref[dom] = packed[dom]
+    write_keys(leaf_items, 4 * LEAF_DEV, 8192, lkeys_ref, lcount_ref)
+    write_keys(coarse_items, LEAF_DEV, 1024, ckeys_ref, ccount_ref)
+    fill(0)
+    each(lambda copy: copy.wait_recv())
+    all_ref[here[0], here[1], core, here[2]] = leaf_moments(
+        arrived_ref[...].reshape(32 * CAP, LANES), table_ref, m2m_ref, lvl, (dom * GROUP + lvl) * LEAF_DEV, part_ref, ids_ref
+    )
+
+    last = []
+    for phase in range(2):
+        direct = []
         for low, middle, high, order in PARTS:
             axis, done = order[phase], order[:phase]
-            first.append(
-                [put(block(done, axis, 0, low, high), device(moved(axis, by), core)) for by in (1, 3)]
-            )
-        stage(2 * phase)
-        fill(2 * phase)
-        second = []
-        for (low, middle, high, order), (right, left) in zip(PARTS, first):
+            direct.append([put(block(done, axis, 0, low, high), device(moved(axis, by), core)) for by in (1, 3, 2)])
+        stage(phase)
+        fill(phase + 1)
+        for (low, middle, high, order), copies in zip(PARTS, direct):
             axis, done = order[phase], order[:phase]
-            right.wait_recv()
-            a = put(block(done, axis, 3, low, middle), device(moved(axis, 1), core))
-            left.wait_recv()
-            b = put(block(done, axis, 1, middle, high), device(moved(axis, 3), core))
-            second.append((a, b))
-            last.append(put(block(done, axis, 3, low, high), twin))
-            last.append(put(block(done, axis, 1, low, high), twin))
-        stage(2 * phase + 1)
-        fill(2 * phase + 1)
-        for (low, middle, high, order), pair in zip(PARTS, second):
-            axis, done = order[phase], order[:phase]
-            for copy in pair:
+            for by, copy in zip((3, 1, 2), copies):
                 copy.wait_recv()
-            last.append(put(block(done, axis, 2, low, high), twin))
+                if phase:
+                    last.append(put(block(done, axis, by, low, high), twin))
+            if not phase:
+                last.append(put(block((axis,), axis, 0, low, high), twin))
+    first, second = [], []
+    for low, middle, high, order in PARTS:
+        axis, done = order[2], order[:2]
+        first.append([put(block(done, axis, 0, low, high), device(moved(axis, by), core)) for by in (1, 3)])
+    stage(2)
+    fill(3)
+    for (low, middle, high, order), (right, left) in zip(PARTS, first):
+        axis, done = order[2], order[:2]
+        right.wait_recv()
+        a = put(block(done, axis, 3, low, middle), device(moved(axis, 1), core))
+        left.wait_recv()
+        b = put(block(done, axis, 1, middle, high), device(moved(axis, 3), core))
+        second.append((a, b))
+        last.append(put(block(done, axis, 3, low, high), twin))
+        last.append(put(block(done, axis, 1, low, high), twin))
+    stage(3)
+    fill(4)
+    for (low, middle, high, order), pair in zip(PARTS, second):
+        axis, done = order[2], order[:2]
+        for copy in pair:
+            copy.wait_recv()
+        last.append(put(block(done, axis, 2, low, high), twin))
+    stage(4)
+    fill(5)
+    stage(5)
+    fill(6)
     stage(6)
-    fill(6)
+    fill(7)
     for copy in last:
         copy.wait_recv()
     for copy in waiting["p"]:
         copy.wait_recv()
     for copy in started:
         copy.wait_send()
+    each(lambda copy: copy.wait_send())
     assert len(started) == COPIES
 
 
-def gather(leaf, parts, coords, charge, leaf_items, coarse_items, ops):
+def gather(atoms, integers, m2m_ops, m2l_ops):
     whole = pl.BlockSpec(memory_space=VMEM)
-    f32 = jnp.float32
+    f32, i32 = jnp.float32, jnp.int32
+    blocks = atoms.shape[1]
     return pl.pallas_call(
         gather_kernel,
         out_shape=(
             jax.ShapeDtypeStruct((4, 4, 2, 4, LEAF_DEV, LANES), f32),
             jax.ShapeDtypeStruct((4, 4, 4, 2, 8, LANES), f32),
-            jax.ShapeDtypeStruct((4,) + charge.shape, f32),
-            jax.ShapeDtypeStruct((64, LANES), jnp.int32),
-            jax.ShapeDtypeStruct((1, LANES), jnp.int32),
-            jax.ShapeDtypeStruct((32, LANES), jnp.int32),
-            jax.ShapeDtypeStruct((1, LANES), jnp.int32),
+            jax.ShapeDtypeStruct(atoms.shape, f32),
+            jax.ShapeDtypeStruct((64, LANES), i32),
+            jax.ShapeDtypeStruct((1, LANES), i32),
+            jax.ShapeDtypeStruct((32, LANES), i32),
+            jax.ShapeDtypeStruct((1, LANES), i32),
             jax.ShapeDtypeStruct(((OFFSETS + 1) * ROWS, LANES), f32),
+            jax.ShapeDtypeStruct((32, CAP, LANES), f32),
+            jax.ShapeDtypeStruct((1, blocks), i32),
+            jax.ShapeDtypeStruct((LEAF_DEV, LANES), i32),
         ),
-        in_specs=[whole] * 10 + [pl.BlockSpec(memory_space=pl.ANY)],
-        out_specs=(whole,) * 8,
+        in_specs=[whole] * 3 + [pl.BlockSpec(memory_space=pl.ANY)],
+        out_specs=(whole,) * 11,
         scratch_shapes=[
+            VMEM((32, CAP, LANES), f32),
+            VMEM((4, LANES, blocks), f32),
+            VMEM((COEF, 8, blocks), f32),
+            VMEM((LANES, blocks), f32),
+            VMEM((4, 4, 2, 8, LANES), f32),
             VMEM((4, 4, 8, LANES), f32),
             VMEM((3, 4, 8, LANES), f32),
             VMEM((3, 8, LANES), f32),
@@ -568,21 +581,20 @@
             pltpu.SemaphoreType.DMA((COPIES,)),
             pltpu.SemaphoreType.DMA((COPIES,)),
             pltpu.SemaphoreType.DMA((2,)),
+            pltpu.SemaphoreType.DMA((32,)),
+            pltpu.SemaphoreType.DMA((32,)),
         ],
         compiler_params=pltpu.CompilerParams(collective_id=0, has_side_effects=True, vmem_limit_bytes=42 * MIB),
         name="gather",
-    )(
-        leaf, parts.reshape(4, 4, 2, 8, LANES), coords, charge,
-        *(a.reshape(-1, LANES) for a in leaf_items + coarse_items), ops.transpose(1, 2, 0),
-    )
+    )(atoms, integers, m2m_ops.transpose(1, 0, 2), m2l_ops.transpose(1, 2, 0))
 
 
 def far_kernel(
-    terms_ref, parent_ref, ids_ref, arrived_ref, ops_ref, pos_ref, q_ref, place_ref, near_ref, matrix_ref,
-    force_ref, phi_ref, got, sent, returned, turned, lines, send_sem, recv_sem
+    terms_ref, parent_ref, ids_ref, arrived_ref, ops_ref, atoms_ref, place_ref, near_ref, matrix_ref,
+    force_ref, phi_ref, basis, got, sent, returned, turned, lines, send_sem, recv_sem
 ):
     dom, lvl = lax.axis_index("dom"), lax.axis_index("lvl")
-    blocks = q_ref.shape[0]
+    blocks = atoms_ref.shape[1]
     barrier = pltpu.get_barrier_semaphore()
 
     def greet(d, carry):
@@ -592,6 +604,9 @@
     for by in (1, 2, 3):
         pl.semaphore_signal(barrier, inc=1, device_id=(dom, (lvl + by) % 4), device_id_type=MESH)
     lax.fori_loop(1, 32, greet, 0)
+    for d in range(3):
+        turned[d] = atoms_ref[d].T
+    shifted = by_octant(parent_ref[...], ops_ref, ids_ref[...][:, 0:1] & 7)
     pl.semaphore_wait(barrier, 34)
 
     shared = []
@@ -608,13 +623,20 @@
         copy.start()
         shared.append(copy)
 
-    octant = ids_ref[...] & 7
-    parent = parent_ref[...]
-    total = terms_ref[lvl]
-    for o in range(8):
-        total = total + dot(jnp.where(octant == o, parent, 0.0), ops_ref[o], ((1,), (1,)))
-    tags = arrived_ref[:, 127:128].astype(jnp.int32)
-    member = (iota((arrived_ref.shape[0], LEAF_DEV), 1) + 1 == tags).astype(jnp.float32)
+    total = shifted + terms_ref[lvl]
+
+    def prepare(i, carry):
+        at = pl.ds(pl.multiple_of(i * 32, 32), 32)
+
+        def emit(row, degree, value):
+            basis[row, at, :] = value
+
+        harmonics(turned[0, at, :], turned[1, at, :], turned[2, at, :], emit)
+        return carry
+
+    lax.fori_loop(0, 2, prepare, 0)
+    tags = arrived_ref[...].reshape(32 * CAP, LANES)[:, 127:128].astype(jnp.int32)
+    member = (iota((32 * CAP, LEAF_DEV), 1) + 1 == tags).astype(jnp.float32)
     for copy in shared:
         copy.wait_recv()
     total = (total + got[0]) + (got[1] + got[2])
@@ -637,8 +659,7 @@
 
     lax.fori_loop(1, 32, start, 0)
     returned[dom] = sent[dom]
-    for d in range(3):
-        turned[d] = pos_ref[d].T
+    lax.fori_loop(2, 4, prepare, 0)
     spread = (iota((32 * CAP, blocks), 0) == place_ref[...]).astype(jnp.float32)
 
     def receive(d, carry):
@@ -651,22 +672,19 @@
 
     def chunk(i, carry):
         at = pl.ds(pl.multiple_of(i * 32, 32), 32)
-        x, y, z = (turned[d, at, :] for d in range(3))
         sums = [None] * 4
-
-        def emit(row, degree, value):
-            starts = [(3, 0)] + ([(d, 96 + 64 * d) for d in range(3)] if degree < TOP else [])
+        for row in range(COEF):
+            value = basis[row, at, :]
+            starts = [(3, 0)] + ([(d, 96 + 64 * d) for d in range(3)] if row < TOP * TOP else [])
             for n, start in starts:
                 term = lines[start + row : start + row + 1, :] * value
                 sums[n] = term if sums[n] is None else sums[n] + term
-
-        harmonics(x, y, z, emit)
         for n in range(4):
             turned[n, at, :] = sums[n]
         return carry
 
     lax.fori_loop(0, 4, chunk, 0)
-    charge = q_ref[...]
+    charge = atoms_ref[3]
     for d in range(3):
         force_ref[d] = near_ref[d] - charge * turned[d].T
     phi_ref[...] = near_ref[3] + turned[3].T
@@ -680,36 +698,33 @@
         copy.wait_send()
 
 
-def far_field(terms, parent_locals, ids, arrived, ops, coords, charge, place, near):
+def far_field(terms, parent_locals, ids, arrived, l2l_ops, atoms, place, near):
     whole = pl.BlockSpec(memory_space=VMEM)
     f32 = jnp.float32
     return pl.pallas_call(
         far_kernel,
         out_shape=(
-            jax.ShapeDtypeStruct(coords.shape, f32),
-            jax.ShapeDtypeStruct(charge.shape, f32),
+            jax.ShapeDtypeStruct((3,) + atoms.shape[1:], f32),
+            jax.ShapeDtypeStruct(atoms.shape[1:], f32),
         ),
-        in_specs=[whole] * 10,
+        in_specs=[whole] * 9,
         out_specs=(whole, whole),
         scratch_shapes=[
+            VMEM((COEF,) + atoms.shape[1:], f32),
             VMEM((3, LEAF_DEV, LANES), f32),
             VMEM((32, CAP, LANES), f32),
             VMEM((32, CAP, LANES), f32),
-            VMEM((4,) + charge.shape, f32),
+            VMEM(atoms.shape, f32),
             VMEM((G_ROWS, LANES), f32),
             pltpu.SemaphoreType.DMA((35,)),
             pltpu.SemaphoreType.DMA((35,)),
         ],
-        compiler_params=pltpu.CompilerParams(collective_id=1, has_side_effects=True, vmem_limit_bytes=16 * MIB),
+        compiler_params=pltpu.CompilerParams(collective_id=1, has_side_effects=True, vmem_limit_bytes=20 * MIB),
         name="far_field",
     )(
-        terms.reshape(GROUP, LEAF_DEV, LANES), parent_locals, ids, arrived, ops, coords, charge, place, near,
+        terms.reshape(GROUP, LEAF_DEV, LANES), parent_locals, ids, arrived, l2l_ops.transpose(1, 0, 2), atoms, place, near,
         jnp.asarray(gradient_matrix()),
     )
-
-
-def padded(ops):
-    return jnp.pad(ops, ((0, 0), (0, LANES - COEF), (0, LANES - COEF)))
 
 
 def shards(
@@ -730,22 +745,12 @@
     blocks = block_leaf.shape[0]
     leaves_all = leaf_slot.shape[0]
     parents_all = leaves_all // 8
-    coords = positions.reshape(3, blocks, LANES)
-    charge = charges.reshape(blocks, LANES)
-    table = leaf_slot.reshape(leaves_all // LANES, LANES)
-
-    packed, place = block_moments(coords, charge, block_leaf.reshape(1, blocks), table)
-    arrived = lax.all_to_all(packed, "dom", split_axis=0, concat_axis=0, tiled=True)
-    leaf_moments, parents_part, ids = leaves(arrived, table, padded(m2m_ops))
-    source_table, parent_table, near, leaf_keys, leaf_count, coarse_keys, coarse_count, turned_ops = gather(
-        leaf_moments,
-        parents_part,
-        coords,
-        charge,
-        (item_target, item_source, item_offset),
-        (coarse_target, coarse_source, coarse_offset),
-        m2l_ops,
-    )
+    atoms = jnp.concatenate([positions.reshape(3, blocks, LANES), charges.reshape(1, blocks, LANES)])
+    integers = [leaf_slot, item_target, item_source, item_offset, coarse_target, coarse_source, coarse_offset, block_leaf]
+    integers = jnp.concatenate([a.reshape(-1, LANES) for a in integers])
+    (
+        source_table, parent_table, near, leaf_keys, leaf_count, coarse_keys, coarse_count, turned_ops, arrived, place, ids
+    ) = gather(atoms, integers, m2m_ops, m2l_ops)
     source_table = source_table.reshape(leaves_all, LANES)
     parent_table = parent_table.reshape(parents_all, LANES)
     terms, parent_locals = translate(
@@ -757,9 +762,7 @@
         parent_table,
         turned_ops.reshape(OFFSETS + 1, ROWS, LANES),
     )
-    forces, potential = far_field(
-        terms, parent_locals, ids, arrived, padded(l2l_ops), coords, charge, place, near
-    )
+    forces, potential = far_field(terms, parent_locals, ids, arrived, l2l_ops, atoms, place, near)
     return forces.reshape(3, blocks * LANES), potential.reshape(blocks * LANES)
 
 

time: 137 us -> 123 us (0.90)
  starting transfers between devices: 8.59 us -> 0 us
  waiting for transfers between devices: 5.44 us -> 0 us
  Pallas kernels: 107 us -> 112 us
  local copies, waits for them, and re-layouts: 13.5 us -> 9.1 us
    pallas_call x1, Pallas kernels: 42.9 us -> 52.1 us  [gather(): pl.pallas_call(gather_kernel, out_shape=(jax.ShapeDtypeStruct((4, 4, 2, 4...]
    all_to_all x1 -> x0, starting transfers between devices: 8.59 us -> none  [shards(): lax.all_to_all(packed, 'dom', split_axis=0, concat_axis=0, tiled=True)]
    all_to_all x1 -> x0, waiting for transfers between devices: 5.44 us -> none  [shards(): lax.all_to_all(packed, 'dom', split_axis=0, concat_axis=0, tiled=True)]
    unnamed x31 -> x16, local copies, waits for them, and re-layouts: 13.4 us -> 8.43 us
    pallas_call x3 -> x1, Pallas kernels: 25.6 us -> 21.1 us  [far_field(): pl.pallas_call(far_kernel, out_shape=(jax.ShapeDtypeStruct((3,) + atoms.s...]
  transfers between devices with their start and end apart: 1 -> 0, of which waited for: 1 -> 0; matrix products, arithmetic and copies ran while one was open for 2% -> 0% of each run, Pallas kernels for 0% -> 0%
where the time goes in v5:
time: 123 us
  Pallas kernels  112 us (91%)
  local copies, waits for them, and re-layouts  9.1 us (7%)
    pallas_call x1, Pallas kernels, gather(): pl.pallas_call(gather_kernel, out_shape=(jax.ShapeDtypeStruct((4, 4, 2, 4...  52.1 us
    pallas_call x1, Pallas kernels, translate(): pl.pallas_call(translate_kernel, out_shape=(jax.ShapeDtypeStruct((4 * LEA...  38.7 us
    pallas_call x1, Pallas kernels, far_field(): pl.pallas_call(far_kernel, out_shape=(jax.ShapeDtypeStruct((3,) + atoms.s...  21.1 us
    unnamed x16, local copies, waits for them, and re-layouts  8.43 us

profile of v5, /device:TPU:1, one launch (start us, length us, event | category | flops | bytes accessed | tf_op | source)
XLA Modules:
  0.0 122.5 jit_solution(11499866080557178825)
XLA Ops:
  0.6 0.8 bitcast_dynamic-update-slice_fusion
  1.4 0.7 constant_dynamic-update-slice_fusion.5
  2.1 0.7 constant_dynamic-update-slice_fusion.4
  2.8 0.7 constant_dynamic-update-slice_fusion.3
  3.5 0.7 constant_dynamic-update-slice_fusion.2
  4.2 0.7 constant_dynamic-update-slice_fusion.1
  4.9 0.7 constant_dynamic-update-slice_fusion
  5.6 0.7 dynamic-update-slice.7.whole_ref
  6.3 1.0 copy.21
  7.3 0.9 pad_maximum_fusion.atoms_ref
  8.1 0.0 copy-start
  8.2 1.0 copy-done
  9.1 52.1 %gather.1 = (f32[4,4,2,4,64,128]{5,4,3,2,1,0:T(8,128)S(1)}, f32[4,4,4,2,8,128]{5,4,3,2,1,0:T(8,128)S(1)}, f32[4,128,128]{2,1,0:T(8,128)S(1)}, s32[64,128]{1,0:T(...) custom-call(f32[4,128,128]{2,1,0:T(8,128)S(1)} %pad_maximum_fusion.a, ...), custom_call_target="tpu_custom_call" | custom-call | tf_op jit(solution)/shard_map/gather/pallas_call | solution.py:552
  61.2 0.0 copy-start.1
  61.2 0.0 copy-start.2
  61.3 38.7 %translate.1 = (f32[256,128]{1,0:T(8,128)S(1)}, f32[64,128]{1,0:T(8,128)S(1)}) custom-call(s32[8192]{0:T(1024)S(1)} %bitcast.35, s32[1,128]{1,0:T(1,128)S(1)} %get-tuple-element.18.leaf_count, s32[4096]{0:T(1024)S(1)} %bitcast.36, s32[1,128]{1,0:T(1,128)S(1)} %get-tuple-element.20.coarse_count, f32[8192,128]{1,0:T(8,128)S(1)} %bitcast.28, ...), custom_call_target="tpu_custom_call" | custom-call | tf_op jit(solution)/shard_map/translate/pallas_call | solution.py:278
  100.0 0.0 copy-done.1
  100.0 0.0 copy-done.2
  100.0 21.1 %far_field.1 = (f32[3,128,128]{2,1,0:T(8,128)S(1)}, f32[128,128]{1,0:T(8,128)S(1)}) custom-call(f32[4,64,128]{2,1,0:T(8,128)S(1)} %bitcast.33, f32[64,128]{1,0:T(8,128)S(1)} %get-tuple-element.25.parent_ref, s32[64,128]{1,0:T(8,128)S(1)} %get-tuple-element.26.ids_ref, f32[32,8,128]{2,1,0:T(8,128)S(1)} %get-tuple-element.27.arrived_ref, ...), custom_call_target="tpu_custom_call" | custom-call | tf_op jit(solution)/shard_map/far_field/pallas_call | solution.py:704
  121.1 0.8 copy.20
  121.9 0.6 copy.30
Async XLA Ops:
  8.1 1.0 copy-start
  61.2 38.7 %copy-start.1 = (f32[8,81,81]{2,0,1:T(8,128)S(1)}, f32[8,81,81]{2,0,1:T(8,128)}, u32[]{:S(2)}) copy-start(f32[8,81,81]{2,0,1:T(8,128)} %param.19) | copy-start | bytes 629860
  61.2 38.7 %copy-start.2 = (f32[288,128]{1,0:T(8,128)S(1)}, f32[288,128]{1,0:T(8,128)}, u32[]{:S(2)}) copy-start(f32[288,128]{1,0:T(8,128)} %constant.2.clone.matrix_ref) | copy-start | bytes 442372

commit v6 on v5

--- a/solution.py
+++ b/solution.py
@@ -231,8 +231,17 @@
     count_ref[...] = jnp.broadcast_to(fours, count_ref.shape)
 
 
-def translate_kernel(leaf_keys, leaf_count, coarse_keys, coarse_count, leaf_src, coarse_src, ops, leaf_out, coarse_out, acc):
-    def work(keys, count, src, out):
+def translate_kernel(
+    leaf_list, leaf_count, coarse_list, coarse_count, leaf_src, coarse_src, ops, leaf_out, coarse_out, acc, leaf_keys, coarse_keys, sems
+):
+    loads = [
+        pltpu.make_async_copy(listing.at[pl.ds(0, keys.shape[0])], keys, sems.at[n])
+        for n, (listing, keys) in enumerate(((coarse_list, coarse_keys), (leaf_list, leaf_keys)))
+    ]
+    for load in loads:
+        load.start()
+
+    def work(load, keys, count, src, out):
         targets = out.shape[0]
 
         def clear(t, carry):
@@ -241,6 +250,7 @@
             return carry
 
         lax.fori_loop(0, targets // 4, clear, 0)
+        load.wait()
 
         def term(key):
             row = src[pl.ds((key >> 9) & (src.shape[0] - 1), 1), :][:, :COEF]
@@ -268,8 +278,8 @@
             padded = jnp.concatenate([columns, jnp.zeros((LANES - ROWS, LANES), jnp.float32)], axis=0)
             out[low : low + size, :] = padded.T[:size]
 
-    work(coarse_keys, coarse_count, coarse_src, coarse_out)
-    work(leaf_keys, leaf_count, leaf_src, leaf_out)
+    work(loads[0], coarse_keys, coarse_count, coarse_src, coarse_out)
+    work(loads[1], leaf_keys, leaf_count, leaf_src, leaf_out)
 
 
 def translate(leaf_keys, leaf_count, coarse_keys, coarse_count, leaf_table, coarse_table, ops):
@@ -281,9 +291,14 @@
             jax.ShapeDtypeStruct((4 * LEAF_DEV, LANES), jnp.float32),
             jax.ShapeDtypeStruct((LEAF_DEV, LANES), jnp.float32),
         ),
-        in_specs=[smem] * 4 + [whole] * 3,
+        in_specs=[pl.BlockSpec(memory_space=pl.ANY), smem] * 2 + [whole] * 3,
         out_specs=(whole, whole),
-        scratch_shapes=[VMEM((4 * LEAF_DEV, ROWS, LANES), jnp.float32)],
+        scratch_shapes=[
+            VMEM((4 * LEAF_DEV, ROWS, LANES), jnp.float32),
+            pltpu.SMEM((5120,), jnp.int32),
+            pltpu.SMEM((3072,), jnp.int32),
+            pltpu.SemaphoreType.DMA((2,)),
+        ],
         compiler_params=pltpu.CompilerParams(vmem_limit_bytes=36 * MIB),
         name="translate",
     )(leaf_keys.reshape(-1), leaf_count, coarse_keys.reshape(-1), coarse_count, leaf_table, coarse_table, ops)
@@ -319,47 +334,30 @@
     lax.fori_loop(low, high, group, 0)
 
 
-PARTS = ((0, 16, 24, (2, 0, 1)), (24, 32, 48, (0, 1, 2)), (48, 56, 64, (1, 2, 0)))
-COPIES = 68
-SLABS = 9
-
-
-def gather_kernel(
-    atoms_ref, whole_ref, m2m_ref, m2l_hbm,
-    all_ref, parent_ref, near_ref, lkeys_ref, lcount_ref, ckeys_ref, ccount_ref, m2l_ref, arrived_ref, place_ref, ids_ref,
-    packed, turned, acc, rows, part_ref, got_c, got_x, got_y, sum_c, sum_x, slabs, send_sem, recv_sem, slab_sem, out_sem, in_sem
-):
-    dom, lvl = lax.axis_index("dom"), lax.axis_index("lvl")
-    here = (dom // 8, (dom // 2) % 4, lvl)
-    core = dom % 2
-    table_ref = whole_ref.at[0:64]
-    leaf_items = [whole_ref.at[64 + 32 * n : 96 + 32 * n] for n in range(3)]
-    coarse_items = [whole_ref.at[160 + 16 * n : 176 + 16 * n] for n in range(3)]
-
-    def device(place, which):
-        return ((place[0] * 4 + place[1]) * 2 + which, place[2])
-
-    def moved(axis, by):
-        return tuple((v + by) % 4 if n == axis else v for n, v in enumerate(here))
-
-    def slab(g, slot):
-        return pltpu.make_async_copy(m2l_hbm.at[pl.ds(g * SLABS, SLABS)], slabs.at[slot], slab_sem.at[slot])
-
-    twin = device(here, 1 - core)
-    m2l_ref[OFFSETS * ROWS :, :] = jnp.zeros((ROWS, LANES), jnp.float32)
-    slab(0, 0).start()
-    barrier = pltpu.get_barrier_semaphore()
-
-    def greet(d, carry):
-        pl.semaphore_signal(barrier, inc=1, device_id=((dom + d) % 32, lvl), device_id_type=MESH)
-        return carry
-
-    lax.fori_loop(1, 32, greet, 0)
-    for by in (1, 2, 3):
-        pl.semaphore_signal(barrier, inc=1, device_id=(dom, (lvl + by) % 4), device_id_type=MESH)
-    block_moments(atoms_ref, table_ref[...], whole_ref[208:209, :], place_ref, packed, turned, acc, rows)
-    pl.semaphore_wait(barrier, 34)
-
+class Place:
+    def __init__(self):
+        dom = lax.axis_index("dom")
+        self.here = (dom // 8, (dom // 2) % 4, lax.axis_index("lvl"))
+        self.core = dom % 2
+        self.twin = self.device(self.here, 1 - self.core)
+
+    def device(self, place, core):
+        return ((place[0] * 4 + place[1]) * 2 + core, place[2])
+
+    def moved(self, axis, by):
+        place = tuple((v + by) % 4 if n == axis else v for n, v in enumerate(self.here))
+        return self.device(place, self.core)
+
+    def greet(self):
+        barrier = pltpu.get_barrier_semaphore()
+        for axis in range(3):
+            for by in (1, 2, 3):
+                pl.semaphore_signal(barrier, inc=1, device_id=self.moved(axis, by), device_id_type=MESH)
+        pl.semaphore_signal(barrier, inc=1, device_id=self.twin, device_id_type=MESH)
+        return barrier
+
+
+def sender(send_sem, recv_sem):
     started = []
 
     def send(source, target, where):
@@ -376,6 +374,55 @@
         started.append(copy)
         return copy
 
+    return started, send
+
+
+def exchange(place, send, source, one, two, target, between):
+    (y, x, z), core = place.here, place.core
+    copy = send(source.at[:, :, 1 - core], one.at[core], place.twin)
+    one[core] = source[:, :, core]
+    between(0)
+    copy.wait_recv()
+    copies = [send(one.at[:, :, (x + by) % 4], two.at[x], place.moved(1, by)) for by in (1, 2, 3)]
+    two[x] = one[:, :, x]
+    between(1)
+    for copy in copies:
+        copy.wait_recv()
+    copies = [send(two.at[:, :, (y + by) % 4], target.at[y], place.moved(0, by)) for by in (1, 2, 3)]
+    target[y] = two[:, :, y]
+    between(2)
+    for copy in copies:
+        copy.wait_recv()
+
+
+PARTS = ((0, 16, 24, (2, 0, 1)), (24, 32, 48, (0, 1, 2)), (48, 56, 64, (1, 2, 0)))
+COPIES = 66
+NEAR_FIRST = 4
+SLABS = 9
+
+
+def gather_kernel(
+    atoms_ref, whole_ref, m2m_ref, m2l_hbm,
+    all_ref, parent_ref, near_ref, lkeys_ref, lcount_ref, ckeys_ref, ccount_ref, m2l_ref, arrived_ref, place_ref, ids_ref,
+    packed, one, two, turned, acc, rows, part_ref, got_c, got_x, got_y, sum_c, sum_x, slabs, send_sem, recv_sem, slab_sem
+):
+    me = Place()
+    here, core, twin = me.here, me.core, me.twin
+    table_ref = whole_ref.at[0:64]
+    leaf_items = [whole_ref.at[64 + 32 * n : 96 + 32 * n] for n in range(3)]
+    coarse_items = [whole_ref.at[160 + 16 * n : 176 + 16 * n] for n in range(3)]
+
+    def slab(g, slot):
+        return pltpu.make_async_copy(m2l_hbm.at[pl.ds(g * SLABS, SLABS)], slabs.at[slot], slab_sem.at[slot])
+
+    m2l_ref[OFFSETS * ROWS :, :] = jnp.zeros((ROWS, LANES), jnp.float32)
+    slab(0, 0).start()
+    barrier = me.greet()
+    block_moments(atoms_ref, table_ref[...], whole_ref[208:209, :], place_ref, packed, turned, acc, rows)
+    pl.semaphore_wait(barrier, 10)
+
+    started, send = sender(send_sem, recv_sem)
+
     def block(done, axis, by, low, high):
         y, x, z = (
             slice(None) if n in done else ((here[n] + by) % 4 if n == axis else here[n]) for n in range(3)
@@ -400,20 +447,20 @@
         if n == 1:
             sum_c[...] = part_ref[:, :, core] + got_c[...]
             waiting["p"] = [
-                send(sum_c.at[:, (here[1] + by) % 4], got_x.at[by - 1], device(moved(1, by), core)) for by in (1, 2, 3)
+                send(sum_c.at[:, (here[1] + by) % 4], got_x.at[by - 1], me.moved(1, by)) for by in (1, 2, 3)
             ]
         elif n == 2:
             sum_x[...] = (sum_c[:, here[1]] + got_x[0]) + (got_x[1] + got_x[2])
             waiting["p"] = [
-                send(sum_x.at[(here[0] + by) % 4], got_y.at[by - 1], device(moved(0, by), core)) for by in (1, 2, 3)
+                send(sum_x.at[(here[0] + by) % 4], got_y.at[by - 1], me.moved(0, by)) for by in (1, 2, 3)
             ]
         elif n == 3:
             parent_ref[here[2], here[0], here[1], core] = (sum_x[here[0]] + got_y[0]) + (got_y[1] + got_y[2])
-            waiting["p"] = [put(parents(()), device(moved(2, by), core)) for by in (1, 2, 3)]
+            waiting["p"] = [put(parents(()), me.moved(2, by)) for by in (1, 2, 3)]
         elif n == 4:
-            waiting["p"] = [put(parents((2,)), device(moved(0, by), core)) for by in (1, 2, 3)]
+            waiting["p"] = [put(parents((2,)), me.moved(0, by)) for by in (1, 2, 3)]
         elif n == 5:
-            waiting["p"] = [put(parents((2, 0)), device(moved(1, by), core)) for by in (1, 2, 3)]
+            waiting["p"] = [put(parents((2, 0)), me.moved(1, by)) for by in (1, 2, 3)]
         elif n == 6:
             waiting["p"] = [put(parents((2, 0, 1)), twin)]
 
@@ -458,37 +505,19 @@
         lax.fori_loop(low, high, group, 0)
 
     def fill(n):
-        if n < 3:
-            sort(60 * n, 60 * n + 60)
-        turn(*((0, 0), (0, 0), (0, 0), (0, 4), (4, 7), (7, 9), (9, 9), (9, 9))[n])
-        near_groups(atoms_ref, atoms_ref.at[3], near_ref, *((0, 0), (0, 0), (0, 0), (0, 0), (0, 0), (0, 2), (2, 6), (6, 16))[n])
-
-    def message(d):
-        goal = (dom + d) % 32
-        return pltpu.make_async_remote_copy(
-            src_ref=packed.at[goal],
-            dst_ref=arrived_ref.at[dom],
-            send_sem=out_sem.at[d],
-            recv_sem=in_sem.at[d],
-            device_id=(goal, lvl),
-            device_id_type=MESH,
-        )
-
-    def each(act):
-        def one(d, carry):
-            act(message(d))
-            return carry
-
-        lax.fori_loop(1, 32, one, 0)
-
-    each(lambda copy: copy.start())
-    arrived_ref[dom] = packed[dom]
-    write_keys(leaf_items, 4 * LEAF_DEV, 8192, lkeys_ref, lcount_ref)
-    write_keys(coarse_items, LEAF_DEV, 1024, ckeys_ref, ccount_ref)
-    fill(0)
-    each(lambda copy: copy.wait_recv())
+        if n == 0:
+            write_keys(leaf_items, 4 * LEAF_DEV, 8192, lkeys_ref, lcount_ref)
+            write_keys(coarse_items, LEAF_DEV, 1024, ckeys_ref, ccount_ref)
+        elif n < 5:
+            sort(44 * n - 44, 44 * n)
+        turn(*((0, 0), (0, 0), (0, 0), (0, 0), (0, 1), (1, 5), (5, 8), (8, 9))[n])
+        if n == 7:
+            near_groups(atoms_ref, atoms_ref.at[3], near_ref, 0, NEAR_FIRST)
+
+    exchange(me, send, packed, one, two, arrived_ref, fill)
+    first_slot = ((here[0] * 4 + here[1]) * 2 + core) * GROUP * LEAF_DEV + here[2] * LEAF_DEV
     all_ref[here[0], here[1], core, here[2]] = leaf_moments(
-        arrived_ref[...].reshape(32 * CAP, LANES), table_ref, m2m_ref, lvl, (dom * GROUP + lvl) * LEAF_DEV, part_ref, ids_ref
+        arrived_ref[...].reshape(32 * CAP, LANES), table_ref, m2m_ref, here[2], first_slot, part_ref, ids_ref
     )
 
     last = []
@@ -496,43 +525,38 @@
         direct = []
         for low, middle, high, order in PARTS:
             axis, done = order[phase], order[:phase]
-            direct.append([put(block(done, axis, 0, low, high), device(moved(axis, by), core)) for by in (1, 3, 2)])
-        stage(phase)
-        fill(phase + 1)
+            direct.append([put(block(done, axis, 0, low, high), me.moved(axis, by)) for by in (1, 3, 2)])
+        stage(2 * phase)
+        fill(phase + 3)
+        stage(2 * phase + 1)
         for (low, middle, high, order), copies in zip(PARTS, direct):
-            axis, done = order[phase], order[:phase]
-            for by, copy in zip((3, 1, 2), copies):
+            for copy in copies:
                 copy.wait_recv()
-                if phase:
-                    last.append(put(block(done, axis, by, low, high), twin))
-            if not phase:
-                last.append(put(block((axis,), axis, 0, low, high), twin))
     first, second = [], []
     for low, middle, high, order in PARTS:
         axis, done = order[2], order[:2]
-        first.append([put(block(done, axis, 0, low, high), device(moved(axis, by), core)) for by in (1, 3)])
-    stage(2)
-    fill(3)
+        first.append([put(block(done, axis, 0, low, high), me.moved(axis, by)) for by in (1, 3)])
+    for low, middle, high, order in PARTS:
+        last.append(put(block(order[:2], order[2], 0, low, high), twin))
+    stage(4)
+    fill(5)
     for (low, middle, high, order), (right, left) in zip(PARTS, first):
         axis, done = order[2], order[:2]
         right.wait_recv()
-        a = put(block(done, axis, 3, low, middle), device(moved(axis, 1), core))
+        a = put(block(done, axis, 3, low, middle), me.moved(axis, 1))
         left.wait_recv()
-        b = put(block(done, axis, 1, middle, high), device(moved(axis, 3), core))
+        b = put(block(done, axis, 1, middle, high), me.moved(axis, 3))
         second.append((a, b))
-        last.append(put(block(done, axis, 3, low, high), twin))
-        last.append(put(block(done, axis, 1, low, high), twin))
-    stage(3)
-    fill(4)
+    for low, middle, high, order in PARTS:
+        last.append(put(block(order[:2], order[2], 3, low, high), twin))
+        last.append(put(block(order[:2], order[2], 1, low, high), twin))
+    stage(5)
+    fill(6)
     for (low, middle, high, order), pair in zip(PARTS, second):
         axis, done = order[2], order[:2]
         for copy in pair:
             copy.wait_recv()
         last.append(put(block(done, axis, 2, low, high), twin))
-    stage(4)
-    fill(5)
-    stage(5)
-    fill(6)
     stage(6)
     fill(7)
     for copy in last:
@@ -541,7 +565,6 @@
         copy.wait_recv()
     for copy in started:
         copy.wait_send()
-    each(lambda copy: copy.wait_send())
     assert len(started) == COPIES
 
 
@@ -560,14 +583,16 @@
             jax.ShapeDtypeStruct((32, LANES), i32),
             jax.ShapeDtypeStruct((1, LANES), i32),
             jax.ShapeDtypeStruct(((OFFSETS + 1) * ROWS, LANES), f32),
-            jax.ShapeDtypeStruct((32, CAP, LANES), f32),
+            jax.ShapeDtypeStruct((4, 4, 2, CAP, LANES), f32),
             jax.ShapeDtypeStruct((1, blocks), i32),
             jax.ShapeDtypeStruct((LEAF_DEV, LANES), i32),
         ),
         in_specs=[whole] * 3 + [pl.BlockSpec(memory_space=pl.ANY)],
         out_specs=(whole,) * 11,
         scratch_shapes=[
-            VMEM((32, CAP, LANES), f32),
+            VMEM((4, 4, 2, CAP, LANES), f32),
+            VMEM((2, 4, 4, CAP, LANES), f32),
+            VMEM((4, 2, 4, CAP, LANES), f32),
             VMEM((4, LANES, blocks), f32),
             VMEM((COEF, 8, blocks), f32),
             VMEM((LANES, blocks), f32),
@@ -581,8 +606,6 @@
             pltpu.SemaphoreType.DMA((COPIES,)),
             pltpu.SemaphoreType.DMA((COPIES,)),
             pltpu.SemaphoreType.DMA((2,)),
-            pltpu.SemaphoreType.DMA((32,)),
-            pltpu.SemaphoreType.DMA((32,)),
         ],
         compiler_params=pltpu.CompilerParams(collective_id=0, has_side_effects=True, vmem_limit_bytes=42 * MIB),
         name="gather",
@@ -591,38 +614,19 @@
 
 def far_kernel(
     terms_ref, parent_ref, ids_ref, arrived_ref, ops_ref, atoms_ref, place_ref, near_ref, matrix_ref,
-    force_ref, phi_ref, basis, got, sent, returned, turned, lines, send_sem, recv_sem
+    force_ref, phi_ref, basis, near, got, sent, one, two, returned, turned, lines, send_sem, recv_sem
 ):
-    dom, lvl = lax.axis_index("dom"), lax.axis_index("lvl")
+    me = Place()
+    lvl = me.here[2]
     blocks = atoms_ref.shape[1]
-    barrier = pltpu.get_barrier_semaphore()
-
-    def greet(d, carry):
-        pl.semaphore_signal(barrier, inc=1, device_id=((dom + d) % 32, lvl), device_id_type=MESH)
-        return carry
-
-    for by in (1, 2, 3):
-        pl.semaphore_signal(barrier, inc=1, device_id=(dom, (lvl + by) % 4), device_id_type=MESH)
-    lax.fori_loop(1, 32, greet, 0)
+    barrier = me.greet()
     for d in range(3):
         turned[d] = atoms_ref[d].T
     shifted = by_octant(parent_ref[...], ops_ref, ids_ref[...][:, 0:1] & 7)
-    pl.semaphore_wait(barrier, 34)
-
-    shared = []
-    for by in (1, 2, 3):
-        goal = (lvl + by) % 4
-        copy = pltpu.make_async_remote_copy(
-            src_ref=terms_ref.at[goal],
-            dst_ref=got.at[by - 1],
-            send_sem=send_sem.at[31 + by],
-            recv_sem=recv_sem.at[31 + by],
-            device_id=(dom, goal),
-            device_id_type=MESH,
-        )
-        copy.start()
-        shared.append(copy)
-
+    pl.semaphore_wait(barrier, 10)
+
+    started, send = sender(send_sem, recv_sem)
+    shared = [send(terms_ref.at[(lvl + by) % 4], got.at[by - 1], me.moved(2, by)) for by in (1, 2, 3)]
     total = shifted + terms_ref[lvl]
 
     def prepare(i, carry):
@@ -634,7 +638,14 @@
         harmonics(turned[0, at, :], turned[1, at, :], turned[2, at, :], emit)
         return carry
 
-    lax.fori_loop(0, 2, prepare, 0)
+    lax.fori_loop(0, 3, prepare, 0)
+    done = NEAR_FIRST * 8
+    near[:, 0:done] = near_ref[:, 0:done]
+
+    def fill(low, high):
+        near_groups(atoms_ref, atoms_ref.at[3], near, low, high)
+
+    fill(4, 8)
     tags = arrived_ref[...].reshape(32 * CAP, LANES)[:, 127:128].astype(jnp.int32)
     member = (iota((32 * CAP, LEAF_DEV), 1) + 1 == tags).astype(jnp.float32)
     for copy in shared:
@@ -642,31 +653,14 @@
     total = (total + got[0]) + (got[1] + got[2])
     sent[...] = dot(member, total).reshape(sent.shape)
 
-    def message(d):
-        goal = (dom + d) % 32
-        return pltpu.make_async_remote_copy(
-            src_ref=sent.at[goal],
-            dst_ref=returned.at[dom],
-            send_sem=send_sem.at[d],
-            recv_sem=recv_sem.at[d],
-            device_id=(goal, lvl),
-            device_id_type=MESH,
-        )
-
-    def start(d, carry):
-        message(d).start()
-        return carry
-
-    lax.fori_loop(1, 32, start, 0)
-    returned[dom] = sent[dom]
-    lax.fori_loop(2, 4, prepare, 0)
+    def between(n):
+        if n == 0:
+            lax.fori_loop(3, 4, prepare, 0)
+        fill(*((8, 10), (10, 13), (13, 16))[n])
+
+    exchange(me, send, sent, one, two, returned, between)
     spread = (iota((32 * CAP, blocks), 0) == place_ref[...]).astype(jnp.float32)
 
-    def receive(d, carry):
-        message(d).wait_recv()
-        return carry
-
-    lax.fori_loop(1, 32, receive, 0)
     columns = dot(returned[...].reshape(32 * CAP, LANES), spread, ((0,), (0,)))
     lines[...] = dot(matrix_ref[...], columns)
 
@@ -686,15 +680,10 @@
     lax.fori_loop(0, 4, chunk, 0)
     charge = atoms_ref[3]
     for d in range(3):
-        force_ref[d] = near_ref[d] - charge * turned[d].T
-    phi_ref[...] = near_ref[3] + turned[3].T
-
-    def leave(d, carry):
-        message(d).wait_send()
-        return carry
-
-    lax.fori_loop(1, 32, leave, 0)
-    for copy in shared:
+        force_ref[d] = near[d] - charge * turned[d].T
+    phi_ref[...] = near[3] + turned[3].T
+
+    for copy in started:
         copy.wait_send()
 
 
@@ -711,13 +700,16 @@
         out_specs=(whole, whole),
         scratch_shapes=[
             VMEM((COEF,) + atoms.shape[1:], f32),
+            VMEM(atoms.shape, f32),
             VMEM((3, LEAF_DEV, LANES), f32),
-            VMEM((32, CAP, LANES), f32),
-            VMEM((32, CAP, LANES), f32),
+            VMEM((4, 4, 2, CAP, LANES), f32),
+            VMEM((2, 4, 4, CAP, LANES), f32),
+            VMEM((4, 2, 4, CAP, LANES), f32),
+            VMEM((4, 4, 2, CAP, LANES), f32),
             VMEM(atoms.shape, f32),
             VMEM((G_ROWS, LANES), f32),
-            pltpu.SemaphoreType.DMA((35,)),
-            pltpu.SemaphoreType.DMA((35,)),
+            pltpu.SemaphoreType.DMA((10,)),
+            pltpu.SemaphoreType.DMA((10,)),
         ],
         compiler_params=pltpu.CompilerParams(collective_id=1, has_side_effects=True, vmem_limit_bytes=20 * MIB),
         name="far_field",

time: 123 us -> 119 us (0.967); the launches traced: 123 us -> 117 us
  Pallas kernels: 112 us -> 106 us
    pallas_call x1, Pallas kernels: 52.1 us -> 48.3 us  [gather(): pl.pallas_call(gather_kernel, out_shape=(jax.ShapeDtypeStruct((4, 4, 2, 4...]
    pallas_call x1, Pallas kernels: 21.1 us -> 18.8 us  [far_field(): pl.pallas_call(far_kernel, out_shape=(jax.ShapeDtypeStruct((3,) + atoms.s...]
where the time goes in v6:
time: 119 us; the launch traced here: 117 us
  Pallas kernels  106 us (89%)
  local copies, waits for them, and re-layouts  9.1 us (8%)
    pallas_call x1, Pallas kernels, gather(): pl.pallas_call(gather_kernel, out_shape=(jax.ShapeDtypeStruct((4, 4, 2, 4...  48.3 us
    pallas_call x1, Pallas kernels, translate(): pl.pallas_call(translate_kernel, out_shape=(jax.ShapeDtypeStruct((4 * LEA...  39.1 us
    pallas_call x1, Pallas kernels, far_field(): pl.pallas_call(far_kernel, out_shape=(jax.ShapeDtypeStruct((3,) + atoms.s...  18.8 us
    unnamed x16, local copies, waits for them, and re-layouts  8.43 us

profile of v6, /device:TPU:1, one launch (start us, length us, event | category | flops | bytes accessed | tf_op | source)
XLA Modules:
  0.0 116.8 jit_solution(9942858032217325542)
XLA Ops:
  0.6 0.8 bitcast_dynamic-update-slice_fusion
  1.4 0.7 constant_dynamic-update-slice_fusion.5
  2.1 0.7 constant_dynamic-update-slice_fusion.4
  2.8 0.7 constant_dynamic-update-slice_fusion.3
  3.5 0.7 constant_dynamic-update-slice_fusion.2
  4.2 0.7 constant_dynamic-update-slice_fusion.1
  4.9 0.7 constant_dynamic-update-slice_fusion
  5.6 0.7 dynamic-update-slice.7.whole_ref
  6.3 1.0 copy.21
  7.3 0.9 pad_maximum_fusion.atoms_ref
  8.1 0.0 copy-start
  8.2 1.0 copy-done
  9.1 48.3 %gather.1 = (f32[4,4,2,4,64,128]{5,4,3,2,1,0:T(8,128)S(1)}, f32[4,4,4,2,8,128]{5,4,3,2,1,0:T(8,128)S(1)}, f32[4,128,128]{2,1,0:T(8,128)S(1)}, s32[64,128]{1,0:T(...) custom-call(f32[4,128,128]{2,1,0:T(8,128)S(1)} %pad_maximum_fusion.a, ...), custom_call_target="tpu_custom_call" | custom-call | tf_op jit(solution)/shard_map/gather/pallas_call | solution.py:575
  57.4 0.0 copy-start.1
  57.4 0.0 copy-start.2
  57.4 39.1 %translate.1 = (f32[256,128]{1,0:T(8,128)S(1)}, f32[64,128]{1,0:T(8,128)S(1)}) custom-call(s32[8192]{0:T(1024)S(1)} %bitcast.35, s32[1,128]{1,0:T(1,128)S(1)} %get-tuple-element.18.leaf_count, s32[4096]{0:T(1024)S(1)} %bitcast.36, s32[1,128]{1,0:T(1,128)S(1)} %get-tuple-element.20.coarse_count, f32[8192,128]{1,0:T(8,128)S(1)} %bitcast.28, ...), custom_call_target="tpu_custom_call" | custom-call | tf_op jit(solution)/shard_map/translate/pallas_call | solution.py:288
  96.5 0.0 copy-done.1
  96.5 0.0 copy-done.2
  96.5 18.8 %far_field.1 = (f32[3,128,128]{2,1,0:T(8,128)S(1)}, f32[128,128]{1,0:T(8,128)S(1)}) custom-call(f32[4,64,128]{2,1,0:T(8,128)S(1)} %bitcast.33, f32[64,128]{1,0:T(8,128)S(1)} %get-tuple-element.25.parent_ref, s32[64,128]{1,0:T(8,128)S(1)} %get-tuple-element.26.ids_ref, f32[4,4,2,8,128]{4,3,2,1,0:T(8,128)S(1)} %get-tuple-element.27.arrived_ref, ...), custom_call_target="tpu_custom_call" | custom-call | tf_op jit(solution)/shard_map/far_field/pallas_call | solution.py:693
  115.4 0.8 copy.20
  116.2 0.6 copy.30
Async XLA Ops:
  8.1 1.0 copy-start
  57.4 39.1 %copy-start.1 = (f32[8,81,81]{2,0,1:T(8,128)S(1)}, f32[8,81,81]{2,0,1:T(8,128)}, u32[]{:S(2)}) copy-start(f32[8,81,81]{2,0,1:T(8,128)} %param.19) | copy-start | bytes 629860
  57.4 39.1 %copy-start.2 = (f32[288,128]{1,0:T(8,128)S(1)}, f32[288,128]{1,0:T(8,128)}, u32[]{:S(2)}) copy-start(f32[288,128]{1,0:T(8,128)} %constant.2.clone.matrix_ref) | copy-start | bytes 442372

commit v7 on v6

--- a/solution.py
+++ b/solution.py
@@ -257,13 +257,13 @@
             return ops[key & 511, :COEF, :COEF] * row
 
         def step(i, carry):
-            for u in range(4):
-                four = [keys[i * 16 + u * 4 + n] for n in range(4)]
+            for u in range(8):
+                four = [keys[i * 32 + u * 4 + n] for n in range(4)]
                 total = (term(four[0]) + term(four[1])) + (term(four[2]) + term(four[3]))
                 acc[four[0] >> 23, :COEF, :COEF] += total
             return carry
 
-        lax.fori_loop(0, (count[0, 0] + 3) // 4, step, 0)
+        lax.fori_loop(0, (count[0, 0] + 7) // 8, step, 0)
         lane = iota((ROWS, LANES), 1)
         for low in range(0, targets, LANES):
             size = min(LANES, targets - low)
@@ -299,39 +299,44 @@
             pltpu.SMEM((3072,), jnp.int32),
             pltpu.SemaphoreType.DMA((2,)),
         ],
-        compiler_params=pltpu.CompilerParams(vmem_limit_bytes=36 * MIB),
+        compiler_params=pltpu.CompilerParams(vmem_limit_bytes=16 * MIB),
         name="translate",
     )(leaf_keys.reshape(-1), leaf_count, coarse_keys.reshape(-1), coarse_count, leaf_table, coarse_table, ops)
 
 
-def near_groups(pos_ref, q_ref, out_ref, low, high):
-    def group(g, carry):
-        at = pl.ds(pl.multiple_of(g * 8, 8), 8)
-        rows = [pos_ref[d, at, :] for d in range(3)] + [q_ref[at, :]]
-        columns = [r.T for r in rows]
-        for b in range(8):
-            xj, yj, zj, qj = (r[b : b + 1, :] for r in rows)
-            xi, yi, zi, qi = (c[:, b : b + 1] for c in columns)
-            sums = [jnp.zeros((8, LANES), jnp.float32) for _ in range(4)]
-            for c in range(4):
-                part = slice(c * 32, c * 32 + 32)
-                dx = xj - xi[part]
-                dy = yj - yi[part]
-                dz = zj - zi[part]
-                inverse = lax.rsqrt(dx * dx + dy * dy + dz * dz + SOFTENING)
-                same = iota((32, LANES), 0) + c * 32 == iota((32, LANES), 1)
-                weighted = jnp.where(same, 0.0, inverse * qi[part])
-                strength = weighted * (inverse * inverse)
-                for n, term in enumerate((strength * dx, strength * dy, strength * dz, weighted)):
-                    sums[n] = sums[n] + ((term[0:8] + term[8:16]) + (term[16:24] + term[24:32]))
-            for n in range(4):
-                line = jnp.sum(sums[n], axis=0, keepdims=True)
-                if n < 3:
-                    line = line * qj
-                out_ref[n, pl.ds(g * 8 + b, 1), :] = line
+def near_tiles(atoms, out, low, high):
+    def tile(t, carry):
+        at = pl.ds(pl.multiple_of(t * 32, 32), 32)
+        x, y, z = (atoms[d, at, :] for d in range(3))
+        own = iota((32, LANES), 0) + t * 32
+
+        def fours(masked):
+            def four(i, sums):
+                for u in range(4):
+                    j = i * 4 + u
+                    xj, yj, zj, qj = (atoms[d, pl.ds(j, 1), :] for d in range(4))
+                    dx, dy, dz = x - xj, y - yj, z - zj
+                    inverse = lax.rsqrt(dx * dx + dy * dy + dz * dz + SOFTENING)
+                    weighted = inverse * qj
+                    if masked:
+                        weighted = jnp.where(own == j, 0.0, weighted)
+                    strength = weighted * (inverse * inverse)
+                    terms = (strength * dx, strength * dy, strength * dz, weighted)
+                    sums = tuple(a + b for a, b in zip(sums, terms))
+                return sums
+
+            return four
+
+        sums = (jnp.zeros((32, LANES), jnp.float32),) * 4
+        sums = lax.fori_loop(0, t * 8, fours(False), sums)
+        sums = lax.fori_loop(t * 8, t * 8 + 8, fours(True), sums)
+        sums = lax.fori_loop(t * 8 + 8, 32, fours(False), sums)
+        for d in range(3):
+            out[d, at, :] = sums[d] * atoms[3, at, :]
+        out[3, at, :] = sums[3]
         return carry
 
-    lax.fori_loop(low, high, group, 0)
+    lax.fori_loop(low, high, tile, 0)
 
 
 class Place:
@@ -397,13 +402,12 @@
 
 PARTS = ((0, 16, 24, (2, 0, 1)), (24, 32, 48, (0, 1, 2)), (48, 56, 64, (1, 2, 0)))
 COPIES = 66
-NEAR_FIRST = 4
 SLABS = 9
 
 
 def gather_kernel(
     atoms_ref, whole_ref, m2m_ref, m2l_hbm,
-    all_ref, parent_ref, near_ref, lkeys_ref, lcount_ref, ckeys_ref, ccount_ref, m2l_ref, arrived_ref, place_ref, ids_ref,
+    all_ref, parent_ref, lkeys_ref, lcount_ref, ckeys_ref, ccount_ref, m2l_ref, arrived_ref, place_ref, ids_ref,
     packed, one, two, turned, acc, rows, part_ref, got_c, got_x, got_y, sum_c, sum_x, slabs, send_sem, recv_sem, slab_sem
 ):
     me = Place()
@@ -511,8 +515,6 @@
         elif n < 5:
             sort(44 * n - 44, 44 * n)
         turn(*((0, 0), (0, 0), (0, 0), (0, 0), (0, 1), (1, 5), (5, 8), (8, 9))[n])
-        if n == 7:
-            near_groups(atoms_ref, atoms_ref.at[3], near_ref, 0, NEAR_FIRST)
 
     exchange(me, send, packed, one, two, arrived_ref, fill)
     first_slot = ((here[0] * 4 + here[1]) * 2 + core) * GROUP * LEAF_DEV + here[2] * LEAF_DEV
@@ -577,7 +579,6 @@
         out_shape=(
             jax.ShapeDtypeStruct((4, 4, 2, 4, LEAF_DEV, LANES), f32),
             jax.ShapeDtypeStruct((4, 4, 4, 2, 8, LANES), f32),
-            jax.ShapeDtypeStruct(atoms.shape, f32),
             jax.ShapeDtypeStruct((64, LANES), i32),
             jax.ShapeDtypeStruct((1, LANES), i32),
             jax.ShapeDtypeStruct((32, LANES), i32),
@@ -588,7 +589,7 @@
             jax.ShapeDtypeStruct((LEAF_DEV, LANES), i32),
         ),
         in_specs=[whole] * 3 + [pl.BlockSpec(memory_space=pl.ANY)],
-        out_specs=(whole,) * 11,
+        out_specs=(whole,) * 10,
         scratch_shapes=[
             VMEM((4, 4, 2, CAP, LANES), f32),
             VMEM((2, 4, 4, CAP, LANES), f32),
@@ -607,20 +608,20 @@
             pltpu.SemaphoreType.DMA((COPIES,)),
             pltpu.SemaphoreType.DMA((2,)),
         ],
-        compiler_params=pltpu.CompilerParams(collective_id=0, has_side_effects=True, vmem_limit_bytes=42 * MIB),
+        compiler_params=pltpu.CompilerParams(collective_id=0, has_side_effects=True, vmem_limit_bytes=24 * MIB),
         name="gather",
     )(atoms, integers, m2m_ops.transpose(1, 0, 2), m2l_ops.transpose(1, 2, 0))
 
 
 def far_kernel(
-    terms_ref, parent_ref, ids_ref, arrived_ref, ops_ref, atoms_ref, place_ref, near_ref, matrix_ref,
+    terms_ref, parent_ref, ids_ref, arrived_ref, ops_ref, atoms_ref, place_ref, matrix_ref,
     force_ref, phi_ref, basis, near, got, sent, one, two, returned, turned, lines, send_sem, recv_sem
 ):
     me = Place()
     lvl = me.here[2]
     blocks = atoms_ref.shape[1]
     barrier = me.greet()
-    for d in range(3):
+    for d in range(4):
         turned[d] = atoms_ref[d].T
     shifted = by_octant(parent_ref[...], ops_ref, ids_ref[...][:, 0:1] & 7)
     pl.semaphore_wait(barrier, 10)
@@ -639,13 +640,7 @@
         return carry
 
     lax.fori_loop(0, 3, prepare, 0)
-    done = NEAR_FIRST * 8
-    near[:, 0:done] = near_ref[:, 0:done]
-
-    def fill(low, high):
-        near_groups(atoms_ref, atoms_ref.at[3], near, low, high)
-
-    fill(4, 8)
+    near_tiles(turned, near, 0, 1)
     tags = arrived_ref[...].reshape(32 * CAP, LANES)[:, 127:128].astype(jnp.int32)
     member = (iota((32 * CAP, LEAF_DEV), 1) + 1 == tags).astype(jnp.float32)
     for copy in shared:
@@ -656,7 +651,7 @@
     def between(n):
         if n == 0:
             lax.fori_loop(3, 4, prepare, 0)
-        fill(*((8, 10), (10, 13), (13, 16))[n])
+        near_tiles(turned, near, n + 1, n + 2)
 
     exchange(me, send, sent, one, two, returned, between)
     spread = (iota((32 * CAP, blocks), 0) == place_ref[...]).astype(jnp.float32)
@@ -673,21 +668,20 @@
             for n, start in starts:
                 term = lines[start + row : start + row + 1, :] * value
                 sums[n] = term if sums[n] is None else sums[n] + term
-        for n in range(4):
-            turned[n, at, :] = sums[n]
+        for n in range(3):
+            near[n, at, :] = near[n, at, :] - turned[3, at, :] * sums[n]
+        near[3, at, :] = near[3, at, :] + sums[3]
         return carry
 
     lax.fori_loop(0, 4, chunk, 0)
-    charge = atoms_ref[3]
     for d in range(3):
-        force_ref[d] = near[d] - charge * turned[d].T
-    phi_ref[...] = near[3] + turned[3].T
-
+        force_ref[d] = near[d].T
+    phi_ref[...] = near[3].T
     for copy in started:
         copy.wait_send()
 
 
-def far_field(terms, parent_locals, ids, arrived, l2l_ops, atoms, place, near):
+def far_field(terms, parent_locals, ids, arrived, l2l_ops, atoms, place):
     whole = pl.BlockSpec(memory_space=VMEM)
     f32 = jnp.float32
     return pl.pallas_call(
@@ -696,7 +690,7 @@
             jax.ShapeDtypeStruct((3,) + atoms.shape[1:], f32),
             jax.ShapeDtypeStruct(atoms.shape[1:], f32),
         ),
-        in_specs=[whole] * 9,
+        in_specs=[whole] * 8,
         out_specs=(whole, whole),
         scratch_shapes=[
             VMEM((COEF,) + atoms.shape[1:], f32),
@@ -714,9 +708,19 @@
         compiler_params=pltpu.CompilerParams(collective_id=1, has_side_effects=True, vmem_limit_bytes=20 * MIB),
         name="far_field",
     )(
-        terms.reshape(GROUP, LEAF_DEV, LANES), parent_locals, ids, arrived, l2l_ops.transpose(1, 0, 2), atoms, place, near,
+        terms.reshape(GROUP, LEAF_DEV, LANES), parent_locals, ids, arrived, l2l_ops.transpose(1, 0, 2), atoms, place,
         jnp.asarray(gradient_matrix()),
     )
+
+
+def stacked(arrays):
+    rows = sum(a.shape[0] for a in arrays)
+    total, start = None, 0
+    for a in arrays:
+        part = jnp.pad(a, ((start, rows - start - a.shape[0]), (0, 0)))
+        total = part if total is None else total + part
+        start += a.shape[0]
+    return total
 
 
 def shards(
@@ -739,9 +743,9 @@
     parents_all = leaves_all // 8
     atoms = jnp.concatenate([positions.reshape(3, blocks, LANES), charges.reshape(1, blocks, LANES)])
     integers = [leaf_slot, item_target, item_source, item_offset, coarse_target, coarse_source, coarse_offset, block_leaf]
-    integers = jnp.concatenate([a.reshape(-1, LANES) for a in integers])
+    integers = stacked([a.reshape(-1, LANES) for a in integers])
     (
-        source_table, parent_table, near, leaf_keys, leaf_count, coarse_keys, coarse_count, turned_ops, arrived, place, ids
+        source_table, parent_table, leaf_keys, leaf_count, coarse_keys, coarse_count, turned_ops, arrived, place, ids
     ) = gather(atoms, integers, m2m_ops, m2l_ops)
     source_table = source_table.reshape(leaves_all, LANES)
     parent_table = parent_table.reshape(parents_all, LANES)
@@ -754,7 +758,7 @@
         parent_table,
         turned_ops.reshape(OFFSETS + 1, ROWS, LANES),
     )
-    forces, potential = far_field(terms, parent_locals, ids, arrived, l2l_ops, atoms, place, near)
+    forces, potential = far_field(terms, parent_locals, ids, arrived, l2l_ops, atoms, place)
     return forces.reshape(3, blocks * LANES), potential.reshape(blocks * LANES)
 
 

time: 119 us -> 105 us (0.88)
  Pallas kernels: 106 us -> 94 us
  local copies, waits for them, and re-layouts: 9.1 us -> 7.53 us
    pallas_call x1, Pallas kernels: 39.1 us -> 33.6 us  [translate(): pl.pallas_call(translate_kernel, out_shape=(jax.ShapeDtypeStruct((4 * LEA...]
    pallas_call x1, Pallas kernels: 48.3 us -> 43.1 us  [gather(): pl.pallas_call(gather_kernel, out_shape=(jax.ShapeDtypeStruct((4, 4, 2, 4...]
    pallas_call x1, Pallas kernels: 18.8 us -> 17.4 us  [far_field(): pl.pallas_call(far_kernel, out_shape=(jax.ShapeDtypeStruct((3,) + atoms.s...]
    unnamed x16 -> x11, local copies, waits for them, and re-layouts: 8.43 us -> 7.53 us
where the time goes in v7:
time: 105 us; the launch traced here: 104 us
  Pallas kernels  94 us (90%)
  local copies, waits for them, and re-layouts  7.53 us (7%)
  other arithmetic  1.75 us (2%)
    pallas_call x1, Pallas kernels, gather(): pl.pallas_call(gather_kernel, out_shape=(jax.ShapeDtypeStruct((4, 4, 2, 4...  43.1 us
    pallas_call x1, Pallas kernels, translate(): pl.pallas_call(translate_kernel, out_shape=(jax.ShapeDtypeStruct((4 * LEA...  33.6 us
    pallas_call x1, Pallas kernels, far_field(): pl.pallas_call(far_kernel, out_shape=(jax.ShapeDtypeStruct((3,) + atoms.s...  17.4 us
    unnamed x11, local copies, waits for them, and re-layouts  7.53 us

profile of v7, /device:TPU:1, one launch (start us, length us, event | category | flops | bytes accessed | tf_op | source)
XLA Modules:
  0.0 104.0 jit_solution(11226704862328082448)
XLA Ops:
  0.6 0.9 pad_add_fusion.whole_ref
  1.5 1.0 copy.21
  2.5 0.9 pad_maximum_fusion.atoms_ref
  3.4 0.0 copy-start
  3.4 4.1 %copy-done = f32[316,81,81]{0,2,1:T(8,128)S(1)} copy-done((f32[316,81,81]{0,2,1:T(8,128)S(1)}, f32[316,81,81]{0,2,1:T(8,128)}, u32[]{:S(2)}) %copy-start) | copy-done | bytes 8293128
  7.5 0.0 copy-start.1
  7.5 1.0 copy-done.1
  8.4 43.1 %gather.1 = (f32[4,4,2,4,64,128]{5,4,3,2,1,0:T(8,128)S(1)}, f32[4,4,4,2,8,128]{5,4,3,2,1,0:T(8,128)S(1)}, s32[64,128]{1,0:T(8,128)S(1)}, s32[1,128]{1,0:T(1,128)...) custom-call(f32[4,128,128]{2,1,0:T(8,128)S(1)} %pad_maximum_fusion.a, ...), custom_call_target="tpu_custom_call" | custom-call | tf_op jit(solution)/shard_map/gather/pallas_call | solution.py:577
  51.5 0.0 copy-start.2
  51.5 0.0 copy-start.3
  51.5 33.6 %translate.1 = (f32[256,128]{1,0:T(8,128)S(1)}, f32[64,128]{1,0:T(8,128)S(1)}) custom-call(s32[8192]{0:T(1024)S(1)} %bitcast.36, s32[1,128]{1,0:T(1,128)S(1)} %get-tuple-element.17.leaf_count, s32[4096]{0:T(1024)S(1)} %bitcast.37, s32[1,128]{1,0:T(1,128)S(1)} %get-tuple-element.19.coarse_count, f32[8192,128]{1,0:T(8,128)S(1)} %bitcast.29, ...), custom_call_target="tpu_custom_call" | custom-call | tf_op jit(solution)/shard_map/translate/pallas_call | solution.py:288
  85.1 0.0 copy-done.2
  85.1 0.0 copy-done.3
  85.2 17.4 %far_field.1 = (f32[3,128,128]{2,1,0:T(8,128)S(1)}, f32[128,128]{1,0:T(8,128)S(1)}) custom-call(f32[4,64,128]{2,1,0:T(8,128)S(1)} %bitcast.34, f32[64,128]{1,0:T(8,128)S(1)} %get-tuple-element.24.parent_ref, s32[64,128]{1,0:T(8,128)S(1)} %get-tuple-element.25.ids_ref, f32[4,4,2,8,128]{4,3,2,1,0:T(8,128)S(1)} %get-tuple-element.26.arrived_ref, ...), custom_call_target="tpu_custom_call" | custom-call | tf_op jit(solution)/shard_map/far_field/pallas_call | solution.py:687
  102.5 0.8 copy.20
  103.4 0.6 copy.23
Async XLA Ops:
  3.4 4.1 %copy-start = (f32[316,81,81]{0,2,1:T(8,128)S(1)}, f32[316,81,81]{0,2,1:T(8,128)}, u32[]{:S(2)}) copy-start(f32[316,81,81]{0,2,1:T(8,128)} %param.20) | copy-start | bytes 24879316
  7.5 1.0 copy-start.1
  51.5 33.6 %copy-start.2 = (f32[8,81,81]{2,0,1:T(8,128)S(1)}, f32[8,81,81]{2,0,1:T(8,128)}, u32[]{:S(2)}) copy-start(f32[8,81,81]{2,0,1:T(8,128)} %param.19) | copy-start | bytes 629860
  51.5 33.6 %copy-start.3 = (f32[288,128]{1,0:T(8,128)S(1)}, f32[288,128]{1,0:T(8,128)}, u32[]{:S(2)}) copy-start(f32[288,128]{1,0:T(8,128)} %constant.4.clone.matrix_ref) | copy-start | bytes 442372

commit v8 on v7

--- a/solution.py
+++ b/solution.py
@@ -402,12 +402,13 @@
 
 PARTS = ((0, 16, 24, (2, 0, 1)), (24, 32, 48, (0, 1, 2)), (48, 56, 64, (1, 2, 0)))
 COPIES = 66
+NEAR_FIRST = 2
 SLABS = 9
 
 
 def gather_kernel(
     atoms_ref, whole_ref, m2m_ref, m2l_hbm,
-    all_ref, parent_ref, lkeys_ref, lcount_ref, ckeys_ref, ccount_ref, m2l_ref, arrived_ref, place_ref, ids_ref,
+    all_ref, parent_ref, near_ref, lkeys_ref, lcount_ref, ckeys_ref, ccount_ref, m2l_ref, arrived_ref, place_ref, ids_ref,
     packed, one, two, turned, acc, rows, part_ref, got_c, got_x, got_y, sum_c, sum_x, slabs, send_sem, recv_sem, slab_sem
 ):
     me = Place()
@@ -514,7 +515,9 @@
             write_keys(coarse_items, LEAF_DEV, 1024, ckeys_ref, ccount_ref)
         elif n < 5:
             sort(44 * n - 44, 44 * n)
-        turn(*((0, 0), (0, 0), (0, 0), (0, 0), (0, 1), (1, 5), (5, 8), (8, 9))[n])
+        turn(*((0, 0), (0, 0), (0, 0), (0, 0), (0, 0), (0, 4), (4, 7), (7, 9))[n])
+        if n in (3, 4):
+            near_tiles(turned, near_ref, n - 3, n - 2)
 
     exchange(me, send, packed, one, two, arrived_ref, fill)
     first_slot = ((here[0] * 4 + here[1]) * 2 + core) * GROUP * LEAF_DEV + here[2] * LEAF_DEV
@@ -579,6 +582,7 @@
         out_shape=(
             jax.ShapeDtypeStruct((4, 4, 2, 4, LEAF_DEV, LANES), f32),
             jax.ShapeDtypeStruct((4, 4, 4, 2, 8, LANES), f32),
+            jax.ShapeDtypeStruct((4, 32 * NEAR_FIRST, blocks), f32),
             jax.ShapeDtypeStruct((64, LANES), i32),
             jax.ShapeDtypeStruct((1, LANES), i32),
             jax.ShapeDtypeStruct((32, LANES), i32),
@@ -589,7 +593,7 @@
             jax.ShapeDtypeStruct((LEAF_DEV, LANES), i32),
         ),
         in_specs=[whole] * 3 + [pl.BlockSpec(memory_space=pl.ANY)],
-        out_specs=(whole,) * 10,
+        out_specs=(whole,) * 11,
         scratch_shapes=[
             VMEM((4, 4, 2, CAP, LANES), f32),
             VMEM((2, 4, 4, CAP, LANES), f32),
@@ -614,7 +618,7 @@
 
 
 def far_kernel(
-    terms_ref, parent_ref, ids_ref, arrived_ref, ops_ref, atoms_ref, place_ref, matrix_ref,
+    terms_ref, parent_ref, ids_ref, arrived_ref, ops_ref, atoms_ref, place_ref, near_ref, matrix_ref,
     force_ref, phi_ref, basis, near, got, sent, one, two, returned, turned, lines, send_sem, recv_sem
 ):
     me = Place()
@@ -640,7 +644,8 @@
         return carry
 
     lax.fori_loop(0, 3, prepare, 0)
-    near_tiles(turned, near, 0, 1)
+    near[:, 0 : 32 * NEAR_FIRST] = near_ref[...]
+    near_tiles(turned, near, 2, 3)
     tags = arrived_ref[...].reshape(32 * CAP, LANES)[:, 127:128].astype(jnp.int32)
     member = (iota((32 * CAP, LEAF_DEV), 1) + 1 == tags).astype(jnp.float32)
     for copy in shared:
@@ -651,7 +656,8 @@
     def between(n):
         if n == 0:
             lax.fori_loop(3, 4, prepare, 0)
-        near_tiles(turned, near, n + 1, n + 2)
+        if n == 1:
+            near_tiles(turned, near, 3, 4)
 
     exchange(me, send, sent, one, two, returned, between)
     spread = (iota((32 * CAP, blocks), 0) == place_ref[...]).astype(jnp.float32)
@@ -681,7 +687,7 @@
         copy.wait_send()
 
 
-def far_field(terms, parent_locals, ids, arrived, l2l_ops, atoms, place):
+def far_field(terms, parent_locals, ids, arrived, l2l_ops, atoms, place, near):
     whole = pl.BlockSpec(memory_space=VMEM)
     f32 = jnp.float32
     return pl.pallas_call(
@@ -690,7 +696,7 @@
             jax.ShapeDtypeStruct((3,) + atoms.shape[1:], f32),
             jax.ShapeDtypeStruct(atoms.shape[1:], f32),
         ),
-        in_specs=[whole] * 8,
+        in_specs=[whole] * 9,
         out_specs=(whole, whole),
         scratch_shapes=[
             VMEM((COEF,) + atoms.shape[1:], f32),
@@ -708,7 +714,7 @@
         compiler_params=pltpu.CompilerParams(collective_id=1, has_side_effects=True, vmem_limit_bytes=20 * MIB),
         name="far_field",
     )(
-        terms.reshape(GROUP, LEAF_DEV, LANES), parent_locals, ids, arrived, l2l_ops.transpose(1, 0, 2), atoms, place,
+        terms.reshape(GROUP, LEAF_DEV, LANES), parent_locals, ids, arrived, l2l_ops.transpose(1, 0, 2), atoms, place, near,
         jnp.asarray(gradient_matrix()),
     )
 
@@ -745,7 +751,7 @@
     integers = [leaf_slot, item_target, item_source, item_offset, coarse_target, coarse_source, coarse_offset, block_leaf]
     integers = stacked([a.reshape(-1, LANES) for a in integers])
     (
-        source_table, parent_table, leaf_keys, leaf_count, coarse_keys, coarse_count, turned_ops, arrived, place, ids
+        source_table, parent_table, near, leaf_keys, leaf_count, coarse_keys, coarse_count, turned_ops, arrived, place, ids
     ) = gather(atoms, integers, m2m_ops, m2l_ops)
     source_table = source_table.reshape(leaves_all, LANES)
     parent_table = parent_table.reshape(parents_all, LANES)
@@ -758,7 +764,7 @@
         parent_table,
         turned_ops.reshape(OFFSETS + 1, ROWS, LANES),
     )
-    forces, potential = far_field(terms, parent_locals, ids, arrived, l2l_ops, atoms, place)
+    forces, potential = far_field(terms, parent_locals, ids, arrived, l2l_ops, atoms, place, near)
     return forces.reshape(3, blocks * LANES), potential.reshape(blocks * LANES)
 
 

time: 105 us -> 106 us (level)
  Pallas kernels: 94 us -> 95.3 us
    pallas_call x1, Pallas kernels: 43.1 us -> 44.4 us  [gather(): pl.pallas_call(gather_kernel, out_shape=(jax.ShapeDtypeStruct((4, 4, 2, 4...]
where the time goes in v8:
time: 106 us; the launch traced here: 105 us
  Pallas kernels  95.3 us (90%)
  local copies, waits for them, and re-layouts  7.53 us (7%)
  other arithmetic  1.75 us (2%)
    pallas_call x1, Pallas kernels, gather(): pl.pallas_call(gather_kernel, out_shape=(jax.ShapeDtypeStruct((4, 4, 2, 4...  44.4 us
    pallas_call x1, Pallas kernels, translate(): pl.pallas_call(translate_kernel, out_shape=(jax.ShapeDtypeStruct((4 * LEA...  33.5 us
    pallas_call x1, Pallas kernels, far_field(): pl.pallas_call(far_kernel, out_shape=(jax.ShapeDtypeStruct((3,) + atoms.s...  17.4 us
    unnamed x11, local copies, waits for them, and re-layouts  7.53 us

profile of v8, /device:TPU:1, one launch (start us, length us, event | category | flops | bytes accessed | tf_op | source)
XLA Modules:
  0.0 105.3 jit_solution(14631001350126362463)
XLA Ops:
  0.6 0.9 pad_add_fusion.whole_ref
  1.5 1.0 copy.21
  2.5 0.9 pad_maximum_fusion.atoms_ref
  3.4 0.0 copy-start
  3.4 4.1 %copy-done = f32[316,81,81]{0,2,1:T(8,128)S(1)} copy-done((f32[316,81,81]{0,2,1:T(8,128)S(1)}, f32[316,81,81]{0,2,1:T(8,128)}, u32[]{:S(2)}) %copy-start) | copy-done | bytes 8293128
  7.5 0.0 copy-start.1
  7.5 1.0 copy-done.1
  8.4 44.4 %gather.1 = (f32[4,4,2,4,64,128]{5,4,3,2,1,0:T(8,128)S(1)}, f32[4,4,4,2,8,128]{5,4,3,2,1,0:T(8,128)S(1)}, f32[4,64,128]{2,1,0:T(8,128)S(1)}, s32[64,128]{1,0:T(8...) custom-call(f32[4,128,128]{2,1,0:T(8,128)S(1)} %pad_maximum_fusion.a, ...), custom_call_target="tpu_custom_call" | custom-call | tf_op jit(solution)/shard_map/gather/pallas_call | solution.py:580
  52.8 0.0 copy-start.2
  52.8 0.0 copy-start.3
  52.9 33.5 %translate.1 = (f32[256,128]{1,0:T(8,128)S(1)}, f32[64,128]{1,0:T(8,128)S(1)}) custom-call(s32[8192]{0:T(1024)S(1)} %bitcast.36, s32[1,128]{1,0:T(1,128)S(1)} %get-tuple-element.18.leaf_count, s32[4096]{0:T(1024)S(1)} %bitcast.37, s32[1,128]{1,0:T(1,128)S(1)} %get-tuple-element.20.coarse_count, f32[8192,128]{1,0:T(8,128)S(1)} %bitcast.29, ...), custom_call_target="tpu_custom_call" | custom-call | tf_op jit(solution)/shard_map/translate/pallas_call | solution.py:288
  86.4 0.0 copy-done.2
  86.4 0.0 copy-done.3
  86.4 17.4 %far_field.1 = (f32[3,128,128]{2,1,0:T(8,128)S(1)}, f32[128,128]{1,0:T(8,128)S(1)}) custom-call(f32[4,64,128]{2,1,0:T(8,128)S(1)} %bitcast.34, f32[64,128]{1,0:T(8,128)S(1)} %get-tuple-element.25.parent_ref, s32[64,128]{1,0:T(8,128)S(1)} %get-tuple-element.26.ids_ref, f32[4,4,2,8,128]{4,3,2,1,0:T(8,128)S(1)} %get-tuple-element.27.arrived_ref, ...), custom_call_target="tpu_custom_call" | custom-call | tf_op jit(solution)/shard_map/far_field/pallas_call | solution.py:693
  103.8 0.8 copy.20
  104.6 0.6 copy.23
Async XLA Ops:
  3.4 4.1 %copy-start = (f32[316,81,81]{0,2,1:T(8,128)S(1)}, f32[316,81,81]{0,2,1:T(8,128)}, u32[]{:S(2)}) copy-start(f32[316,81,81]{0,2,1:T(8,128)} %param.20) | copy-start | bytes 24879316
  7.5 1.0 copy-start.1
  52.8 33.5 %copy-start.2 = (f32[8,81,81]{2,0,1:T(8,128)S(1)}, f32[8,81,81]{2,0,1:T(8,128)}, u32[]{:S(2)}) copy-start(f32[8,81,81]{2,0,1:T(8,128)} %param.19) | copy-start | bytes 629860
  52.8 33.5 %copy-start.3 = (f32[288,128]{1,0:T(8,128)S(1)}, f32[288,128]{1,0:T(8,128)}, u32[]{:S(2)}) copy-start(f32[288,128]{1,0:T(8,128)} %constant.4.clone.matrix_ref) | copy-start | bytes 442372

commit v9 on v8

--- a/solution.py
+++ b/solution.py
@@ -625,13 +625,13 @@
     lvl = me.here[2]
     blocks = atoms_ref.shape[1]
     barrier = me.greet()
+    pl.semaphore_wait(barrier, 10)
+
+    started, send = sender(send_sem, recv_sem)
+    shared = [send(terms_ref.at[(lvl + by) % 4], got.at[by - 1], me.moved(2, by)) for by in (1, 2, 3)]
     for d in range(4):
         turned[d] = atoms_ref[d].T
     shifted = by_octant(parent_ref[...], ops_ref, ids_ref[...][:, 0:1] & 7)
-    pl.semaphore_wait(barrier, 10)
-
-    started, send = sender(send_sem, recv_sem)
-    shared = [send(terms_ref.at[(lvl + by) % 4], got.at[by - 1], me.moved(2, by)) for by in (1, 2, 3)]
     total = shifted + terms_ref[lvl]
 
     def prepare(i, carry):

time: 106 us -> 106 us (level)
  no operation moved by 1% of the time
where the time goes in v9:
time: 106 us; the launch traced here: 105 us
  Pallas kernels  95.3 us (90%)
  local copies, waits for them, and re-layouts  7.53 us (7%)
  other arithmetic  1.75 us (2%)
    pallas_call x1, Pallas kernels, gather(): pl.pallas_call(gather_kernel, out_shape=(jax.ShapeDtypeStruct((4, 4, 2, 4...  44.4 us
    pallas_call x1, Pallas kernels, translate(): pl.pallas_call(translate_kernel, out_shape=(jax.ShapeDtypeStruct((4 * LEA...  33.5 us
    pallas_call x1, Pallas kernels, far_field(): pl.pallas_call(far_kernel, out_shape=(jax.ShapeDtypeStruct((3,) + atoms.s...  17.4 us
    unnamed x11, local copies, waits for them, and re-layouts  7.53 us

profile of v9, /device:TPU:1, one launch (start us, length us, event | category | flops | bytes accessed | tf_op | source)
XLA Modules:
  0.0 105.3 jit_solution(12447111324714940285)
XLA Ops:
  0.6 0.9 pad_add_fusion.whole_ref
  1.5 1.0 copy.21
  2.5 0.9 pad_maximum_fusion.atoms_ref
  3.4 0.0 copy-start
  3.4 4.1 %copy-done = f32[316,81,81]{0,2,1:T(8,128)S(1)} copy-done((f32[316,81,81]{0,2,1:T(8,128)S(1)}, f32[316,81,81]{0,2,1:T(8,128)}, u32[]{:S(2)}) %copy-start) | copy-done | bytes 8293128
  7.5 0.0 copy-start.1
  7.5 1.0 copy-done.1
  8.4 44.4 %gather.1 = (f32[4,4,2,4,64,128]{5,4,3,2,1,0:T(8,128)S(1)}, f32[4,4,4,2,8,128]{5,4,3,2,1,0:T(8,128)S(1)}, f32[4,64,128]{2,1,0:T(8,128)S(1)}, s32[64,128]{1,0:T(8...) custom-call(f32[4,128,128]{2,1,0:T(8,128)S(1)} %pad_maximum_fusion.a, ...), custom_call_target="tpu_custom_call" | custom-call | tf_op jit(solution)/shard_map/gather/pallas_call | solution.py:580
  52.8 0.0 copy-start.2
  52.8 0.0 copy-start.3
  52.9 33.5 %translate.1 = (f32[256,128]{1,0:T(8,128)S(1)}, f32[64,128]{1,0:T(8,128)S(1)}) custom-call(s32[8192]{0:T(1024)S(1)} %bitcast.36, s32[1,128]{1,0:T(1,128)S(1)} %get-tuple-element.18.leaf_count, s32[4096]{0:T(1024)S(1)} %bitcast.37, s32[1,128]{1,0:T(1,128)S(1)} %get-tuple-element.20.coarse_count, f32[8192,128]{1,0:T(8,128)S(1)} %bitcast.29, ...), custom_call_target="tpu_custom_call" | custom-call | tf_op jit(solution)/shard_map/translate/pallas_call | solution.py:288
  86.3 0.0 copy-done.2
  86.3 0.0 copy-done.3
  86.3 17.4 %far_field.1 = (f32[3,128,128]{2,1,0:T(8,128)S(1)}, f32[128,128]{1,0:T(8,128)S(1)}) custom-call(f32[4,64,128]{2,1,0:T(8,128)S(1)} %bitcast.34, f32[64,128]{1,0:T(8,128)S(1)} %get-tuple-element.25.parent_ref, s32[64,128]{1,0:T(8,128)S(1)} %get-tuple-element.26.ids_ref, f32[4,4,2,8,128]{4,3,2,1,0:T(8,128)S(1)} %get-tuple-element.27.arrived_ref, ...), custom_call_target="tpu_custom_call" | custom-call | tf_op jit(solution)/shard_map/far_field/pallas_call | solution.py:693
  103.8 0.8 copy.20
  104.6 0.6 copy.23
Async XLA Ops:
  3.4 4.1 %copy-start = (f32[316,81,81]{0,2,1:T(8,128)S(1)}, f32[316,81,81]{0,2,1:T(8,128)}, u32[]{:S(2)}) copy-start(f32[316,81,81]{0,2,1:T(8,128)} %param.20) | copy-start | bytes 24879316
  7.5 1.0 copy-start.1
  52.8 33.5 %copy-start.2 = (f32[8,81,81]{2,0,1:T(8,128)S(1)}, f32[8,81,81]{2,0,1:T(8,128)}, u32[]{:S(2)}) copy-start(f32[8,81,81]{2,0,1:T(8,128)} %param.19) | copy-start | bytes 629860
  52.8 33.5 %copy-start.3 = (f32[288,128]{1,0:T(8,128)S(1)}, f32[288,128]{1,0:T(8,128)}, u32[]{:S(2)}) copy-start(f32[288,128]{1,0:T(8,128)} %constant.4.clone.matrix_ref) | copy-start | bytes 442372
